TPU v7x, 32 devices: a whole 2x2x4 slice. The times are simulated.
32 devices in a mesh: groups: 2 (over y), leaf: 4 (over z), pair: 2 (over x), rhs: 2 (over core).
Axes of the slice: x: 2, y: 2, z: 4, core: 2. Of those that a mesh axis runs over, the one named last changes fastest.
Arguments:
- points: bfloat16 [128, 512, 64], P(('groups', 'leaf')), parts along dimension 0, may hold values from -6 to 6
- weights: bfloat16 [65536, 32], P(('groups', 'leaf'), 'rhs'), parts along dimension 0, may hold values from -6 to 6
- interp: bfloat16 [128, 256, 256], P(('groups', 'leaf')), parts along dimension 0, may hold values from -0.375 to 0.375
- tree_order: int32 [8, 8192], P(('groups', 'leaf')), parts along dimension 0, may hold values from 0 to 8191, each once within a row
- skel_order: int32 [128, 512], P(('groups', 'leaf')), parts along dimension 0, may hold values from 0 to 511, each once within a row
- near_pairs: int32 [128, 16], P(('groups', 'leaf'), 'pair'), parts along dimension 0, may hold values from 0 to 63, as said below
- far_pairs: int32 [128, 8], P(('groups', 'leaf'), 'pair'), parts along dimension 0, may hold values from 0 to 63, as said below
Outputs:
- product: float32 [65536, 32], P(('groups', 'leaf'), 'rhs'), parts along dimension 0
There are 2 independent parts, one for each index of `groups`. A program takes and returns all parts, laid end to end along the dimension named above; each array names one. Nothing has to cross between parts.
Inputs may be any that keep to these rules, and one draw needn't show every extreme that they name: `tree_order`: each row is a permutation of 0 to 8191. `skel_order`: each row is a permutation of 0 to 511; its first 256 entries are the skeleton points. `near_pairs`: every entry lies within 8 of its row's leaf; every row holds its own leaf and a leaf exactly 8 away. `far_pairs`: take the block of rows b * 16 to (b + 1) * 16 - 1 and columns p * 4 to (p + 1) * 4 - 1: its entries never lie in rows' own leaves b * 16 to (b + 1) * 16 - 1, and every block of leaves c * 16 to (c + 1) * 16 - 1 that its entries name is named by exactly 32 of them.
All inputs are finite; a program needn't handle non-finite values.
Results may differ from a plain program's by a relative error of at most 0.0035.
Values may be sent and summed in bfloat16 or wider, within the bound.
No kernel may reach another device: no remote copies, remote signals or barrier semaphores. Data moves between devices by JAX's collectives and lax.ppermute only.
A program may use at most 128 MiB of HBM per device.

v0:
```python
import jax
import jax.numpy as jnp
from jax import lax
from jax.sharding import PartitionSpec as P


def with_halo(cells, sides, width):
    for axis, dim in sides:
        count = lax.axis_size(axis)
        ends = count - 1
        head = lax.slice_in_dim(cells, 0, width, axis=dim)
        tail = lax.slice_in_dim(cells, cells.shape[dim] - width, cells.shape[dim], axis=dim)
        cells = jnp.concatenate(
            [
                lax.ppermute(tail, axis, [(i, (i + 1) % count) for i in range(ends)]),
                cells,
                lax.ppermute(head, axis, [((i + 1) % count, i) for i in range(ends)]),
            ],
            axis=dim,
        )
    return cells


def squares_of(features):
    return jnp.sum(jnp.square(features.astype(jnp.float32)), axis=-1)


def kernel_block(targets, target_sq, sources, source_sq, kernel_scale):
    inner = jnp.einsum("gmd,gnd->gmn", targets, sources, preferred_element_type=jnp.float32)
    exponent = (2.0 * inner - target_sq[:, :, None] - source_sq[:, None, :]) * kernel_scale
    return jnp.exp(exponent).astype(jnp.bfloat16)


def in_groups(function, operands, leaf_count):
    group_size = max(1, leaf_count // 8)
    turn_count = leaf_count // group_size
    shaped = jax.tree.map(
        lambda member: member.reshape((turn_count, group_size) + member.shape[1:]), operands
    )
    result = lax.map(function, shaped)
    return result.reshape((leaf_count,) + result.shape[2:])


def pick(table, index_ids):
    count = table.shape[0]
    one_hot = (index_ids[..., None] == jnp.arange(count, dtype=jnp.int32)).astype(table.dtype)
    flat = table.reshape(count, -1)
    picked = jnp.dot(one_hot.reshape(-1, count), flat, preferred_element_type=jnp.float32)
    return picked.astype(table.dtype).reshape(index_ids.shape + table.shape[1:])


def invert(order_rows):
    count = order_rows.shape[-1]
    rows = order_rows.reshape(-1, count)
    steps = jnp.broadcast_to(jnp.arange(count, dtype=jnp.int32)[None, :], rows.shape)
    row_ids = jnp.arange(rows.shape[0], dtype=jnp.int32)[:, None]
    inverse = jnp.zeros(rows.shape, jnp.int32).at[row_ids, rows].set(steps)
    return inverse.reshape(order_rows.shape)


def on_device(points, weights, interp, tree_order, skel_order, near_pairs, far_pairs):
    leaf_dev, leaf_size, feature_dim = points.shape
    skel_rank = interp.shape[1]
    rhs_cols = weights.shape[1]
    near_span = min(8, leaf_dev)
    kernel_scale = 2.5 / feature_dim
    block_order = tree_order[0]
    tree_weights = weights[block_order].reshape(leaf_dev, leaf_size, rhs_cols)
    order_hot = (
        skel_order[:, :, None] == jnp.arange(leaf_size, dtype=jnp.int32)[None, None, :]
    ).astype(jnp.bfloat16)
    ordered = jnp.einsum(
        "lij,ljc->lic", order_hot, tree_weights, preferred_element_type=jnp.float32
    ).astype(jnp.bfloat16)
    combined = jnp.einsum(
        "lrk,lkc->lrc", interp, ordered[:, skel_rank:], preferred_element_type=jnp.float32
    )
    skel_weights = (ordered[:, :skel_rank].astype(jnp.float32) + combined).astype(jnp.bfloat16)
    skel_points = jnp.einsum(
        "lij,ljd->lid", order_hot[:, :skel_rank], points, preferred_element_type=jnp.float32
    ).astype(jnp.bfloat16)
    skel_sq = squares_of(skel_points)
    joined = jnp.concatenate(
        [points.reshape(leaf_dev, -1), tree_weights.reshape(leaf_dev, -1)], axis=1
    )
    extended = with_halo(joined, (("leaf", 0),), near_span)
    split_at = leaf_size * feature_dim
    halo_points = extended[:, :split_at].reshape(-1, leaf_size, feature_dim)
    halo_weights = extended[:, split_at:].reshape(-1, leaf_size, rhs_cols)
    first_leaf = lax.axis_index("leaf") * leaf_dev
    local_ids = near_pairs - (first_leaf - near_span)

    def near_group(operands):
        target_points, target_sq, source_ids = operands
        group_size = source_ids.shape[0]
        sources = pick(halo_points, source_ids).reshape(group_size, -1, feature_dim)
        source_sq = squares_of(sources)
        source_weights = pick(halo_weights, source_ids).reshape(group_size, -1, rhs_cols)
        block = kernel_block(target_points, target_sq, sources, source_sq, kernel_scale)
        return jnp.einsum("gmn,gnc->gmc", block, source_weights, preferred_element_type=jnp.float32)

    own_sq = squares_of(points)
    near_part = in_groups(near_group, (points, own_sq, local_ids), leaf_dev)
    leaf_count = lax.axis_size("leaf")
    sources_flat = far_pairs.reshape(-1)
    slot_count = sources_flat.shape[0]
    capacity = max(2, 2 * slot_count // leaf_count)
    owners = sources_flat // leaf_dev
    within = sources_flat % leaf_dev
    one_hot = (owners[:, None] == jnp.arange(leaf_count, dtype=jnp.int32)[None, :]).astype(
        jnp.int32
    )
    earlier = jnp.sum((jnp.cumsum(one_hot, axis=0) - one_hot) * one_hot, axis=1)
    positions = owners * capacity + earlier
    requests = (
        jnp.zeros((leaf_count * capacity,), jnp.int32)
        .at[positions]
        .set(within)
        .reshape(leaf_count, capacity)
    )
    wanted = lax.all_to_all(requests, "leaf", split_axis=0, concat_axis=0, tiled=True)
    fetched_points, fetched_weights = (
        lax.all_to_all(pick(skel_points, wanted), "leaf", split_axis=0, concat_axis=0, tiled=True),
        lax.all_to_all(pick(skel_weights, wanted), "leaf", split_axis=0, concat_axis=0, tiled=True),
    )
    slot_points = pick(fetched_points.reshape(-1, skel_rank, feature_dim), positions).reshape(
        leaf_dev, -1, feature_dim
    )
    slot_weights = pick(fetched_weights.reshape(-1, skel_rank, rhs_cols), positions).reshape(
        leaf_dev, -1, rhs_cols
    )

    def far_group(operands):
        target_points, target_sq, sources, source_weights = operands
        block = kernel_block(target_points, target_sq, sources, squares_of(sources), kernel_scale)
        return jnp.einsum("gmn,gnc->gmc", block, source_weights, preferred_element_type=jnp.float32)

    skel_part = in_groups(far_group, (skel_points, skel_sq, slot_points, slot_weights), leaf_dev)
    near_total, skel_total = lax.psum((near_part, skel_part), "pair")
    skel_field = skel_total.astype(jnp.bfloat16)
    rest_field = jnp.einsum("lrk,lrc->lkc", interp, skel_field, preferred_element_type=jnp.float32)
    expanded = jnp.concatenate([skel_field.astype(jnp.float32), rest_field], axis=1)
    skel_inverse = invert(skel_order)
    placed = jnp.take_along_axis(expanded, skel_inverse[:, :, None], axis=1)
    tree_field = (near_total + placed).reshape(-1, rhs_cols)
    block_inverse = invert(block_order)
    return tree_field[block_inverse]


def solution(mesh):
    return jax.shard_map(
        on_device,
        mesh=mesh,
        in_specs=(
            P(("groups", "leaf"), None, None),
            P(("groups", "leaf"), "rhs"),
            P(("groups", "leaf"), None, None),
            P(("groups", "leaf"), None),
            P(("groups", "leaf"), None),
            P(("groups", "leaf"), "pair"),
            P(("groups", "leaf"), "pair"),
        ),
        out_specs=P(("groups", "leaf"), "rhs"),
        check_vma=False,
    )
```

profile of v0, /device:TPU:8, one launch (start us, length us, event | category | flops | bytes accessed | tf_op | source)
XLA Modules:
  0.0 687.7 jit_solution(186095951715067025)
XLA Ops:
  18.2 29.9 %gather_fusion = bf16[8192,16]{1,0:T(8,128)(2,1)} fusion(bf16[8192,16]{1,0:T(8,128)(2,1)} %copy.41, s32[8192]{0:T(1024)S(1)} %broadcast_clamp_fusion.1), kind=kCustom, calls=%fused_computation | custom fusion | bytes 557056 | tf_op jit(solution)/shard_map/gather | solution.py:68
  74.5 30.6 %scatter_custom_fusion.1 = s32[8192]{0:T(1024)S(1)} fusion(s32[8192]{0:T(1024)} %bitcast.130, s32[8192]{0:T(1024)S(1)} %bitcast.131, s32[]{:T(128)} %copy.83), kind=kCustom, calls=%fused_computation.94 | custom fusion | bytes 33280
  115.7 30.7 %scatter_custom_fusion.2 = s32[8192]{0:T(1024)S(1)} fusion(s32[8192]{0:T(1024)S(1)} %broadcast_select_fusion, s32[8192]{0:T(1024)S(1)} %iota.36, s32[]{:T(128)} %copy.83), kind=kCustom, calls=%fused_computation.92 | custom fusion | bytes 32772
  168.3 11.3 %reshape.263 = bf16[4,32,256,64]{3,2,1,0:T(8,128)(2,1)} reshape(bf16[128,16384]{1,0:T(8,128)(2,1)} %convolution_convert_fusion.2) | data formatting | bytes 8388608 | tf_op jit(solution)/shard_map/reshape | solution.py:49
  179.7 8.5 %copy.47 = bf16[4,32,256,64]{2,3,1,0:T(8,128)(2,1)} copy(bf16[4,32,256,64]{3,2,1,0:T(8,128)(2,1)} %reshape.263) | data formatting | bytes 8388608 | tf_op jit(solution)/shard_map/reshape | solution.py:49
  199.6 7.2 %copy.52 = bf16[4,32,256,16]{2,3,1,0:T(8,128)(2,1)} copy(bf16[4,32,256,16]{1,0,3,2:T(4,128)(2,1)} %reshape.267) | data formatting | bytes 2097152 | tf_op jit(solution)/shard_map/reshape | solution.py:49
  216.6 16.6 %all-to-all-done.2 = bf16[4,32,256,16]{2,3,1,0:T(8,128)(2,1)} async-done(((bf16[4,32,256,16]{2,3,1,0:T(8,128)(2,1)}), bf16[4,32,256,16]{2,3,1,0:T(8,128)(2,1)}, u32[]{:S(2)}, u32[]{:S(2)}) %all-to-all-start.2) | async-done | bytes 1048608 | tf_op jit(solution)/shard_map/all_to_all | solution.py:124
  233.2 8.2 %all-to-all-start.1 = ((bf16[4,32,256,64]{2,3,1,0:T(8,128)(2,1)}), bf16[4,32,256,64]{2,3,1,0:T(8,128)(2,1)}, u32[]{:S(2)}, u32[]{:S(2)}) async-start(bf16[4,32,256,64]{2,3,1,0:T(8,128)(2,1)} %copy.47), calls=%async_computation.1 | async-start | bytes 8388608 | tf_op jit(solution)/shard_map/all_to_all | solution.py:123
  241.6 173.0 %while.20 = (s32[]{:T(128)}, f32[8,2,512,16]{2,3,1,0:T(8,128)}, bf16[8,2,512,64]{2,3,1,0:T(8,128)(2,1)}, s32[8,2,8]{2,1,0:T(2,128)}, bf16[32,32768]{1,0:T(8,128)...) while((s32[]{:T(128)}, f32[8,2,512,16]{2,3,1,0:T(8,128)}, ...), condition=%wide.region_3.4_spmd, body=%wide.region_1.3_spmd.sunk | while | flops 736224256 | bytes 12072413 | solution.py:40
  254.5 8.7 %fusion.88 = f32[8,2,512,16]{2,3,1,0:T(8,128)} fusion(f32[8,2,512,16]{2,3,1,0:T(8,128)} %get-tuple-element.215, s32[]{:T(128)} %get-tuple-element.214, bf16[2,4096,16]{2,1,0:T(8,128)(2,1)} %reshape.351, bf16[2,4096,64]{2,1,0:T(8,128)(2,1)} %reshape.352, f32[2,4096]{1,0:T(2,128)S(1)} %multiply_reduce_fusion.7, ...), kind=kOutput, calls=%fused_computation.12.clone.1 | convolution fusion | flops 692060160 | bytes 4428800 | tf_op jit(solution)/shard_map/while/body/eval_jaxpr/gmn,gnc->gmc/dot_general | solution.py:100
  276.0 8.7 %fusion.88 = f32[8,2,512,16]{2,3,1,0:T(8,128)} fusion(f32[8,2,512,16]{2,3,1,0:T(8,128)} %get-tuple-element.215, s32[]{:T(128)} %get-tuple-element.214, bf16[2,4096,16]{2,1,0:T(8,128)(2,1)} %reshape.351, bf16[2,4096,64]{2,1,0:T(8,128)(2,1)} %reshape.352, f32[2,4096]{1,0:T(2,128)S(1)} %multiply_reduce_fusion.7, ...), kind=kOutput, calls=%fused_computation.12.clone.1 | convolution fusion | flops 692060160 | bytes 4428800 | tf_op jit(solution)/shard_map/while/body/eval_jaxpr/gmn,gnc->gmc/dot_general | solution.py:100
  297.7 8.7 %fusion.88 = f32[8,2,512,16]{2,3,1,0:T(8,128)} fusion(f32[8,2,512,16]{2,3,1,0:T(8,128)} %get-tuple-element.215, s32[]{:T(128)} %get-tuple-element.214, bf16[2,4096,16]{2,1,0:T(8,128)(2,1)} %reshape.351, bf16[2,4096,64]{2,1,0:T(8,128)(2,1)} %reshape.352, f32[2,4096]{1,0:T(2,128)S(1)} %multiply_reduce_fusion.7, ...), kind=kOutput, calls=%fused_computation.12.clone.1 | convolution fusion | flops 692060160 | bytes 4428800 | tf_op jit(solution)/shard_map/while/body/eval_jaxpr/gmn,gnc->gmc/dot_general | solution.py:100
  319.3 8.7 %fusion.88 = f32[8,2,512,16]{2,3,1,0:T(8,128)} fusion(f32[8,2,512,16]{2,3,1,0:T(8,128)} %get-tuple-element.215, s32[]{:T(128)} %get-tuple-element.214, bf16[2,4096,16]{2,1,0:T(8,128)(2,1)} %reshape.351, bf16[2,4096,64]{2,1,0:T(8,128)(2,1)} %reshape.352, f32[2,4096]{1,0:T(2,128)S(1)} %multiply_reduce_fusion.7, ...), kind=kOutput, calls=%fused_computation.12.clone.1 | convolution fusion | flops 692060160 | bytes 4428800 | tf_op jit(solution)/shard_map/while/body/eval_jaxpr/gmn,gnc->gmc/dot_general | solution.py:100
  340.9 8.7 %fusion.88 = f32[8,2,512,16]{2,3,1,0:T(8,128)} fusion(f32[8,2,512,16]{2,3,1,0:T(8,128)} %get-tuple-element.215, s32[]{:T(128)} %get-tuple-element.214, bf16[2,4096,16]{2,1,0:T(8,128)(2,1)} %reshape.351, bf16[2,4096,64]{2,1,0:T(8,128)(2,1)} %reshape.352, f32[2,4096]{1,0:T(2,128)S(1)} %multiply_reduce_fusion.7, ...), kind=kOutput, calls=%fused_computation.12.clone.1 | convolution fusion | flops 692060160 | bytes 4428800 | tf_op jit(solution)/shard_map/while/body/eval_jaxpr/gmn,gnc->gmc/dot_general | solution.py:100
  362.5 8.7 %fusion.88 = f32[8,2,512,16]{2,3,1,0:T(8,128)} fusion(f32[8,2,512,16]{2,3,1,0:T(8,128)} %get-tuple-element.215, s32[]{:T(128)} %get-tuple-element.214, bf16[2,4096,16]{2,1,0:T(8,128)(2,1)} %reshape.351, bf16[2,4096,64]{2,1,0:T(8,128)(2,1)} %reshape.352, f32[2,4096]{1,0:T(2,128)S(1)} %multiply_reduce_fusion.7, ...), kind=kOutput, calls=%fused_computation.12.clone.1 | convolution fusion | flops 692060160 | bytes 4428800 | tf_op jit(solution)/shard_map/while/body/eval_jaxpr/gmn,gnc->gmc/dot_general | solution.py:100
  384.2 8.7 %fusion.88 = f32[8,2,512,16]{2,3,1,0:T(8,128)} fusion(f32[8,2,512,16]{2,3,1,0:T(8,128)} %get-tuple-element.215, s32[]{:T(128)} %get-tuple-element.214, bf16[2,4096,16]{2,1,0:T(8,128)(2,1)} %reshape.351, bf16[2,4096,64]{2,1,0:T(8,128)(2,1)} %reshape.352, f32[2,4096]{1,0:T(2,128)S(1)} %multiply_reduce_fusion.7, ...), kind=kOutput, calls=%fused_computation.12.clone.1 | convolution fusion | flops 692060160 | bytes 4428800 | tf_op jit(solution)/shard_map/while/body/eval_jaxpr/gmn,gnc->gmc/dot_general | solution.py:100
  405.8 8.7 %fusion.88 = f32[8,2,512,16]{2,3,1,0:T(8,128)} fusion(f32[8,2,512,16]{2,3,1,0:T(8,128)} %get-tuple-element.215, s32[]{:T(128)} %get-tuple-element.214, bf16[2,4096,16]{2,1,0:T(8,128)(2,1)} %reshape.351, bf16[2,4096,64]{2,1,0:T(8,128)(2,1)} %reshape.352, f32[2,4096]{1,0:T(2,128)S(1)} %multiply_reduce_fusion.7, ...), kind=kOutput, calls=%fused_computation.12.clone.1 | convolution fusion | flops 692060160 | bytes 4428800 | tf_op jit(solution)/shard_map/while/body/eval_jaxpr/gmn,gnc->gmc/dot_general | solution.py:100
  418.1 8.5 %copy.53 = bf16[4,32,256,16]{1,0,3,2:T(4,128)(2,1)} copy(bf16[4,32,256,16]{2,3,1,0:T(8,128)(2,1)} %all-to-all-done.2) | data formatting | bytes 2097152 | tf_op jit(solution)/shard_map/all_to_all | solution.py:124
  442.5 8.4 %copy.48 = bf16[4,32,256,64]{3,2,1,0:T(8,128)(2,1)} copy(bf16[4,32,256,64]{2,3,1,0:T(8,128)(2,1)} %all-to-all-done.1) | data formatting | bytes 8388608 | tf_op jit(solution)/shard_map/all_to_all | solution.py:123
  450.9 10.7 %reshape_reshape.10 = bf16[128,16384]{1,0:T(8,128)(2,1)} reshape(bf16[4,32,256,64]{3,2,1,0:T(8,128)(2,1)} %copy.48) | data formatting | bytes 8388608 | tf_op jit(solution)/shard_map/reshape;reshape | solution.py:47
  477.2 23.8 %while.21 = (s32[]{:T(128)}, f32[8,2,256,16]{2,3,1,0:T(8,128)S(1)}, bf16[8,2,256,64]{2,3,1,0:T(8,128)(2,1)}, bf16[8,2,1024,64]{2,3,1,0:T(8,128)(2,1)}, f32[8,2,2...) while((s32[]{:T(128)}, f32[8,2,256,16]{2,3,1,0:T(8,128)S(1)}, ...), condition=%wide.region_12.13_spmd, body=%wide.region_10.12_spmd.sunk | while | flops 86898688 | bytes 712789 | solution.py:40
  501.0 18.0 %all-reduce.5 = bf16[16,256,16]{1,2,0:T(8,128)(2,1)S(1)} all-reduce(f32[16,256,16]{1,2,0:T(8,128)S(1)} %bitcast.126), channel_id=1, replica_groups=mesh['groups'=2,'leaf'=4,'pair'=2,'rhs'=2] {'pair'}, use_global_device_ids=true, to_apply=%region_13.14 | all-reduce | flops 65536 | bytes 393216 | tf_op jit(solution)/shard_map/psum | solution.py:139
  522.1 118.6 %gather_fusion.2 = f32[8192,16]{1,0:T(8,128)} fusion(f32[16,512,16]{2,1,0:T(8,128)} %copy.56, s32[8192]{0:T(1024)S(1)} %bitcast.119), kind=kCustom, calls=%fused_computation.2 | custom fusion | bytes 1114112 | tf_op jit(solution)/shard_map/jit(take_along_axis)/gather | solution.py:144
  647.0 29.9 %gather_fusion.1 = f32[8192,16]{1,0:T(8,128)} fusion(f32[8192,16]{1,0:T(8,128)} %bitcast.120, s32[8192]{0:T(1024)S(1)} %broadcast_clamp_fusion), kind=kCustom, calls=%fused_computation.1 | custom fusion | bytes 1081344 | tf_op jit(solution)/shard_map/gather | solution.py:147
  (205 shorter events, 266.2 us)
Async XLA Ops:
  6.5 139.9 %copy-start = (bf16[16,256,256]{2,1,0:T(8,128)(2,1)S(1)}, bf16[16,256,256]{2,1,0:T(8,128)(2,1)}, u32[]{:S(2)}) copy-start(bf16[16,256,256]{2,1,0:T(8,128)(2,1)} %param.13) | copy-start | bytes 6291460
  9.5 152.5 %all-to-all-start = ((s32[4,1,32]{2,1,0:T(1,128)}), s32[4,1,32]{2,1,0:T(1,128)}, u32[]{:S(2)}, u32[]{:S(2)}) async-start(s32[4,1,32]{2,1,0:T(1,128)} %bitcast.17), calls=%async_computation | async-start | bytes 4096 | tf_op jit(solution)/shard_map/all_to_all | solution.py:121
  18.2 35.3 %copy-start.2 = (bf16[16,512,64]{1,2,0:T(8,128)(2,1)S(1)}, bf16[16,512,64]{1,2,0:T(8,128)(2,1)}, u32[]{:S(2)}) copy-start(bf16[16,512,64]{1,2,0:T(8,128)(2,1)} %param.11) | copy-start | bytes 3145732
  55.3 14.4 %copy-start.4 = (s32[16,512]{1,0:T(8,128)S(1)}, s32[16,512]{1,0:T(8,128)}, u32[]{:S(2)}) copy-start(s32[16,512]{1,0:T(8,128)} %param.15) | copy-start | bytes 98308
  60.3 13.4 %copy-start.12 = (s32[2]{0:T(128)S(1)}, s32[2]{0:T(128)}, u32[]{:S(2)}) copy-start(s32[2]{0:T(128)} %constant.118) | copy-start | bytes 28
  60.3 13.5 %copy-start.11 = (s32[2]{0:T(128)S(1)}, s32[2]{0:T(128)}, u32[]{:S(2)}) copy-start(s32[2]{0:T(128)} %constant.121) | copy-start | bytes 28
  60.3 45.5 %copy-start.5 = (s32[1,8192]{1,0:T(1,128)S(1)}, s32[1,8192]{1,0:T(1,128)}, u32[]{:S(2)}) copy-start(s32[1,8192]{1,0:T(1,128)} %param.14) | copy-start | bytes 98308
  62.5 149.4 %collective-permute-start = (bf16[8,40960]{1,0:T(8,128)(2,1)}, bf16[8,40960]{1,0:T(8,128)(2,1)}, u32[]{:S(2)}, u32[]{:S(2)}) collective-permute-start(bf16[8,40960]{1,0:T(8,128)(2,1)} %get-tuple-element.120), channel_id=1, source_target_pairs={{0,4},{4,8},{8,12},{1,5},{5,9},{9,13},{2,6},{6,10},{10,14},{3,7},{... | collective-permute-start | bytes 1966088 | tf_op jit(solution)/shard_map/ppermute | solution.py:15
  65.8 146.0 %collective-permute-start.1 = (bf16[8,40960]{1,0:T(8,128)(2,1)}, bf16[8,40960]{1,0:T(8,128)(2,1)}, u32[]{:S(2)}, u32[]{:S(2)}) collective-permute-start(bf16[8,40960]{1,0:T(8,128)(2,1)} %get-tuple-element.121), channel_id=1, source_target_pairs={{4,0},{8,4},{12,8},{5,1},{9,5},{13,9},{6,2},{10,6},{14,10},{7,3},{... | collective-permute-start | bytes 1966088 | tf_op jit(solution)/shard_map/ppermute | solution.py:17
  105.9 4.9 copy-start.1
  110.7 4.5 copy-start.8
  110.7 4.6 copy-start.10
  110.7 4.7 copy-start.13
  146.4 15.5 %copy-start.7 = (f32[16,256]{1,0:T(8,128)S(1)}, f32[16,256]{1,0:T(8,128)}, u32[]{:S(2)}) copy-start(f32[16,256]{1,0:T(8,128)} %get-tuple-element.124) | copy-start | bytes 49156
  206.7 26.4 %all-to-all-start.2 = ((bf16[4,32,256,16]{2,3,1,0:T(8,128)(2,1)}), bf16[4,32,256,16]{2,3,1,0:T(8,128)(2,1)}, u32[]{:S(2)}, u32[]{:S(2)}) async-start(bf16[4,32,256,16]{2,3,1,0:T(8,128)(2,1)} %copy.52), calls=%async_computation.2 | async-start | bytes 2097152 | tf_op jit(solution)/shard_map/all_to_all | solution.py:124
  233.2 209.3 %all-to-all-start.1 = ((bf16[4,32,256,64]{2,3,1,0:T(8,128)(2,1)}), bf16[4,32,256,64]{2,3,1,0:T(8,128)(2,1)}, u32[]{:S(2)}, u32[]{:S(2)}) async-start(bf16[4,32,256,64]{2,3,1,0:T(8,128)(2,1)} %copy.47), calls=%async_computation.1 | async-start | bytes 8388608 | tf_op jit(solution)/shard_map/all_to_all | solution.py:123
  241.4 399.4 %all-reduce.4.cloned.1.call-start = ((), (), s32[]{:S(2)}) async-start(), calls=%async_computation.3 | async-start | bytes 8388608 | tf_op jit(solution)/shard_map/psum | solution.py:139
  418.0 14.0 %copy-start.9 = (s32[64]{0:T(128)S(1)}, s32[64]{0:T(128)}, u32[]{:S(2)}) copy-start(s32[64]{0:T(128)} %multiply_add_fusion) | copy-start | bytes 772
  472.3 4.9 copy-start.3
  522.1 118.6 %copy-start.6 = (pred[16,512]{1,0:T(8,128)(4,1)S(1)}, pred[16,512]{1,0:T(8,128)(4,1)}, u32[]{:S(2)}) copy-start(pred[16,512]{1,0:T(8,128)(4,1)} %compare_and_fusion) | copy-start | bytes 24580
Sparse Core Ops, SparseCore 0:
  418.2 114.4 all-reduce.3
where the time goes:
time: 701 us; the launch traced here: 688 us
  local copies, waits for them, and re-layouts  426 us (61%)
  matrix products  136 us (19%)
  other arithmetic  50.6 us (7%)
  starting transfers between devices  25.5 us (4%)
  blocking collectives  18 us (3%)
  waiting for transfers between devices  16.6 us (2%)
  between operations  14.2 us (2%)
    gather x1, local copies, waits for them, and re-layouts, on_device(): placed = jnp.take_along_axis(expanded, skel_inverse[:, :, None], axis=1)  119 us
    dot_general x8, matrix products, near_group(): jnp.einsum('gmn,gnc->gmc', block, source_weights, preferred_element_type=...  69.9 us
    unnamed x39, local copies, waits for them, and re-layouts  68.7 us
    dot_general x20, matrix products, pick(): jnp.dot(one_hot.reshape(-1, count), flat, preferred_element_type=jnp.floa...  39.4 us
    reshape x4, local copies, waits for them, and re-layouts, pick(): return picked.astype(table.dtype).reshape(index_ids.shape + table.shape[1:])  33.8 us
    gather x2, local copies, waits for them, and re-layouts, on_device(): return tree_field[block_inverse]  33.4 us
    reduce_sum x17, other arithmetic, squares_of(): return jnp.sum(jnp.square(features.astype(jnp.float32)), axis=-1)  32.1 us
    gather x1, local copies, waits for them, and re-layouts, on_device(): tree_weights = weights[block_order].reshape(leaf_dev, leaf_size, rhs_cols)  29.9 us
  transfers between devices with their start and end apart: 6, of which 1 were waited for; matrix products, arithmetic and copies ran while one was open for 83% of the time, Pallas kernels for 0%

commit v1 on v0

v1 whole, which is shorter than its diff:
```python
import functools

import jax
import jax.numpy as jnp
from jax import lax
from jax.experimental import pallas as pl
from jax.experimental.pallas import tpu as pltpu
from jax.sharding import PartitionSpec as P

BF = jnp.bfloat16
F32 = jnp.float32
LOG2E = 1.4426950408889634
EXTRA = 16
VMEM = pl.BlockSpec(memory_space=pltpu.VMEM)
SMEM = pl.BlockSpec(memory_space=pltpu.SMEM)
PARAMS = pltpu.CompilerParams(vmem_limit_bytes=48 << 20)


def call(body, shapes, specs, args, scratch=(), out_specs=None):
    outs = [jax.ShapeDtypeStruct(s, d) for s, d in shapes]
    return pl.pallas_call(
        body,
        out_shape=outs,
        in_specs=specs,
        out_specs=[VMEM] * len(outs) if out_specs is None else out_specs,
        scratch_shapes=list(scratch),
        compiler_params=PARAMS,
    )(*args)


def extra_rows(feat, ones_first):
    wide = feat.astype(F32)
    half = -0.5 * jnp.sum(wide * wide, axis=0, keepdims=True)
    high = half.astype(BF).astype(F32)
    mid = (half - high).astype(BF).astype(F32)
    low = half - high - mid
    row = lax.broadcasted_iota(jnp.int32, (EXTRA, feat.shape[1]), 0)
    at = 3 if ones_first else 0
    ones = (row < 3) if ones_first else (row >= 3) & (row < 6)
    picked = jnp.where(row == at, high, jnp.where(row == at + 1, mid, jnp.where(row == at + 2, low, 0.0)))
    return jnp.where(ones, 1.0, picked).astype(BF)


def as_targets(feat):
    return jnp.concatenate([feat, extra_rows(feat, False)], axis=0)


def as_sources(feat):
    return jnp.concatenate([feat, extra_rows(feat, True)], axis=0).astype(F32).T.astype(BF)


def one_hot(row_ids, count):
    rows = lax.broadcasted_iota(jnp.int32, (count, row_ids.shape[1]), 0)
    return jnp.where(rows == row_ids, 1.0, 0.0).astype(BF)


def dot(a, b):
    return jnp.dot(a, b, preferred_element_type=F32)


def dot_last(a, b):
    return lax.dot_general(a, b, (((1,), (1,)), ((), ())), preferred_element_type=F32)


def gauss(sources, targets, scale):
    return jnp.exp2(dot(sources, targets) * scale).astype(BF)


def skel_points_body(cls_ref, skel_ref, out_ref):
    rank = out_ref.shape[2]
    for j in range(cls_ref.shape[0]):
        hot = one_hot(skel_ref[j, :, :rank], cls_ref.shape[2])
        out_ref[j] = dot(cls_ref[j], hot).astype(BF)


def weights_body(own_ref, other_ref, order_ref, skel_ref, interp_ref, tw_ref, sw_ref, stack):
    cols = own_ref.shape[0]
    step = 2 * cols
    width = stack.shape[1]
    turns = own_ref.shape[1] // width
    rank = sw_ref.shape[2]
    for hi in range(turns):
        span = slice(hi * width, (hi + 1) * width)
        stack[hi * step : hi * step + cols] = own_ref[:, span]
        stack[hi * step + cols : (hi + 1) * step] = other_ref[:, span]

    def leaf(j, _):
        ids = order_ref[j]
        hi_ids = lax.shift_right_logical(ids, width.bit_length() - 1)
        picked = dot(stack[...], one_hot(ids & (width - 1), width))
        total = jnp.zeros((step, ids.shape[1]), F32)
        for hi in range(turns):
            total = total + jnp.where(hi_ids == hi, picked[hi * step : (hi + 1) * step], 0.0)
        tree = total.astype(BF)
        tw_ref[j] = tree
        ordered = dot(tree, one_hot(skel_ref[j], ids.shape[1]))
        combined = dot_last(ordered[:, rank:].astype(BF), interp_ref[j])
        sw_ref[j] = (ordered[:, :rank] + combined).astype(BF)
        return 0

    lax.fori_loop(0, order_ref.shape[0], leaf, 0)


def near_sum(t, first, count, most, scale, cnt_ref, slots, tgt, src, weights, write):
    found = jnp.int32(0)
    for e in range(count):
        slots[found] = jnp.int32(e)
        found = found + jnp.where(cnt_ref[t, first + e] > 0, 1, 0)
    for k in range(1, most + 1):

        @pl.when(found == k)
        def _():
            names = [slots[j] for j in range(k)]
            size = src.shape[1]
            block = gauss(jnp.concatenate([src[s] for s in names], axis=0), tgt[t], scale)
            total = None
            for j, s in enumerate(names):
                times = cnt_ref[t, first + s].astype(F32)
                part = dot(weights[s], block[j * size : (j + 1) * size]) * times
                total = part if total is None else total + part
            write(t, total)

    return found


def near_body(halo, scale, where_ref, cnt_ref, pts_ref, tw_ref, skel_ref, near_ref, tgt_ref, far_tgt_ref, src, slots):
    leaves = pts_ref.shape[0]
    mine = tw_ref.shape[0]
    classes = leaves // mine
    rank = far_tgt_ref.shape[2]

    def sources(j, _):
        src[j] = as_sources(pts_ref[j * classes + where_ref[0]])
        return 0

    lax.fori_loop(0, mine, sources, 0)

    def write(t, value):
        near_ref[t] = value

    def target(t, _):
        tgt_ref[t] = as_targets(pts_ref[t])
        found = near_sum(t, halo, mine, mine, scale, cnt_ref, slots, tgt_ref, src, tw_ref, write)

        @pl.when(found == 0)
        def _():
            near_ref[t] = jnp.zeros(near_ref.shape[1:], F32)

        hot = one_hot(skel_ref[t, :, :rank], pts_ref.shape[2])
        far_tgt_ref[t] = as_targets(dot(pts_ref[t], hot).astype(BF))
        return 0

    lax.fori_loop(0, leaves, target, 0)


def far_body(
    halo, mine, scale, cnt_ref, far_ref, near_ref, tgt_ref, left_p, right_p, left_w, right_w, far_tgt, far_p, far_w,
    interp_ref, skel_ref, own_ref, other_ref, src, wts, far_src, field, slots, far_t, far_s,
):
    leaves, cols2, size = near_ref.shape
    rank = far_tgt.shape[2]
    cols = cols2 // 2
    for j in range(halo):
        src[j] = as_sources(left_p[j])
        src[halo + j] = as_sources(right_p[j])
        wts[j] = left_w[j]
        wts[halo + j] = right_w[j]

    def write(t, value):
        near_ref[t] += value

    def target(t, _):
        half = leaves // 2

        @pl.when(t < half)
        def _():
            near_sum(t, 0, halo, halo, scale, cnt_ref, slots, tgt_ref, src, wts, write)

        @pl.when(t >= half)
        def _():
            near_sum(t, halo + mine, halo, halo, scale, cnt_ref, slots, tgt_ref, src.at[halo:], wts.at[halo:], write)

        field[t] = jnp.zeros(field.shape[1:], F32)
        return 0

    lax.fori_loop(0, leaves, target, 0)

    def far_sources(j, _):
        far_src[j] = as_sources(far_p[j])
        return 0

    lax.fori_loop(0, far_p.shape[0], far_sources, 0)
    slots_per = far_ref.shape[1]

    def listing(i, found):
        t = i // slots_per
        s = far_ref[t, i - t * slots_per]
        far_t[found] = t
        far_s[found] = s
        return found + jnp.where(s >= 0, 1, 0)

    found = lax.fori_loop(0, leaves * slots_per, listing, jnp.int32(0))
    group = 4
    for j in range(group):
        far_t[found + j] = jnp.int32(leaves)
        far_s[found + j] = jnp.int32(0)

    def far_group(g, _):
        for j in range(group):
            t = far_t[g * group + j]
            s = far_s[g * group + j]
            tt = jnp.minimum(t, leaves - 1)
            field[t] += dot(far_w[s], gauss(far_src[s], far_tgt[tt], scale))
        return 0

    lax.fori_loop(0, (found + group - 1) // group, far_group, 0)

    for t in range(leaves):
        skel = field[t].astype(BF)
        rest = dot(skel, interp_ref[t]).astype(BF)
        expanded = jnp.concatenate([skel, rest], axis=1)
        total = near_ref[t] + dot_last(expanded, one_hot(skel_ref[t], size))
        own_ref[:, t * size : (t + 1) * size] = total[:cols]
        other_ref[:, t * size : (t + 1) * size] = total[cols:].astype(BF)


def place_body(count, order_ref, *refs):
    parts, out_ref, acc = refs[:count], refs[count], refs[count + 1]
    cols, total = out_ref.shape
    width = acc.shape[1]
    turns = total // width
    chunk = 1024
    for at in range(0, total, chunk):
        span = slice(at, at + chunk)
        value = parts[0][:, span].astype(F32)
        for part in parts[1:]:
            value = value + part[:, span].astype(F32)
        ids = order_ref[:, span]
        hi_ids = lax.shift_right_logical(ids, width.bit_length() - 1)
        masked = [jnp.where(hi_ids == hi, value, 0.0).astype(BF) for hi in range(turns)]
        part = dot_last(jnp.concatenate(masked, axis=0), one_hot(ids & (width - 1), width))
        acc[...] = part if at == 0 else acc[...] + part
    for hi in range(turns):
        out_ref[:, hi * width : (hi + 1) * width] = acc[hi * cols : (hi + 1) * cols]


def ring(count, by):
    return [(i, (i + by) % count) for i in range(count)]


def from_others(value, axis):
    count = lax.axis_size(axis)
    return [lax.ppermute(value, axis, ring(count, by)) for by in range(1, count)]


def on_device(points, weights, interp, tree_order, skel_order, near_pairs, far_pairs):
    leaves, size, dim = points.shape
    rank = interp.shape[1]
    cols = weights.shape[1]
    blocks, pair_n, rhs_n = (lax.axis_size(a) for a in ("leaf", "pair", "rhs"))
    classes = pair_n * rhs_n
    mine = leaves // classes
    span = min(8, leaves)
    halo = span // classes
    block, mine_id = lax.axis_index("leaf"), lax.axis_index("pair") * rhs_n + lax.axis_index("rhs")
    scale = 2.0 * 2.5 / dim * LOG2E
    slot_n = far_pairs.shape[1] * pair_n

    def of_class(array):
        cut = array.reshape((mine, classes) + array.shape[1:])
        return lax.dynamic_index_in_dim(cut, mine_id, 1, keepdims=False)

    pts = points.transpose(0, 2, 1)
    wts = weights.T
    order = tree_order.reshape(leaves, 1, size)
    skel = skel_order.reshape(leaves, 1, size)
    (other_wts,) = from_others(wts, "rhs")
    cls_pts = of_class(pts)
    up, down = [(i, i + 1) for i in range(blocks - 1)], [(i + 1, i) for i in range(blocks - 1)]
    left_p = lax.ppermute(cls_pts[mine - halo :], "leaf", up)
    right_p = lax.ppermute(cls_pts[:halo], "leaf", down)
    pairs = jnp.concatenate([near_pairs, far_pairs], axis=1)
    every = jnp.stack([pairs] + from_others(pairs, "pair"), axis=1)
    near_n = near_pairs.shape[1]
    near_all = every[:, :, :near_n].reshape(leaves, -1) - (block * leaves - span)
    far_all = every[:, :, near_n:].reshape(leaves, -1)
    table = (jnp.arange(2 * halo + mine, dtype=jnp.int32) * classes + mine_id)[None, :, None]
    cnt = jnp.sum((near_all[:, None, :] == table).astype(jnp.int32), axis=2)
    owner, within = far_all // leaves, far_all % leaves
    piece = (block - owner) % blocks - 1
    far_ids = jnp.where(within % classes == mine_id, piece * mine + within // classes, -1)

    skel_cls, order_cls, interp_cls = of_class(skel), of_class(order), of_class(interp)
    (skel_p,) = call(skel_points_body, [((mine, dim, rank), BF)], [VMEM] * 2, (cls_pts, skel_cls))
    far_p = jnp.concatenate(from_others(skel_p, "leaf"), axis=0)
    tree_w, skel_w = call(
        weights_body,
        [((mine, 2 * cols, size), BF), ((mine, 2 * cols, rank), BF)],
        [VMEM] * 5,
        (wts, other_wts, order_cls, skel_cls, interp_cls),
        [pltpu.VMEM((2 * cols * (leaves * size // 256), 256), BF)],
    )
    left_w = lax.ppermute(tree_w[mine - halo :], "leaf", up)
    right_w = lax.ppermute(tree_w[:halo], "leaf", down)
    far_w = jnp.concatenate(from_others(skel_w, "leaf"), axis=0)
    wide = dim + EXTRA
    near, tgt, far_tgt = call(
        functools.partial(near_body, halo, scale),
        [((leaves, 2 * cols, size), F32), ((leaves, wide, size), BF), ((leaves, wide, rank), BF)],
        [SMEM, SMEM, VMEM, VMEM, VMEM],
        (mine_id.reshape(1), cnt, pts, tree_w, skel),
        [pltpu.VMEM((mine, size, wide), BF), pltpu.SMEM((mine + 1,), jnp.int32)],
    )
    far_n = (blocks - 1) * mine
    own, other = call(
        functools.partial(far_body, halo, mine, scale),
        [((cols, leaves * size), F32), ((cols, leaves * size), BF)],
        [SMEM, SMEM] + [VMEM] * 11,
        (cnt, far_ids, near, tgt, left_p, right_p, left_w, right_w, far_tgt, far_p, far_w, interp, skel),
        [
            pltpu.VMEM((2 * halo, size, wide), BF),
            pltpu.VMEM((2 * halo, 2 * cols, size), BF),
            pltpu.VMEM((far_n, rank, wide), BF),
            pltpu.VMEM((leaves + 1, 2 * cols, rank), F32),
            pltpu.SMEM((halo + 1,), jnp.int32),
            pltpu.SMEM((leaves * slot_n + 8,), jnp.int32),
            pltpu.SMEM((leaves * slot_n + 8,), jnp.int32),
        ],
    )
    (back,) = from_others(other, "rhs")
    both = (own + back.astype(F32)).astype(BF)
    parts = [both] + from_others(both, "pair") if pair_n == 2 else list(lax.all_gather(both, "pair"))
    (out,) = call(
        functools.partial(place_body, len(parts)),
        [((cols, leaves * size), F32)],
        [VMEM] * (1 + len(parts)),
        (tree_order, *parts),
        [pltpu.VMEM((leaves * size // 256 * cols, 256), F32)],
    )
    return out.T


def solution(mesh):
    return jax.shard_map(
        on_device,
        mesh=mesh,
        in_specs=(
            P(("groups", "leaf"), None, None),
            P(("groups", "leaf"), "rhs"),
            P(("groups", "leaf"), None, None),
            P(("groups", "leaf"), None),
            P(("groups", "leaf"), None),
            P(("groups", "leaf"), "pair"),
            P(("groups", "leaf"), "pair"),
        ),
        out_specs=P(("groups", "leaf"), "rhs"),
        check_vma=False,
    )
```

time: 701 us -> 84.1 us (0.12); the launches traced: 688 us -> 83.9 us
  local copies, waits for them, and re-layouts: 426 us -> 5.14 us
  matrix products: 136 us -> 0 us
  other arithmetic: 50.6 us -> 2.11 us
  Pallas kernels: 0 us -> 41.5 us
  blocking collectives: 18 us -> 0 us
  between operations: 14.2 us -> 0.3 us
    gather x4 -> x0, local copies, waits for them, and re-layouts: 182 us -> none  [the longest x1 119 us: on_device(): placed = jnp.take_along_axis(expanded, skel_inverse[:, :, None], axis=1)]
    dot_general x40 -> x0, matrix products: 136 us -> none  [the longest x8 69.9 us: near_group(): jnp.einsum('gmn,gnc->gmc', block, source_weights, preferred_element_type=...]
    reshape x28 -> x2, local copies, waits for them, and re-layouts: 95.5 us -> 0.1 us  [the longest x1 0.07 us: on_device(): far_all = every[:, :, near_n:].reshape(leaves, -1)]
    unnamed x39 -> x10, local copies, waits for them, and re-layouts: 68.7 us -> 1.29 us
    pallas_call x0 -> x5, Pallas kernels: none -> 41.5 us  [call(): pl.pallas_call(body, out_shape=outs, in_specs=specs, out_specs=[VMEM] * l...]
    another operation x5 -> x2, local copies, waits for them, and re-layouts: 33.4 us -> 0.86 us  [of_class(): cut = array.reshape((mine, classes) + array.shape[1:])]
    reduce_sum x18 -> x1, other arithmetic: 32.3 us -> 0.41 us  [on_device(): cnt = jnp.sum((near_all[:, None, :] == table).astype(jnp.int32), axis=2)]
    all_to_all x3 -> x0, starting transfers between devices: 18.6 us -> none  [the longest x1 8.18 us: on_device(): lax.all_to_all(pick(skel_points, wanted), 'leaf', split_axis=0, concat_ax...]
  transfers between devices with their start and end apart: 6 -> 14, of which waited for: 1 -> 4; matrix products, arithmetic and copies ran while one was open for 83% -> 6% of each run, Pallas kernels for 0% -> 21%
where the time goes in v1:
time: 84.1 us; the launch traced here: 83.9 us
  Pallas kernels  41.5 us (49%)
  starting transfers between devices  20.9 us (25%)
  waiting for transfers between devices  13.9 us (17%)
  local copies, waits for them, and re-layouts  5.14 us (6%)
  other arithmetic  2.11 us (3%)
    pallas_call x5, Pallas kernels, call(): pl.pallas_call(body, out_shape=outs, in_specs=specs, out_specs=[VMEM] * l...  41.5 us
    ppermute x10, waiting for transfers between devices, from_others(): lax.ppermute(value, axis, ring(count, by))  9.88 us
    ppermute x10, starting transfers between devices, from_others(): lax.ppermute(value, axis, ring(count, by))  9.26 us
    ppermute x1, starting transfers between devices, on_device(): left_p = lax.ppermute(cls_pts[mine - halo:], 'leaf', up)  3.92 us
    ppermute x1, waiting for transfers between devices, on_device(): left_w = lax.ppermute(tree_w[mine - halo:], 'leaf', up)  3.84 us
    ppermute x1, starting transfers between devices, on_device(): right_w = lax.ppermute(tree_w[:halo], 'leaf', down)  3.82 us
    squeeze x4, local copies, waits for them, and re-layouts, of_class(): return lax.dynamic_index_in_dim(cut, mine_id, 1, keepdims=False)  2.11 us
    ppermute x1, starting transfers between devices, on_device(): left_w = lax.ppermute(tree_w[mine - halo:], 'leaf', up)  2.02 us
  transfers between devices with their start and end apart: 14, of which 4 were waited for; matrix products, arithmetic and copies ran while one was open for 6% of the time, Pallas kernels for 21%

profile of v1, /device:TPU:8, one launch (start us, length us, event | category | flops | bytes accessed | tf_op | source)
XLA Modules:
  0.0 83.9 jit_solution(1294184399958716679)
XLA Ops:
  0.0 0.8 %reshape_reshape.7 = s32[4,4,1,512]{3,1,0,2:T(4,128)S(1)} reshape(s32[16,512]{1,0:T(8,128)} %param.11) | data formatting | bytes 65536 | tf_op jit(solution)/shard_map/reshape;reshape | solution.py:270
  0.9 1.0 %dynamic-slice_bitcast_fusion.1 = (bf16[4,64,512]{2,1,0:T(8,128)(2,1)S(1)}, bf16[4,1,64,512]{3,2,0,1:T(8,128)(2,1)S(1)}) fusion(bf16[4,4,64,512]{3,2,1,0:T(8,128)(2,1)} %bitcast.31, s32[]{:T(128)S(6)} %select_n.42), kind=kLoop, calls=%fused_computation.3 | loop fusion | bytes 786436 | tf_op jit(solution)/shard_map/jit(dynamic_index_in_dim)/squeeze | solution.py:271
  2.3 3.0 %collective-permute-start.7 = (bf16[4,64,256]{2,1,0:T(8,128)(2,1)S(1)}, bf16[4,64,256]{2,1,0:T(8,128)(2,1)S(1)}, u32[]{:S(2)}, u32[]{:S(2)}) collective-permute-start(bf16[4,64,256]{2,1,0:T(8,128)(2,1)S(1)} %shard_map.75), channel_id=1, source_target_pairs={{0,8},{4,12},{8,0},{12,4},{1,9},{5,13},{9,1},{13,5},{2,10},{6,14},... | collective-permute-start | bytes 393224 | tf_op jit(solution)/shard_map/ppermute | solution.py:253
  5.3 2.5 %collective-permute-start.6 = (bf16[4,64,256]{2,1,0:T(8,128)(2,1)S(1)}, bf16[4,64,256]{2,1,0:T(8,128)(2,1)S(1)}, u32[]{:S(2)}, u32[]{:S(2)}) collective-permute-start(bf16[4,64,256]{2,1,0:T(8,128)(2,1)S(1)} %shard_map.75), channel_id=1, source_target_pairs={{0,4},{4,8},{8,12},{12,0},{1,5},{5,9},{9,13},{13,1},{2,6},{6,10},{... | collective-permute-start | bytes 393224 | tf_op jit(solution)/shard_map/ppermute | solution.py:253
  7.8 0.7 constant_dynamic-update-slice_fusion.1
  8.4 0.7 constant_dynamic-update-slice_fusion
  9.1 1.5 %collective-permute-start = (s32[16,12]{0,1:T(8,128)S(1)}, s32[16,12]{0,1:T(8,128)S(1)}, u32[]{:S(2)}, u32[]{:S(2)}) collective-permute-start(s32[16,12]{0,1:T(8,128)S(1)} %constant_dynamic-update-slice_fusion), channel_id=1, source_target_pairs={{0,2},{2,0},{1,3},{3,1},{4,6},{6,4},{5,7},{7,5},{8,10},{10,8},{9,1... | collective-permute-start | bytes 2312 | tf_op jit(solution)/shard_map/ppermute | solution.py:253
  10.6 0.6 broadcast.51
  11.2 1.5 %reduce.3 = s32[8192]{0:T(1024)S(1)} reduce(s32[1,8192]{1,0:T(1,128)} %order_ref.1, s32[]{:T(128)} %broadcast.51), dimensions={0}, to_apply=%param.10.reduce_sub_computation.3 | reduce | bytes 65540 | tf_op args[3]
  12.8 1.1 %dynamic-slice_bitcast_fusion.interp_ref = bf16[4,256,256]{2,1,0:T(8,128)(2,1)S(1)} fusion(bf16[4,4,256,256]{3,2,1,0:T(8,128)(2,1)} %bitcast.35, s32[]{:T(128)S(6)} %select_n.42), kind=kLoop, calls=%fused_computation.1 | loop fusion | bytes 1048580 | tf_op jit(solution)/shard_map/jit(dynamic_index_in_dim)/squeeze | solution.py:271
  14.0 1.9 %collective-permute-start.3 = (bf16[2,64,512]{2,1,0:T(8,128)(2,1)S(1)}, bf16[2,64,512]{2,1,0:T(8,128)(2,1)S(1)}, u32[]{:S(2)}, u32[]{:S(2)}) collective-permute-start(bf16[2,64,512]{2,1,0:T(8,128)(2,1)S(1)} %get-tuple-element.21), channel_id=1, source_target_pairs={{4,0},{8,4},{12,8},{5,1},{9,5},{13,9},{6,2},{10,6},{14,10},{7,3},{... | collective-permute-start | bytes 393224 | tf_op jit(solution)/shard_map/ppermute | solution.py:281
  16.1 0.4 convert_reduce_fusion.cnt_ref
  16.5 3.9 %collective-permute-start.2 = (bf16[2,64,512]{2,1,0:T(8,128)(2,1)S(1)}, bf16[2,64,512]{2,1,0:T(8,128)(2,1)S(1)}, u32[]{:S(2)}, u32[]{:S(2)}) collective-permute-start(bf16[2,64,512]{2,1,0:T(8,128)(2,1)S(1)} %get-tuple-element.22), channel_id=1, source_target_pairs={{0,4},{4,8},{8,12},{1,5},{5,9},{9,13},{2,6},{6,10},{10,14},{3,7},{... | collective-permute-start | bytes 393224 | tf_op jit(solution)/shard_map/ppermute | solution.py:280
  20.6 3.0 %shard_map.73 = (bf16[4,32,512]{2,1,0:T(8,128)(2,1)S(1)}, bf16[4,32,256]{2,1,0:T(8,128)(2,1)S(1)}) custom-call(bf16[16,8192]{1,0:T(8,128)(2,1)S(1)} %bitcast.34, bf16[16,8192]{1,0:T(8,128)(2,1)S(1)} %collective-permute-done.1.other_ref, s32[4,1,512]{2,1,0:T(1,128)S(1)} %dynamic-slice_bitcast_fusion.4.order_ref, ...), custom_call_target="tpu_custom_call" | custom-call | tf_op jit(solution)/shard_map/pallas_call | solution.py:21
  23.6 1.5 %collective-permute-start.10 = (bf16[4,32,256]{2,1,0:T(8,128)(2,1)S(1)}, bf16[4,32,256]{2,1,0:T(8,128)(2,1)S(1)}, u32[]{:S(2)}, u32[]{:S(2)}) collective-permute-start(bf16[4,32,256]{2,1,0:T(8,128)(2,1)S(1)} %get-tuple-element.16), channel_id=1, source_target_pairs={{0,8},{4,12},{8,0},{12,4},{1,9},{5,13},{9,1},{13,5},{2,10},{6,14},... | collective-permute-start | bytes 196616 | tf_op jit(solution)/shard_map/ppermute | solution.py:253
  25.0 0.6 collective-permute-start.9
  25.6 14.6 %shard_map.74 = (f32[16,32,512]{2,1,0:T(8,128)S(1)}, bf16[16,80,512]{2,1,0:T(8,128)(2,1)S(1)}, bf16[16,80,256]{2,1,0:T(8,128)(2,1)S(1)}) custom-call(s32[1]{0:T(128)} %bitcast.4.where_ref, s32[16,8]{1,0:T(8,128)S(1)} %convert_reduce_fusion.cnt_ref, bf16[16,64,512]{2,1,0:T(8,128)(2,1)S(1)} %bitcast.32, bf16[4,32,512]{2,1,0:T(8,128)(2,1)S(1)} %get-tuple-element.12.tw_ref, ...), custom_call_target="tpu_custom_call" | custom-call | tf_op jit(solution)/shard_map/pallas_call | solution.py:21
  40.3 3.8 %collective-permute-start.5 = (bf16[2,32,512]{2,1,0:T(8,128)(2,1)S(1)}, bf16[2,32,512]{2,1,0:T(8,128)(2,1)S(1)}, u32[]{:S(2)}, u32[]{:S(2)}) collective-permute-start(bf16[2,32,512]{2,1,0:T(8,128)(2,1)S(1)} %get-tuple-element.23), channel_id=1, source_target_pairs={{4,0},{8,4},{12,8},{5,1},{9,5},{13,9},{6,2},{10,6},{14,10},{7,3},{... | collective-permute-start | bytes 196616 | tf_op jit(solution)/shard_map/ppermute | solution.py:304
  44.1 2.0 %collective-permute-start.4 = (bf16[2,32,512]{2,1,0:T(8,128)(2,1)S(1)}, bf16[2,32,512]{2,1,0:T(8,128)(2,1)S(1)}, u32[]{:S(2)}, u32[]{:S(2)}) collective-permute-start(bf16[2,32,512]{2,1,0:T(8,128)(2,1)S(1)} %get-tuple-element.24), channel_id=1, source_target_pairs={{0,4},{4,8},{8,12},{1,5},{5,9},{9,13},{2,6},{6,10},{10,14},{3,7},{... | collective-permute-start | bytes 196616 | tf_op jit(solution)/shard_map/ppermute | solution.py:303
  46.4 3.8 %collective-permute-done.4.left_w = bf16[2,32,512]{2,1,0:T(8,128)(2,1)S(1)} collective-permute-done((bf16[2,32,512]{2,1,0:T(8,128)(2,1)S(1)}, bf16[2,32,512]{2,1,0:T(8,128)(2,1)S(1)}, u32[]{:S(2)}, u32[]{:S(2)}) %collective-permute-start.4) | collective-permute-done | bytes 65568 | tf_op jit(solution)/shard_map/ppermute | solution.py:303
  50.3 20.4 %shard_map.76 = (f32[16,8192]{1,0:T(8,128)S(1)}, bf16[16,8192]{1,0:T(8,128)(2,1)S(1)}) custom-call(s32[16,8]{1,0:T(8,128)S(1)} %convert_reduce_fusion.cnt_ref, s32[16,8]{1,0:T(8,128)S(1)} %fusion.6.far_ref, f32[16,32,512]{2,1,0:T(8,128)S(1)} %get-tuple-element.13.near_ref, bf16[16,80,512]{2,1,0:T(8,128)(2,1)S(1)} %get-tuple-element.14.tgt_ref, ...), custom_call_target="tpu_custom_call" | custom-call | tf_op jit(solution)/shard_map/pallas_call | solution.py:21
  70.7 1.5 %collective-permute-done.12 = bf16[16,8192]{1,0:T(8,128)(2,1)S(1)} collective-permute-done((bf16[16,8192]{1,0:T(8,128)(2,1)S(1)}, bf16[16,8192]{1,0:T(8,128)(2,1)S(1)}, u32[]{:S(2)}, u32[]{:S(2)}) %collective-permute-start.12) | collective-permute-done | bytes 262176 | tf_op jit(solution)/shard_map/ppermute | solution.py:253
  72.4 8.3 %collective-permute-done.13.refs_1_ = bf16[16,8192]{1,0:T(8,128)(2,1)S(1)} collective-permute-done((bf16[16,8192]{1,0:T(8,128)(2,1)S(1)}, bf16[16,8192]{1,0:T(8,128)(2,1)S(1)}, u32[]{:S(2)}, u32[]{:S(2)}) %collective-permute-start.13) | collective-permute-done | bytes 262176 | tf_op jit(solution)/shard_map/ppermute | solution.py:253
  80.7 3.2 %shard_map.77 = f32[16,8192]{1,0:T(8,128)} custom-call(s32[1,8192]{1,0:T(1,128)S(1)} %copy-done.2, bf16[16,8192]{1,0:T(8,128)(2,1)S(1)} %add_convert_fusion.refs_0_, bf16[16,8192]{1,0:T(8,128)(2,1)S(1)} %collective-permute-done.13.refs_1_), custom_call_target="tpu_custom_call" | custom-call | tf_op jit(solution)/shard_map/pallas_call | solution.py:21
  (40 shorter events, 1.2 us)
Async XLA Ops:
  0.0 13.9 %copy-start.3 = (s32[16,512]{1,0:T(8,128)S(1)}, s32[16,512]{1,0:T(8,128)}, u32[]{:S(2)}) copy-start(s32[16,512]{1,0:T(8,128)} %param.11) | copy-start | bytes 98308
  0.0 20.5 %copy-start.1 = (bf16[8192,16]{0,1:T(8,128)(2,1)S(1)}, bf16[8192,16]{0,1:T(8,128)(2,1)}, u32[]{:S(2)}) copy-start(bf16[8192,16]{0,1:T(8,128)(2,1)} %param.8) | copy-start | bytes 786436
  2.2 23.4 %copy-start = (bf16[16,512,64]{1,2,0:T(8,128)(2,1)S(1)}, bf16[16,512,64]{1,2,0:T(8,128)(2,1)}, u32[]{:S(2)}) copy-start(bf16[16,512,64]{1,2,0:T(8,128)(2,1)} %param.7) | copy-start | bytes 3145732
  2.2 14.3 %collective-permute-start.8 = (bf16[4,64,256]{2,1,0:T(8,128)(2,1)S(1)}, bf16[4,64,256]{2,1,0:T(8,128)(2,1)S(1)}, u32[]{:S(2)}, u32[]{:S(2)}) collective-permute-start(bf16[4,64,256]{2,1,0:T(8,128)(2,1)S(1)} %shard_map.75), channel_id=1, source_target_pairs={{0,12},{4,0},{8,4},{12,8},{1,13},{5,1},{9,5},{13,9},{2,14},{6,2},{... | collective-permute-start | bytes 393224 | tf_op jit(solution)/shard_map/ppermute | solution.py:253
  2.3 18.2 %collective-permute-start.7 = (bf16[4,64,256]{2,1,0:T(8,128)(2,1)S(1)}, bf16[4,64,256]{2,1,0:T(8,128)(2,1)S(1)}, u32[]{:S(2)}, u32[]{:S(2)}) collective-permute-start(bf16[4,64,256]{2,1,0:T(8,128)(2,1)S(1)} %shard_map.75), channel_id=1, source_target_pairs={{0,8},{4,12},{8,0},{12,4},{1,9},{5,13},{9,1},{13,5},{2,10},{6,14},... | collective-permute-start | bytes 393224 | tf_op jit(solution)/shard_map/ppermute | solution.py:253
  5.3 15.2 %collective-permute-start.6 = (bf16[4,64,256]{2,1,0:T(8,128)(2,1)S(1)}, bf16[4,64,256]{2,1,0:T(8,128)(2,1)S(1)}, u32[]{:S(2)}, u32[]{:S(2)}) collective-permute-start(bf16[4,64,256]{2,1,0:T(8,128)(2,1)S(1)} %shard_map.75), channel_id=1, source_target_pairs={{0,4},{4,8},{8,12},{12,0},{1,5},{5,9},{9,13},{13,1},{2,6},{6,10},{... | collective-permute-start | bytes 393224 | tf_op jit(solution)/shard_map/ppermute | solution.py:253
  9.1 4.8 %collective-permute-start = (s32[16,12]{0,1:T(8,128)S(1)}, s32[16,12]{0,1:T(8,128)S(1)}, u32[]{:S(2)}, u32[]{:S(2)}) collective-permute-start(s32[16,12]{0,1:T(8,128)S(1)} %constant_dynamic-update-slice_fusion), channel_id=1, source_target_pairs={{0,2},{2,0},{1,3},{3,1},{4,6},{6,4},{5,7},{7,5},{8,10},{10,8},{9,1... | collective-permute-start | bytes 2312 | tf_op jit(solution)/shard_map/ppermute | solution.py:253
  10.6 9.9 %collective-permute-start.1 = (bf16[16,8192]{1,0:T(8,128)(2,1)}, bf16[16,8192]{1,0:T(8,128)(2,1)S(1)}, u32[]{:S(2)}, u32[]{:S(2)}) collective-permute-start(bf16[16,8192]{1,0:T(8,128)(2,1)} %bitcast.33), channel_id=1, source_target_pairs={{0,1},{1,0},{2,3},{3,2},{4,5},{5,4},{6,7},{7,6},{8,9},{9,8},{10,11... | collective-permute-start | bytes 786440 | tf_op jit(solution)/shard_map/ppermute | solution.py:253
  14.0 32.2 %collective-permute-start.3 = (bf16[2,64,512]{2,1,0:T(8,128)(2,1)S(1)}, bf16[2,64,512]{2,1,0:T(8,128)(2,1)S(1)}, u32[]{:S(2)}, u32[]{:S(2)}) collective-permute-start(bf16[2,64,512]{2,1,0:T(8,128)(2,1)S(1)} %get-tuple-element.21), channel_id=1, source_target_pairs={{4,0},{8,4},{12,8},{5,1},{9,5},{13,9},{6,2},{10,6},{14,10},{7,3},{... | collective-permute-start | bytes 393224 | tf_op jit(solution)/shard_map/ppermute | solution.py:281
  16.5 29.7 %collective-permute-start.2 = (bf16[2,64,512]{2,1,0:T(8,128)(2,1)S(1)}, bf16[2,64,512]{2,1,0:T(8,128)(2,1)S(1)}, u32[]{:S(2)}, u32[]{:S(2)}) collective-permute-start(bf16[2,64,512]{2,1,0:T(8,128)(2,1)S(1)} %get-tuple-element.22), channel_id=1, source_target_pairs={{0,4},{4,8},{8,12},{1,5},{5,9},{9,13},{2,6},{6,10},{10,14},{3,7},{... | collective-permute-start | bytes 393224 | tf_op jit(solution)/shard_map/ppermute | solution.py:280
  23.5 16.7 %collective-permute-start.11 = (bf16[4,32,256]{2,1,0:T(8,128)(2,1)S(1)}, bf16[4,32,256]{2,1,0:T(8,128)(2,1)S(1)}, u32[]{:S(2)}, u32[]{:S(2)}) collective-permute-start(bf16[4,32,256]{2,1,0:T(8,128)(2,1)S(1)} %get-tuple-element.16), channel_id=1, source_target_pairs={{0,12},{4,0},{8,4},{12,8},{1,13},{5,1},{9,5},{13,9},{2,14},{6,2},{... | collective-permute-start | bytes 196616 | tf_op jit(solution)/shard_map/ppermute | solution.py:253
  23.6 20.5 %collective-permute-start.10 = (bf16[4,32,256]{2,1,0:T(8,128)(2,1)S(1)}, bf16[4,32,256]{2,1,0:T(8,128)(2,1)S(1)}, u32[]{:S(2)}, u32[]{:S(2)}) collective-permute-start(bf16[4,32,256]{2,1,0:T(8,128)(2,1)S(1)} %get-tuple-element.16), channel_id=1, source_target_pairs={{0,8},{4,12},{8,0},{12,4},{1,9},{5,13},{9,1},{13,5},{2,10},{6,14},... | collective-permute-start | bytes 196616 | tf_op jit(solution)/shard_map/ppermute | solution.py:253
  25.0 21.1 %collective-permute-start.9 = (bf16[4,32,256]{2,1,0:T(8,128)(2,1)S(1)}, bf16[4,32,256]{2,1,0:T(8,128)(2,1)S(1)}, u32[]{:S(2)}, u32[]{:S(2)}) collective-permute-start(bf16[4,32,256]{2,1,0:T(8,128)(2,1)S(1)} %get-tuple-element.16), channel_id=1, source_target_pairs={{0,4},{4,8},{8,12},{12,0},{1,5},{5,9},{9,13},{13,1},{2,6},{6,10},{... | collective-permute-start | bytes 196616 | tf_op jit(solution)/shard_map/ppermute | solution.py:253
  40.3 6.2 %collective-permute-start.5 = (bf16[2,32,512]{2,1,0:T(8,128)(2,1)S(1)}, bf16[2,32,512]{2,1,0:T(8,128)(2,1)S(1)}, u32[]{:S(2)}, u32[]{:S(2)}) collective-permute-start(bf16[2,32,512]{2,1,0:T(8,128)(2,1)S(1)} %get-tuple-element.23), channel_id=1, source_target_pairs={{4,0},{8,4},{12,8},{5,1},{9,5},{13,9},{6,2},{10,6},{14,10},{7,3},{... | collective-permute-start | bytes 196616 | tf_op jit(solution)/shard_map/ppermute | solution.py:304
  44.1 6.2 %collective-permute-start.4 = (bf16[2,32,512]{2,1,0:T(8,128)(2,1)S(1)}, bf16[2,32,512]{2,1,0:T(8,128)(2,1)S(1)}, u32[]{:S(2)}, u32[]{:S(2)}) collective-permute-start(bf16[2,32,512]{2,1,0:T(8,128)(2,1)S(1)} %get-tuple-element.24), channel_id=1, source_target_pairs={{0,4},{4,8},{8,12},{1,5},{5,9},{9,13},{2,6},{6,10},{10,14},{3,7},{... | collective-permute-start | bytes 196616 | tf_op jit(solution)/shard_map/ppermute | solution.py:303
  50.3 30.5 %copy-start.2 = (s32[1,8192]{1,0:T(1,128)S(1)}, s32[1,8192]{1,0:T(1,128)}, u32[]{:S(2)}) copy-start(s32[1,8192]{1,0:T(1,128)} %order_ref.1) | copy-start | bytes 98308
  70.7 1.6 %collective-permute-start.12 = (bf16[16,8192]{1,0:T(8,128)(2,1)S(1)}, bf16[16,8192]{1,0:T(8,128)(2,1)S(1)}, u32[]{:S(2)}, u32[]{:S(2)}) collective-permute-start(bf16[16,8192]{1,0:T(8,128)(2,1)S(1)} %get-tuple-element.18), channel_id=1, source_target_pairs={{0,1},{1,0},{2,3},{3,2},{4,5},{5,4},{6,7},{7,6},{8,9},{9,8},{10,11... | collective-permute-start | bytes 786440 | tf_op jit(solution)/shard_map/ppermute | solution.py:253
  72.3 8.4 %collective-permute-start.13 = (bf16[16,8192]{1,0:T(8,128)(2,1)S(1)}, bf16[16,8192]{1,0:T(8,128)(2,1)S(1)}, u32[]{:S(2)}, u32[]{:S(2)}) collective-permute-start(bf16[16,8192]{1,0:T(8,128)(2,1)S(1)} %add_convert_fusion.refs_0_), channel_id=1, source_target_pairs={{0,2},{2,0},{1,3},{3,1},{4,6},{6,4},{5,7},{7,5},{8,10},{10,8},{9,1... | collective-permute-start | bytes 786440 | tf_op jit(solution)/shard_map/ppermute | solution.py:253

commit v2 on v1

v2 whole, which is shorter than its diff:
```python
import functools

import jax
import jax.numpy as jnp
from jax import lax
from jax.experimental import pallas as pl
from jax.experimental.pallas import tpu as pltpu
from jax.sharding import PartitionSpec as P

BF = jnp.bfloat16
F32 = jnp.float32
LOG2E = 1.4426950408889634
EXTRA = 16
GROUP = 4
VMEM = pl.BlockSpec(memory_space=pltpu.VMEM)
SMEM = pl.BlockSpec(memory_space=pltpu.SMEM)
PARAMS = pltpu.CompilerParams(vmem_limit_bytes=48 << 20)


def call(body, shapes, specs, args, scratch=(), flops=0, out_specs=None):
    outs = [jax.ShapeDtypeStruct(s, d) for s, d in shapes]
    return pl.pallas_call(
        body,
        out_shape=outs,
        in_specs=specs,
        out_specs=out_specs or [VMEM] * len(outs),
        scratch_shapes=list(scratch),
        compiler_params=PARAMS,
        cost_estimate=pl.CostEstimate(flops=flops, bytes_accessed=1 << 20, transcendentals=0),
    )(*args)


def extra_rows(feat, ones_first):
    wide = feat.astype(F32)
    half = -0.5 * jnp.sum(wide * wide, axis=0, keepdims=True)
    high = half.astype(BF).astype(F32)
    mid = (half - high).astype(BF).astype(F32)
    low = half - high - mid
    row = lax.broadcasted_iota(jnp.int32, (EXTRA, feat.shape[1]), 0)
    at = 3 if ones_first else 0
    ones = (row < 3) if ones_first else (row >= 3) & (row < 6)
    picked = jnp.where(row == at, high, jnp.where(row == at + 1, mid, jnp.where(row == at + 2, low, 0.0)))
    return jnp.where(ones, 1.0, picked).astype(BF)


def as_targets(feat):
    return jnp.concatenate([feat, extra_rows(feat, False)], axis=0)


def as_sources(feat):
    return jnp.concatenate([feat, extra_rows(feat, True)], axis=0).astype(F32).T.astype(BF)


def one_hot(row_ids, count):
    rows = lax.broadcasted_iota(jnp.int32, (count, row_ids.shape[1]), 0)
    return jnp.where(rows == row_ids, 1.0, 0.0).astype(BF)


def dot(a, b):
    return jnp.dot(a, b, preferred_element_type=F32)


def dot_last(a, b):
    return lax.dot_general(a, b, (((1,), (1,)), ((), ())), preferred_element_type=F32)


def gauss(sources, targets, scale):
    return jnp.exp2(dot(sources, targets) * scale).astype(BF)


def halo_body(ids_ref, pts_ref, near_ref, far_ref, up_ref, down_ref, pairs_ref, sems):
    halo = up_ref.shape[0]
    mine = ids_ref[2]
    classes = ids_ref[3]
    copies = []
    for j in range(halo):
        first = mine + j * classes
        last = mine + (pts_ref.shape[0] // 2) + j * classes
        copies.append(pltpu.make_async_copy(pts_ref.at[last], up_ref.at[j], sems.at[j]))
        copies.append(pltpu.make_async_copy(pts_ref.at[first], down_ref.at[j], sems.at[halo + j]))
    for copy in copies:
        copy.start()
    near_n = near_ref.shape[0]
    pairs_ref[:near_n] = near_ref[...]
    pairs_ref[near_n:] = far_ref[...]
    for copy in copies:
        copy.wait()


def weights_body(
    blocks, classes, near_n, ids_ref, own_ref, other_ref, order_ref, skel_ref, interp_ref, pts_ref, *refs
):
    pair_refs = refs[:-7]
    tw_ref, up_ref, down_ref, message_ref, cnt_ref, far_ref, stack = refs[-7:]
    cols = own_ref.shape[0]
    step = 2 * cols
    width = stack.shape[1]
    turns = own_ref.shape[1] // width
    mine, _, size = tw_ref.shape
    halo = up_ref.shape[0]
    rank = message_ref.shape[2]
    dim = pts_ref.shape[1]
    leaves = pts_ref.shape[0]
    block, base, me = ids_ref[0], ids_ref[1], ids_ref[2]
    for hi in range(turns):
        span = slice(hi * width, (hi + 1) * width)
        stack[hi * step : hi * step + cols] = own_ref[:, span]
        stack[hi * step + cols : (hi + 1) * step] = other_ref[:, span]

    for e in range(cnt_ref.shape[0]):
        wanted = base + e * classes + me
        total = None
        for ref in pair_refs:
            part = jnp.sum(jnp.where(ref[:near_n] == wanted, 1, 0), axis=0, keepdims=True)
            total = part if total is None else total + part
        cnt_ref[e : e + 1] = total
    far_n = far_ref.shape[0] // len(pair_refs)
    for k, ref in enumerate(pair_refs):
        named = ref[near_n:]
        owner = lax.div(named, leaves)
        within = lax.rem(named, leaves)
        piece = lax.rem(block - owner + blocks, blocks) - 1
        target = lax.broadcasted_iota(jnp.int32, named.shape, 1)
        code = target * 256 + piece * mine + lax.div(within, classes)
        far_ref[k * far_n : (k + 1) * far_n] = jnp.where(lax.rem(within, classes) == me, code, -1)

    for j in range(mine):
        leaf = j * classes + me
        ids = order_ref[:, pl.ds(pl.multiple_of(leaf * size, size), size)]
        hi_ids = lax.shift_right_logical(ids, width.bit_length() - 1)
        picked = dot(stack[...], one_hot(ids & (width - 1), width))
        total = jnp.zeros((step, size), F32)
        for hi in range(turns):
            total = total + jnp.where(hi_ids == hi, picked[hi * step : (hi + 1) * step], 0.0)
        tree = total.astype(BF)
        tw_ref[j] = tree
        if j < halo:
            down_ref[j] = tree
        if j >= mine - halo:
            up_ref[j - (mine - halo)] = tree
        hot = one_hot(skel_ref[pl.ds(leaf, 1), :], size)
        ordered = dot(tree, hot)
        combined = dot_last(ordered[:, rank:].astype(BF), interp_ref[leaf])
        message_ref[j, :dim] = dot(pts_ref[leaf], hot[:, :rank]).astype(BF)
        message_ref[j, dim:] = (ordered[:, :rank] + combined).astype(BF)


def near_sum(t, first, count, most, scale, cnt_ref, slots, tgt, src, weights, write, shift=0):
    found = jnp.int32(0)
    for e in range(count):
        slots[found] = jnp.int32(e)
        found = found + jnp.where(cnt_ref[first + e, t] > 0, 1, 0)
    for k in range(most + 1):

        @pl.when(found == k)
        def _():
            names = [slots[j] for j in range(k)]
            if k == 0:
                write(t, jnp.zeros((weights.shape[1], tgt.shape[2]), F32))
                return
            size = src.shape[1]
            block = gauss(jnp.concatenate([src[s + shift] for s in names], axis=0), tgt[t], scale)
            total = None
            for j, s in enumerate(names):
                times = cnt_ref[first + s, t].astype(F32)
                part = dot(weights[s + shift], block[j * size : (j + 1) * size]) * times
                total = part if total is None else total + part
            write(t, total)


def near_body(
    halo, scale, ids_ref, cnt_ref, pts_ref, tw_ref, left_p, right_p, near_ref, tgt_ref, edge_src, src, slots
):
    leaves = pts_ref.shape[0]
    mine = tw_ref.shape[0]
    classes = leaves // mine

    def sources(j, _):
        src[j] = as_sources(pts_ref[j * classes + ids_ref[2]])
        return 0

    lax.fori_loop(0, mine, sources, 0)
    for j in range(halo):
        edge_src[j] = as_sources(left_p[j])
        edge_src[halo + j] = as_sources(right_p[j])

    def write(t, value):
        near_ref[t] = value

    def target(t, _):
        tgt_ref[t] = as_targets(pts_ref[t])
        near_sum(t, halo, mine, mine, scale, cnt_ref, slots, tgt_ref, src, tw_ref, write)
        return 0

    lax.fori_loop(0, leaves, target, 0)


def edge_body(
    halo, mine, scale, cnt_ref, near_ref, tgt_ref, src, left_w, right_w, pts_ref, skel_ref, order_ref,
    own_ref, other_ref, far_tgt_ref, comp_ref, wts, slots,
):
    leaves, cols2, size = near_ref.shape
    cols = cols2 // 2
    rank = far_tgt_ref.shape[2]
    for j in range(halo):
        wts[j] = left_w[j]
        wts[halo + j] = right_w[j]

    def write(t, value):
        total = near_ref[t] + value
        own_ref[:, pl.ds(pl.multiple_of(t * size, size), size)] = total[:cols]
        other_ref[:, pl.ds(pl.multiple_of(t * size, size), size)] = total[cols:].astype(BF)

    def target(t, _):
        right = jnp.where(t < leaves // 2, 0, 1)
        near_sum(t, right * (halo + mine), halo, halo, scale, cnt_ref, slots, tgt_ref, src, wts, write, right * halo)
        span = pl.ds(pl.multiple_of(t * size, size), size)
        hot = one_hot(skel_ref[pl.ds(t, 1), :], size)
        far_tgt_ref[t] = as_targets(dot(pts_ref[t], hot[:, :rank]).astype(BF))
        ids = order_ref[:, span]
        row = lax.broadcasted_iota(jnp.int32, (16, size), 0)
        halves = jnp.where(row == 0, lax.shift_right_logical(ids, 8), jnp.where(row == 1, ids & 255, 0))
        moved = dot(halves.astype(F32).astype(BF), hot)
        comp_ref[:, span] = (moved[:1] * 256.0 + moved[1:2]).astype(jnp.int32)
        return 0

    lax.fori_loop(0, leaves, target, 0)


def sources_body(mine, far_ref, *refs):
    pieces = refs[:-3]
    far_src, far_w, names = refs[-3:]
    dim = pieces[0].shape[1] - far_w.shape[1]
    for k, piece in enumerate(pieces):
        for j in range(mine):
            far_src[k * mine + j] = as_sources(piece[j, :dim])
            far_w[k * mine + j] = piece[j, dim:]
    found = jnp.int32(0)
    for t in range(far_ref.shape[1]):
        for i in range(far_ref.shape[0]):
            code = far_ref[i, t]
            names[1 + found] = code
            found = found + jnp.where(code >= 0, 1, 0)
    names[0] = found
    for j in range(GROUP):
        names[1 + found + j] = jnp.int32(far_ref.shape[1] * 256)


def far_body(scale, names, far_src, far_w, far_tgt, after_ref, own_ref, other_ref, field):
    leaves, _, rank = far_tgt.shape
    cols = own_ref.shape[0]
    field[...] = jnp.zeros_like(field)

    def far_group(g, _):
        codes = [names[1 + g * GROUP + j] for j in range(GROUP)]
        targets = [lax.shift_right_logical(c, 8) for c in codes]
        blocks = [gauss(far_src[c & 255], far_tgt[t & (leaves - 1)], scale) for c, t in zip(codes, targets)]
        parts = [dot(far_w[c & 255], block) for c, block in zip(codes, blocks)]
        for t, part in zip(targets, parts):
            field[t] += part
        return 0

    lax.fori_loop(0, lax.div(names[0] + GROUP - 1, GROUP), far_group, 0)
    for t in range(leaves):
        own_ref[:, t * rank : (t + 1) * rank] = field[t, :cols]
        other_ref[:, t * rank : (t + 1) * rank] = field[t, cols:].astype(BF)


def scatter(ids, value, width, turns):
    hi_ids = lax.shift_right_logical(ids, width.bit_length() - 1)
    masked = [jnp.where(hi_ids == hi, value, 0.0).astype(BF) for hi in range(turns)]
    return dot_last(jnp.concatenate(masked, axis=0), one_hot(ids & (width - 1), width))


def place_near_body(order_ref, *refs):
    near, acc = refs[:-1], refs[-1]
    total = order_ref.shape[1]
    width = acc.shape[1]
    chunk = 1024
    for at in range(0, total, chunk):
        span = slice(at, at + chunk)
        value = sum(ref[:, span].astype(F32) for ref in near)
        part = scatter(order_ref[:, span], value, width, total // width)
        acc[...] = part if at == 0 else acc[...] + part


def place_far_body(comp_ref, interp_ref, start_ref, *refs):
    far, out_ref, acc = refs[:-2], refs[-2], refs[-1]
    cols, total = out_ref.shape
    width = acc.shape[1]
    turns = total // width
    leaves, rank, _ = interp_ref.shape
    size = total // leaves
    for t in range(leaves):
        skel = sum(ref[:, t * rank : (t + 1) * rank].astype(F32) for ref in far).astype(BF)
        value = jnp.concatenate([skel.astype(F32), dot(skel, interp_ref[t])], axis=1)
        part = scatter(comp_ref[:, t * size : (t + 1) * size], value, width, turns)
        acc[...] = (start_ref if t == 0 else acc)[...] + part
    for hi in range(turns):
        out_ref[:, hi * width : (hi + 1) * width] = acc[hi * cols : (hi + 1) * cols]


def ring(count, by):
    return [(i, (i + by) % count) for i in range(count)]


def from_others(value, axis):
    count = lax.axis_size(axis)
    return [lax.ppermute(value, axis, ring(count, by)) for by in range(1, count)]


def over_pair(value, pair_n):
    if pair_n == 2:
        return [value] + from_others(value, "pair")
    return list(lax.all_gather(value, "pair"))


def on_device(points, weights, interp, tree_order, skel_order, near_pairs, far_pairs):
    leaves, size, dim = points.shape
    rank = interp.shape[1]
    cols = weights.shape[1]
    blocks, pair_n, rhs_n = (lax.axis_size(a) for a in ("leaf", "pair", "rhs"))
    classes = pair_n * rhs_n
    mine = leaves // classes
    span = min(8, leaves)
    halo = span // classes
    block = lax.axis_index("leaf")
    mine_id = lax.axis_index("pair") * rhs_n + lax.axis_index("rhs")
    scale = 2.0 * 2.5 / dim * LOG2E
    near_n, far_n = near_pairs.shape[1], far_pairs.shape[1]
    wide = dim + EXTRA
    mega = 10 ** 9
    ids = jnp.stack([block, block * leaves - span, mine_id, jnp.int32(classes)]).astype(jnp.int32)
    pts = points.transpose(0, 2, 1)
    wts = weights.T
    up, down = [(i, i + 1) for i in range(blocks - 1)], [(i + 1, i) for i in range(blocks - 1)]
    (other_wts,) = from_others(wts, "rhs")
    up_p, down_p, pairs = call(
        halo_body,
        [((halo, dim, size), BF), ((halo, dim, size), BF), ((near_n + far_n, leaves), jnp.int32)],
        [SMEM, pl.BlockSpec(memory_space=pl.ANY), VMEM, VMEM],
        (ids, pts, near_pairs.T, far_pairs.T),
        [pltpu.SemaphoreType.DMA((2 * halo,))],
    )
    every = [pairs] + from_others(pairs, "pair")
    left_p = lax.ppermute(up_p, "leaf", up)
    right_p = lax.ppermute(down_p, "leaf", down)
    tree_w, up_w, down_w, message, cnt, far_ids = call(
        functools.partial(weights_body, blocks, classes, near_n),
        [
            ((mine, 2 * cols, size), BF),
            ((halo, 2 * cols, size), BF),
            ((halo, 2 * cols, size), BF),
            ((mine, dim + 2 * cols, rank), BF),
            ((2 * halo + mine, leaves), jnp.int32),
            ((pair_n * far_n, leaves), jnp.int32),
        ],
        [SMEM] + [VMEM] * (6 + pair_n),
        (ids, wts, other_wts, tree_order, skel_order, interp, pts, *every),
        [pltpu.VMEM((2 * cols * (leaves * size // 256), 256), BF)],
        flops=3 * mega,
    )
    left_w = lax.ppermute(up_w, "leaf", up)
    right_w = lax.ppermute(down_w, "leaf", down)
    pieces = from_others(message, "leaf")
    near, tgt, edge_src = call(
        functools.partial(near_body, halo, scale),
        [((leaves, 2 * cols, size), F32), ((leaves, wide, size), BF), ((2 * halo, size, wide), BF)],
        [SMEM, SMEM, VMEM, VMEM, VMEM, VMEM],
        (ids, cnt, pts, tree_w, left_p, right_p),
        [pltpu.VMEM((mine, size, wide), BF), pltpu.SMEM((mine + 1,), jnp.int32)],
        flops=14 * mega,
    )
    near_own, near_other, far_tgt, comp = call(
        functools.partial(edge_body, halo, mine, scale),
        [((cols, leaves * size), F32), ((cols, leaves * size), BF), ((leaves, wide, rank), BF), ((1, leaves * size), jnp.int32)],
        [SMEM] + [VMEM] * 8,
        (cnt, near, tgt, edge_src, left_w, right_w, pts, skel_order, tree_order),
        [
            pltpu.VMEM((2 * halo, 2 * cols, size), BF),
            pltpu.SMEM((halo + 1,), jnp.int32),
        ],
        flops=6 * mega,
    )
    (near_back,) = from_others(near_other, "rhs")
    near_sum_own = (near_own + near_back.astype(F32)).astype(BF)
    near_parts = over_pair(near_sum_own, pair_n)
    piece_n = (blocks - 1) * mine
    far_src, far_w, names = call(
        functools.partial(sources_body, mine),
        [((piece_n, rank, wide), BF), ((piece_n, 2 * cols, rank), BF), ((leaves * pair_n * far_n + 16,), jnp.int32)],
        [SMEM] + [VMEM] * (blocks - 1),
        (far_ids, *pieces),
        out_specs=[VMEM, VMEM, SMEM],
        flops=2 * mega,
    )
    far_own, far_other = call(
        functools.partial(far_body, scale),
        [((cols, leaves * rank), F32), ((cols, leaves * rank), BF)],
        [SMEM, VMEM, VMEM, VMEM, pl.BlockSpec(memory_space=pl.ANY)],
        (names, far_src, far_w, far_tgt, near_sum_own),
        [pltpu.VMEM((leaves + 1, 2 * cols, rank), F32)],
        flops=4 * mega,
    )
    (far_back,) = from_others(far_other, "rhs")
    far_parts = over_pair((far_own + far_back.astype(F32)).astype(BF), pair_n)
    acc_shape = (leaves * size // 256 * cols, 256)
    (acc,) = call(
        place_near_body,
        [(acc_shape, F32)],
        [VMEM] * (1 + pair_n),
        (tree_order, *near_parts),
        flops=3 * mega,
    )
    (out,) = call(
        place_far_body,
        [((cols, leaves * size), F32)],
        [VMEM] * (3 + pair_n),
        (comp, interp, acc, *far_parts),
        [pltpu.VMEM(acc_shape, F32)],
        flops=4 * mega,
    )
    return out.T


def solution(mesh):
    return jax.shard_map(
        on_device,
        mesh=mesh,
        in_specs=(
            P(("groups", "leaf"), None, None),
            P(("groups", "leaf"), "rhs"),
            P(("groups", "leaf"), None, None),
            P(("groups", "leaf"), None),
            P(("groups", "leaf"), None),
            P(("groups", "leaf"), "pair"),
            P(("groups", "leaf"), "pair"),
        ),
        out_specs=P(("groups", "leaf"), "rhs"),
        check_vma=False,
    )
```

time: 84.1 us -> 76.9 us (0.914)
  waiting for transfers between devices: 13.9 us -> 8.04 us
  Pallas kernels: 41.5 us -> 39 us
  other arithmetic: 2.11 us -> 0.15 us
  local copies, waits for them, and re-layouts: 5.14 us -> 6.67 us
  starting transfers between devices: 20.9 us -> 21.8 us
    unnamed x10 -> x22, local copies, waits for them, and re-layouts: 1.29 us -> 6.67 us
    ppermute x4, waiting for transfers between devices: 4.07 us -> 0.01 us  [the longest x1 0.01 us: on_device(): left_p = lax.ppermute(up_p, 'leaf', up)]
    pallas_call x5 -> x8, Pallas kernels: 41.5 us -> 39 us  [call(): pl.pallas_call(body, out_shape=outs, in_specs=specs, out_specs=out_specs...]
    squeeze x4 -> x0, local copies, waits for them, and re-layouts: 2.11 us -> none  [of_class(): return lax.dynamic_index_in_dim(cut, mine_id, 1, keepdims=False)]
    ppermute x10 -> x9, waiting for transfers between devices: 9.88 us -> 8.03 us  [from_others(): lax.ppermute(value, axis, ring(count, by))]
    unnamed x1 -> x0, other arithmetic: 1.52 us -> none
    ppermute x10 -> x9, starting transfers between devices: 9.26 us -> 10.2 us  [from_others(): lax.ppermute(value, axis, ring(count, by))]
    another operation x2 -> x0, local copies, waits for them, and re-layouts: 0.86 us -> none  [of_class(): cut = array.reshape((mine, classes) + array.shape[1:])]
  transfers between devices with their start and end apart: 14 -> 13, of which waited for: 4 -> 2; matrix products, arithmetic and copies ran while one was open for 6% -> 0% of each run, Pallas kernels for 21% -> 38%
where the time goes in v2:
time: 76.9 us; the launch traced here: 75.9 us
  Pallas kernels  39 us (51%)
  starting transfers between devices  21.8 us (28%)
  waiting for transfers between devices  8.04 us (10%)
  local copies, waits for them, and re-layouts  6.67 us (9%)
    pallas_call x8, Pallas kernels, call(): pl.pallas_call(body, out_shape=outs, in_specs=specs, out_specs=out_specs...  39 us
    ppermute x9, starting transfers between devices, from_others(): lax.ppermute(value, axis, ring(count, by))  10.2 us
    ppermute x9, waiting for transfers between devices, from_others(): lax.ppermute(value, axis, ring(count, by))  8.03 us
    unnamed x22, local copies, waits for them, and re-layouts  6.67 us
    ppermute x1, starting transfers between devices, on_device(): right_w = lax.ppermute(down_w, 'leaf', down)  3.92 us
    ppermute x1, starting transfers between devices, on_device(): left_p = lax.ppermute(up_p, 'leaf', up)  3.47 us
    ppermute x1, starting transfers between devices, on_device(): right_p = lax.ppermute(down_p, 'leaf', down)  2.36 us
    ppermute x1, starting transfers between devices, on_device(): left_w = lax.ppermute(up_w, 'leaf', up)  1.91 us
  transfers between devices with their start and end apart: 13, of which 2 were waited for; matrix products, arithmetic and copies ran while one was open for 0% of the time, Pallas kernels for 38%

profile of v2, /device:TPU:8, one launch (start us, length us, event | category | flops | bytes accessed | tf_op | source)
XLA Modules:
  0.0 75.9 jit_solution(3736767682461141152)
XLA Ops:
  0.1 1.2 %copy-done = bf16[16,512,64]{1,2,0:T(8,128)(2,1)S(1)} copy-done((bf16[16,512,64]{1,2,0:T(8,128)(2,1)S(1)}, bf16[16,512,64]{1,2,0:T(8,128)(2,1)}, u32[]{:S(2)}) %copy-start) | copy-done | bytes 1048600
  2.7 0.9 %shard_map.73 = (bf16[2,64,512]{2,1,0:T(8,128)(2,1)S(1)}, bf16[2,64,512]{2,1,0:T(8,128)(2,1)S(1)}, s32[12,16]{1,0:T(8,128)S(1)}) custom-call(s32[4]{0:T(128)S(1)} %pad_add_fusion.ids_ref, bf16[16,64,512]{2,1,0:T(8,128)(2,1)S(1)} %bitcast.8, s32[8,16]{1,0:T(8,128)S(1)} %bitcast.12, s32[4,16]{1,0:T(4,128)S(1)} %bitcast.13), custom_call_target="tpu_custom_call" | custom-call | bytes 1048576 | tf_op jit(solution)/shard_map/pallas_call | solution.py:22
  3.6 1.6 %collective-permute-start.1 = (s32[12,16]{1,0:T(8,128)S(1)}, s32[12,16]{1,0:T(8,128)S(1)}, u32[]{:S(2)}, u32[]{:S(2)}) collective-permute-start(s32[12,16]{1,0:T(8,128)S(1)} %get-tuple-element.26.refs_0_), channel_id=1, source_target_pairs={{0,2},{2,0},{1,3},{3,1},{4,6},{6,4},{5,7},{7,5},{8,10},{10,8},{9,1... | collective-permute-start | bytes 2312 | tf_op jit(solution)/shard_map/ppermute | solution.py:309
  5.2 3.5 %collective-permute-start.2 = (bf16[2,64,512]{2,1,0:T(8,128)(2,1)S(1)}, bf16[2,64,512]{2,1,0:T(8,128)(2,1)S(1)}, u32[]{:S(2)}, u32[]{:S(2)}) collective-permute-start(bf16[2,64,512]{2,1,0:T(8,128)(2,1)S(1)} %get-tuple-element.29), channel_id=1, source_target_pairs={{0,4},{4,8},{8,12},{1,5},{5,9},{9,13},{2,6},{6,10},{10,14},{3,7},{... | collective-permute-start | bytes 393224 | tf_op jit(solution)/shard_map/ppermute | solution.py:346
  8.6 2.4 %collective-permute-start.3 = (bf16[2,64,512]{2,1,0:T(8,128)(2,1)S(1)}, bf16[2,64,512]{2,1,0:T(8,128)(2,1)S(1)}, u32[]{:S(2)}, u32[]{:S(2)}) collective-permute-start(bf16[2,64,512]{2,1,0:T(8,128)(2,1)S(1)} %get-tuple-element.30), channel_id=1, source_target_pairs={{4,0},{8,4},{12,8},{5,1},{9,5},{13,9},{6,2},{10,6},{14,10},{7,3},{... | collective-permute-start | bytes 393224 | tf_op jit(solution)/shard_map/ppermute | solution.py:347
  11.1 1.6 %copy-done.4 = bf16[16,256,256]{2,1,0:T(8,128)(2,1)S(1)} copy-done((bf16[16,256,256]{2,1,0:T(8,128)(2,1)S(1)}, bf16[16,256,256]{2,1,0:T(8,128)(2,1)}, u32[]{:S(2)}) %copy-start.4) | copy-done | bytes 2097176
  12.6 0.9 %copy-done.6 = bf16[8192,16]{0,1:T(8,128)(2,1)S(1)} copy-done((bf16[8192,16]{0,1:T(8,128)(2,1)S(1)}, bf16[8192,16]{0,1:T(8,128)(2,1)}, u32[]{:S(2)}) %copy-start.6) | copy-done | bytes 262168
  13.6 0.8 copy-done.7
  14.3 0.8 copy-done.9
  15.1 3.2 %shard_map.74 = (bf16[4,32,512]{2,1,0:T(8,128)(2,1)S(1)}, bf16[2,32,512]{2,1,0:T(8,128)(2,1)S(1)}, bf16[2,32,512]{2,1,0:T(8,128)(2,1)S(1)}, bf16[4,96,256]{2,1,0...) custom-call(s32[4]{0:T(128)S(1)} %pad_add_fusion.ids_ref, bf16[16,8192]{1,0:T(8,128)(2,1)S(1)} %bitcast.15, ...), custom_call_target="tpu_custom_call" | custom-call | flops 3000000000 | bytes 1048576 | tf_op jit(solution)/shard_map/pallas_call | solution.py:22
  18.3 2.0 %collective-permute-start.8 = (bf16[4,96,256]{2,1,0:T(8,128)(2,1)S(1)}, bf16[4,96,256]{2,1,0:T(8,128)(2,1)S(1)}, u32[]{:S(2)}, u32[]{:S(2)}) collective-permute-start(bf16[4,96,256]{2,1,0:T(8,128)(2,1)S(1)} %get-tuple-element.40), channel_id=1, source_target_pairs={{0,4},{4,8},{8,12},{12,0},{1,5},{5,9},{9,13},{13,1},{2,6},{6,10},{... | collective-permute-start | bytes 589832 | tf_op jit(solution)/shard_map/ppermute | solution.py:309
  20.3 4.4 %collective-permute-start.9 = (bf16[4,96,256]{2,1,0:T(8,128)(2,1)S(1)}, bf16[4,96,256]{2,1,0:T(8,128)(2,1)S(1)}, u32[]{:S(2)}, u32[]{:S(2)}) collective-permute-start(bf16[4,96,256]{2,1,0:T(8,128)(2,1)S(1)} %get-tuple-element.40), channel_id=1, source_target_pairs={{0,8},{4,12},{8,0},{12,4},{1,9},{5,13},{9,1},{13,5},{2,10},{6,14},... | collective-permute-start | bytes 589832 | tf_op jit(solution)/shard_map/ppermute | solution.py:309
  24.7 1.9 %collective-permute-start.4 = (bf16[2,32,512]{2,1,0:T(8,128)(2,1)S(1)}, bf16[2,32,512]{2,1,0:T(8,128)(2,1)S(1)}, u32[]{:S(2)}, u32[]{:S(2)}) collective-permute-start(bf16[2,32,512]{2,1,0:T(8,128)(2,1)S(1)} %get-tuple-element.34), channel_id=1, source_target_pairs={{0,4},{4,8},{8,12},{1,5},{5,9},{9,13},{2,6},{6,10},{10,14},{3,7},{... | collective-permute-start | bytes 196616 | tf_op jit(solution)/shard_map/ppermute | solution.py:363
  26.7 3.9 %collective-permute-start.5 = (bf16[2,32,512]{2,1,0:T(8,128)(2,1)S(1)}, bf16[2,32,512]{2,1,0:T(8,128)(2,1)S(1)}, u32[]{:S(2)}, u32[]{:S(2)}) collective-permute-start(bf16[2,32,512]{2,1,0:T(8,128)(2,1)S(1)} %get-tuple-element.35), channel_id=1, source_target_pairs={{4,0},{8,4},{12,8},{5,1},{9,5},{13,9},{6,2},{10,6},{14,10},{7,3},{... | collective-permute-start | bytes 196616 | tf_op jit(solution)/shard_map/ppermute | solution.py:364
  30.6 11.6 %shard_map.75 = (f32[16,32,512]{2,1,0:T(8,128)S(1)}, bf16[16,80,512]{2,1,0:T(8,128)(2,1)S(1)}, bf16[4,512,80]{2,1,0:T(8,128)(2,1)S(1)}) custom-call(s32[4]{0:T(128)S(1)} %pad_add_fusion.ids_ref, s32[8,16]{1,0:T(8,128)S(1)} %get-tuple-element.27.cnt_ref, bf16[16,64,512]{2,1,0:T(8,128)(2,1)S(1)} %bitcast.10, bf16[4,32,512]{2,1,0:T(8,128)(2,1)S(1)} %get-tuple-element.28.tw_ref, ...), custom_call_target="tpu_custom_call" | custom-call | flops 14000000000 | bytes 1048576 | tf_op jit(solution)/shard_map/pallas_call | solution.py:22
  42.3 9.0 %shard_map.76 = (f32[16,8192]{1,0:T(8,128)S(1)}, bf16[16,8192]{1,0:T(8,128)(2,1)S(1)}, bf16[16,80,256]{2,1,0:T(8,128)(2,1)S(1)}, s32[1,8192]{1,0:T(1,128)S(1)}) custom-call(s32[8,16]{1,0:T(8,128)S(1)} %get-tuple-element.27.cnt_ref, f32[16,32,512]{2,1,0:T(8,128)S(1)} %get-tuple-element.31.near_ref, bf16[16,80,512]{2,1,0:T(8,128)(2,1)S(1)} %get-tuple-element.32.tgt_ref, ...), custom_call_target="tpu_custom_call" | custom-call | flops 6000000000 | bytes 1048576 | tf_op jit(solution)/shard_map/pallas_call | solution.py:22
  51.4 1.6 %shard_map.78 = (bf16[12,256,80]{2,1,0:T(8,128)(2,1)S(1)}, bf16[12,32,256]{2,1,0:T(8,128)(2,1)S(1)}, s32[144]{0:T(256)S(1)}) custom-call(s32[8,16]{1,0:T(8,128)S(1)} %get-tuple-element.39.far_ref, bf16[4,96,256]{2,1,0:T(8,128)(2,1)S(1)} %collective-permute-done.8.refs_0_, bf16[4,96,256]{2,1,0:T(8,128)(2,1)S(1)} %collective-permute-done.9.refs_1_, ...), custom_call_target="tpu_custom_call" | custom-call | flops 2000000000 | bytes 1048576 | tf_op jit(solution)/shard_map/pallas_call | solution.py:22
  53.1 4.6 %shard_map.79 = (f32[16,4096]{1,0:T(8,128)S(1)}, bf16[16,4096]{1,0:T(8,128)(2,1)S(1)}) custom-call(s32[144]{0:T(256)S(1)} %get-tuple-element.41.names, bf16[12,256,80]{2,1,0:T(8,128)(2,1)S(1)} %get-tuple-element.42.far_src, bf16[12,32,256]{2,1,0:T(8,128)(2,1)S(1)} %get-tuple-element.43.far_w, bf16[16,80,256]{2,1,0:T(8,128)(2,1)S(1)} %get-tuple-element.44.far_tgt, ...), custom_call_target="tpu_custom_call" | custom-call | flops 4000000000 | bytes 1048576 | tf_op jit(solution)/shard_map/pallas_call | solution.py:22
  57.8 1.0 %collective-permute-start.11 = (bf16[16,4096]{1,0:T(8,128)(2,1)S(1)}, bf16[16,4096]{1,0:T(8,128)(2,1)S(1)}, u32[]{:S(2)}, u32[]{:S(2)}) collective-permute-start(bf16[16,4096]{1,0:T(8,128)(2,1)S(1)} %get-tuple-element.46), channel_id=1, source_target_pairs={{0,1},{1,0},{2,3},{3,2},{4,5},{5,4},{6,7},{7,6},{8,9},{9,8},{10,11... | collective-permute-start | bytes 393224 | tf_op jit(solution)/shard_map/ppermute | solution.py:309
  58.7 1.0 %collective-permute-done.11 = bf16[16,4096]{1,0:T(8,128)(2,1)S(1)} collective-permute-done((bf16[16,4096]{1,0:T(8,128)(2,1)S(1)}, bf16[16,4096]{1,0:T(8,128)(2,1)S(1)}, u32[]{:S(2)}, u32[]{:S(2)}) %collective-permute-start.11) | collective-permute-done | bytes 131104 | tf_op jit(solution)/shard_map/ppermute | solution.py:309
  59.8 1.1 %collective-permute-start.12 = (bf16[16,4096]{1,0:T(8,128)(2,1)S(1)}, bf16[16,4096]{1,0:T(8,128)(2,1)S(1)}, u32[]{:S(2)}, u32[]{:S(2)}) collective-permute-start(bf16[16,4096]{1,0:T(8,128)(2,1)S(1)} %add_convert_fusion.1.refs_0_), channel_id=1, source_target_pairs={{0,2},{2,0},{1,3},{3,1},{4,6},{6,4},{5,7},{7,5},{8,10},{10,8},{9,1... | collective-permute-start | bytes 393224 | tf_op jit(solution)/shard_map/ppermute | solution.py:309
  60.9 7.0 %collective-permute-done.7.refs_1_ = bf16[16,8192]{1,0:T(8,128)(2,1)S(1)} collective-permute-done((bf16[16,8192]{1,0:T(8,128)(2,1)S(1)}, bf16[16,8192]{1,0:T(8,128)(2,1)S(1)}, u32[]{:S(2)}, u32[]{:S(2)}) %collective-permute-start.7) | collective-permute-done | bytes 262176 | tf_op jit(solution)/shard_map/ppermute | solution.py:309
  67.9 2.4 %shard_map.77.start_ref = f32[512,256]{1,0:T(8,128)S(1)} custom-call(s32[1,8192]{1,0:T(1,128)S(1)} %copy-done.10, bf16[16,8192]{1,0:T(8,128)(2,1)S(1)} %add_convert_fusion.refs_0_.after_ref, bf16[16,8192]{1,0:T(8,128)(2,1)S(1)} %collective-permute-done.7.refs_1_), custom_call_target="tpu_custom_call" | custom-call | flops 3000000000 | bytes 1048576 | tf_op jit(solution)/shard_map/pallas_call | solution.py:22
  70.3 5.7 %shard_map.80 = f32[16,8192]{1,0:T(8,128)} custom-call(s32[1,8192]{1,0:T(1,128)S(1)} %get-tuple-element.36.comp_ref, bf16[16,256,256]{2,1,0:T(8,128)(2,1)S(1)} %copy-done.5, f32[512,256]{1,0:T(8,128)S(1)} %shard_map.77.start_ref, bf16[16,4096]{1,0:T(8,128)(2,1)S(1)} %add_convert_fusion.1.refs_0_, bf16[16,4096]{1,0:T(8,128)(2,1)S(1)} %collective-permute-done.12.refs_1_), custom_call_target="tpu_custom_call" | custom-call | flops 4000000000 | bytes 1048576 | tf_op jit(solution)/shard_map/pallas_call | solution.py:22
  (35 shorter events, 1.7 us)
Async XLA Ops:
  0.0 11.0 %collective-permute-start = (bf16[16,8192]{1,0:T(8,128)(2,1)}, bf16[16,8192]{1,0:T(8,128)(2,1)S(1)}, u32[]{:S(2)}, u32[]{:S(2)}) collective-permute-start(bf16[16,8192]{1,0:T(8,128)(2,1)} %bitcast.14), channel_id=1, source_target_pairs={{0,1},{1,0},{2,3},{3,2},{4,5},{5,4},{6,7},{7,6},{8,9},{9,8},{10,11... | collective-permute-start | bytes 786440 | tf_op jit(solution)/shard_map/ppermute | solution.py:309
  0.1 1.2 %copy-start = (bf16[16,512,64]{1,2,0:T(8,128)(2,1)S(1)}, bf16[16,512,64]{1,2,0:T(8,128)(2,1)}, u32[]{:S(2)}) copy-start(bf16[16,512,64]{1,2,0:T(8,128)(2,1)} %param.7) | copy-start | bytes 3145732
  1.3 0.7 copy-start.2
  2.0 0.7 copy-start.3
  3.6 7.4 %collective-permute-start.1 = (s32[12,16]{1,0:T(8,128)S(1)}, s32[12,16]{1,0:T(8,128)S(1)}, u32[]{:S(2)}, u32[]{:S(2)}) collective-permute-start(s32[12,16]{1,0:T(8,128)S(1)} %get-tuple-element.26.refs_0_), channel_id=1, source_target_pairs={{0,2},{2,0},{1,3},{3,1},{4,6},{6,4},{5,7},{7,5},{8,10},{10,8},{9,1... | collective-permute-start | bytes 2312 | tf_op jit(solution)/shard_map/ppermute | solution.py:309
  5.2 19.6 %collective-permute-start.2 = (bf16[2,64,512]{2,1,0:T(8,128)(2,1)S(1)}, bf16[2,64,512]{2,1,0:T(8,128)(2,1)S(1)}, u32[]{:S(2)}, u32[]{:S(2)}) collective-permute-start(bf16[2,64,512]{2,1,0:T(8,128)(2,1)S(1)} %get-tuple-element.29), channel_id=1, source_target_pairs={{0,4},{4,8},{8,12},{1,5},{5,9},{9,13},{2,6},{6,10},{10,14},{3,7},{... | collective-permute-start | bytes 393224 | tf_op jit(solution)/shard_map/ppermute | solution.py:346
  8.6 18.0 %collective-permute-start.3 = (bf16[2,64,512]{2,1,0:T(8,128)(2,1)S(1)}, bf16[2,64,512]{2,1,0:T(8,128)(2,1)S(1)}, u32[]{:S(2)}, u32[]{:S(2)}) collective-permute-start(bf16[2,64,512]{2,1,0:T(8,128)(2,1)S(1)} %get-tuple-element.30), channel_id=1, source_target_pairs={{4,0},{8,4},{12,8},{5,1},{9,5},{13,9},{6,2},{10,6},{14,10},{7,3},{... | collective-permute-start | bytes 393224 | tf_op jit(solution)/shard_map/ppermute | solution.py:347
  11.0 1.6 %copy-start.4 = (bf16[16,256,256]{2,1,0:T(8,128)(2,1)S(1)}, bf16[16,256,256]{2,1,0:T(8,128)(2,1)}, u32[]{:S(2)}) copy-start(bf16[16,256,256]{2,1,0:T(8,128)(2,1)} %interp_ref.3) | copy-start | bytes 6291460
  12.6 0.9 %copy-start.6 = (bf16[8192,16]{0,1:T(8,128)(2,1)S(1)}, bf16[8192,16]{0,1:T(8,128)(2,1)}, u32[]{:S(2)}) copy-start(bf16[8192,16]{0,1:T(8,128)(2,1)} %param.8) | copy-start | bytes 786436
  13.6 0.8 copy-start.7
  14.3 0.8 copy-start.9
  18.3 33.1 %collective-permute-start.10 = (bf16[4,96,256]{2,1,0:T(8,128)(2,1)S(1)}, bf16[4,96,256]{2,1,0:T(8,128)(2,1)S(1)}, u32[]{:S(2)}, u32[]{:S(2)}) collective-permute-start(bf16[4,96,256]{2,1,0:T(8,128)(2,1)S(1)} %get-tuple-element.40), channel_id=1, source_target_pairs={{0,12},{4,0},{8,4},{12,8},{1,13},{5,1},{9,5},{13,9},{2,14},{6,2},{... | collective-permute-start | bytes 589832 | tf_op jit(solution)/shard_map/ppermute | solution.py:309
  18.3 33.1 %collective-permute-start.8 = (bf16[4,96,256]{2,1,0:T(8,128)(2,1)S(1)}, bf16[4,96,256]{2,1,0:T(8,128)(2,1)S(1)}, u32[]{:S(2)}, u32[]{:S(2)}) collective-permute-start(bf16[4,96,256]{2,1,0:T(8,128)(2,1)S(1)} %get-tuple-element.40), channel_id=1, source_target_pairs={{0,4},{4,8},{8,12},{12,0},{1,5},{5,9},{9,13},{13,1},{2,6},{6,10},{... | collective-permute-start | bytes 589832 | tf_op jit(solution)/shard_map/ppermute | solution.py:309
  20.3 31.1 %collective-permute-start.9 = (bf16[4,96,256]{2,1,0:T(8,128)(2,1)S(1)}, bf16[4,96,256]{2,1,0:T(8,128)(2,1)S(1)}, u32[]{:S(2)}, u32[]{:S(2)}) collective-permute-start(bf16[4,96,256]{2,1,0:T(8,128)(2,1)S(1)} %get-tuple-element.40), channel_id=1, source_target_pairs={{0,8},{4,12},{8,0},{12,4},{1,9},{5,13},{9,1},{13,5},{2,10},{6,14},... | collective-permute-start | bytes 589832 | tf_op jit(solution)/shard_map/ppermute | solution.py:309
  24.7 17.5 %collective-permute-start.4 = (bf16[2,32,512]{2,1,0:T(8,128)(2,1)S(1)}, bf16[2,32,512]{2,1,0:T(8,128)(2,1)S(1)}, u32[]{:S(2)}, u32[]{:S(2)}) collective-permute-start(bf16[2,32,512]{2,1,0:T(8,128)(2,1)S(1)} %get-tuple-element.34), channel_id=1, source_target_pairs={{0,4},{4,8},{8,12},{1,5},{5,9},{9,13},{2,6},{6,10},{10,14},{3,7},{... | collective-permute-start | bytes 196616 | tf_op jit(solution)/shard_map/ppermute | solution.py:363
  26.7 15.6 %collective-permute-start.5 = (bf16[2,32,512]{2,1,0:T(8,128)(2,1)S(1)}, bf16[2,32,512]{2,1,0:T(8,128)(2,1)S(1)}, u32[]{:S(2)}, u32[]{:S(2)}) collective-permute-start(bf16[2,32,512]{2,1,0:T(8,128)(2,1)S(1)} %get-tuple-element.35), channel_id=1, source_target_pairs={{4,0},{8,4},{12,8},{5,1},{9,5},{13,9},{6,2},{10,6},{14,10},{7,3},{... | collective-permute-start | bytes 196616 | tf_op jit(solution)/shard_map/ppermute | solution.py:364
  30.6 11.7 %copy-start.1 = (bf16[16,512,64]{1,2,0:T(8,128)(2,1)S(1)}, bf16[16,512,64]{1,2,0:T(8,128)(2,1)}, u32[]{:S(2)}) copy-start(bf16[16,512,64]{1,2,0:T(8,128)(2,1)} %param.7) | copy-start | bytes 3145732
  30.6 11.7 %copy-start.8 = (s32[16,512]{1,0:T(8,128)S(1)}, s32[16,512]{1,0:T(8,128)}, u32[]{:S(2)}) copy-start(s32[16,512]{1,0:T(8,128)} %skel_ref.3) | copy-start | bytes 98308
  30.6 11.7 %copy-start.10 = (s32[1,8192]{1,0:T(1,128)S(1)}, s32[1,8192]{1,0:T(1,128)}, u32[]{:S(2)}) copy-start(s32[1,8192]{1,0:T(1,128)} %order_ref.5) | copy-start | bytes 98308
  51.3 1.7 %collective-permute-start.6 = (bf16[16,8192]{1,0:T(8,128)(2,1)S(1)}, bf16[16,8192]{1,0:T(8,128)(2,1)S(1)}, u32[]{:S(2)}, u32[]{:S(2)}) collective-permute-start(bf16[16,8192]{1,0:T(8,128)(2,1)S(1)} %get-tuple-element.38), channel_id=1, source_target_pairs={{0,1},{1,0},{2,3},{3,2},{4,5},{5,4},{6,7},{7,6},{8,9},{9,8},{10,11... | collective-permute-start | bytes 786440 | tf_op jit(solution)/shard_map/ppermute | solution.py:309
  57.8 2.0 %collective-permute-start.11 = (bf16[16,4096]{1,0:T(8,128)(2,1)S(1)}, bf16[16,4096]{1,0:T(8,128)(2,1)S(1)}, u32[]{:S(2)}, u32[]{:S(2)}) collective-permute-start(bf16[16,4096]{1,0:T(8,128)(2,1)S(1)} %get-tuple-element.46), channel_id=1, source_target_pairs={{0,1},{1,0},{2,3},{3,2},{4,5},{5,4},{6,7},{7,6},{8,9},{9,8},{10,11... | collective-permute-start | bytes 393224 | tf_op jit(solution)/shard_map/ppermute | solution.py:309
  58.7 9.2 %collective-permute-start.7 = (bf16[16,8192]{1,0:T(8,128)(2,1)S(1)}, bf16[16,8192]{1,0:T(8,128)(2,1)S(1)}, u32[]{:S(2)}, u32[]{:S(2)}) collective-permute-start(bf16[16,8192]{1,0:T(8,128)(2,1)S(1)} %add_convert_fusion.refs_0_.after_ref), channel_id=1, source_target_pairs={{0,2},{2,0},{1,3},{3,1},{4,6},{6,4},{5,7},{7,5},{8,10},{10,8},{9,1... | collective-permute-start | bytes 786440 | tf_op jit(solution)/shard_map/ppermute | solution.py:309
  59.7 10.5 %copy-start.5 = (bf16[16,256,256]{2,1,0:T(8,128)(2,1)S(1)}, bf16[16,256,256]{2,1,0:T(8,128)(2,1)}, u32[]{:S(2)}) copy-start(bf16[16,256,256]{2,1,0:T(8,128)(2,1)} %interp_ref.3) | copy-start | bytes 6291460
  59.8 10.5 %collective-permute-start.12 = (bf16[16,4096]{1,0:T(8,128)(2,1)S(1)}, bf16[16,4096]{1,0:T(8,128)(2,1)S(1)}, u32[]{:S(2)}, u32[]{:S(2)}) collective-permute-start(bf16[16,4096]{1,0:T(8,128)(2,1)S(1)} %add_convert_fusion.1.refs_0_), channel_id=1, source_target_pairs={{0,2},{2,0},{1,3},{3,1},{4,6},{6,4},{5,7},{7,5},{8,10},{10,8},{9,1... | collective-permute-start | bytes 393224 | tf_op jit(solution)/shard_map/ppermute | solution.py:309

commit v3 on v2

--- a/solution.py
+++ b/solution.py
@@ -11,13 +11,12 @@
 F32 = jnp.float32
 LOG2E = 1.4426950408889634
 EXTRA = 16
-GROUP = 4
+GROUP = 8
 VMEM = pl.BlockSpec(memory_space=pltpu.VMEM)
 SMEM = pl.BlockSpec(memory_space=pltpu.SMEM)
-PARAMS = pltpu.CompilerParams(vmem_limit_bytes=48 << 20)
-
-
-def call(body, shapes, specs, args, scratch=(), flops=0, out_specs=None):
+
+
+def call(body, shapes, specs, args, scratch=(), flops=0, out_specs=None, grant=48):
     outs = [jax.ShapeDtypeStruct(s, d) for s, d in shapes]
     return pl.pallas_call(
         body,
@@ -25,7 +24,7 @@
         in_specs=specs,
         out_specs=out_specs or [VMEM] * len(outs),
         scratch_shapes=list(scratch),
-        compiler_params=PARAMS,
+        compiler_params=pltpu.CompilerParams(vmem_limit_bytes=grant << 20),
         cost_estimate=pl.CostEstimate(flops=flops, bytes_accessed=1 << 20, transcendentals=0),
     )(*args)
 
@@ -68,45 +67,57 @@
     return jnp.exp2(dot(sources, targets) * scale).astype(BF)
 
 
-def halo_body(ids_ref, pts_ref, near_ref, far_ref, up_ref, down_ref, pairs_ref, sems):
-    halo = up_ref.shape[0]
-    mine = ids_ref[2]
-    classes = ids_ref[3]
-    copies = []
+def halo_body(ids_ref, pts_ref, near_ref, far_ref, first_ref, second_ref, pairs_ref, near_buf, far_buf, sems):
+    halo = first_ref.shape[0]
+    even = 1 - lax.rem(ids_ref[0], 2)
+    mine, classes = ids_ref[2], ids_ref[3]
+    half = pts_ref.shape[0] // 2
+    copies = [
+        pltpu.make_async_copy(near_ref, near_buf, sems.at[2 * halo]),
+        pltpu.make_async_copy(far_ref, far_buf, sems.at[2 * halo + 1]),
+    ]
     for j in range(halo):
-        first = mine + j * classes
-        last = mine + (pts_ref.shape[0] // 2) + j * classes
-        copies.append(pltpu.make_async_copy(pts_ref.at[last], up_ref.at[j], sems.at[j]))
-        copies.append(pltpu.make_async_copy(pts_ref.at[first], down_ref.at[j], sems.at[halo + j]))
+        leaf = mine + j * classes
+        copies.append(pltpu.make_async_copy(pts_ref.at[leaf + even * half], first_ref.at[j], sems.at[j]))
+        copies.append(pltpu.make_async_copy(pts_ref.at[leaf + (1 - even) * half], second_ref.at[j], sems.at[halo + j]))
     for copy in copies:
         copy.start()
-    near_n = near_ref.shape[0]
-    pairs_ref[:near_n] = near_ref[...]
-    pairs_ref[near_n:] = far_ref[...]
     for copy in copies:
         copy.wait()
+    near_n = near_ref.shape[0]
+    pairs_ref[:near_n] = near_buf[...]
+    pairs_ref[near_n:] = far_buf[...]
 
 
 def weights_body(
     blocks, classes, near_n, ids_ref, own_ref, other_ref, order_ref, skel_ref, interp_ref, pts_ref, *refs
 ):
-    pair_refs = refs[:-7]
-    tw_ref, up_ref, down_ref, message_ref, cnt_ref, far_ref, stack = refs[-7:]
+    pair_refs = refs[:-13]
+    tw_ref, up_ref, mid_ref, down_ref, cnt_ref, far_ref = refs[-13:-7]
+    stack, own_buf, order_buf, skel_buf, interp_buf, pts_buf, sems = refs[-7:]
     cols = own_ref.shape[0]
     step = 2 * cols
     width = stack.shape[1]
     turns = own_ref.shape[1] // width
     mine, _, size = tw_ref.shape
-    halo = up_ref.shape[0]
-    rank = message_ref.shape[2]
+    rank = mid_ref.shape[1]
     dim = pts_ref.shape[1]
+    tall = dim + step
+    cuts = size // rank
+    halo = (up_ref.shape[0] - mid_ref.shape[0]) // (cuts * step)
     leaves = pts_ref.shape[0]
     block, base, me = ids_ref[0], ids_ref[1], ids_ref[2]
-    for hi in range(turns):
-        span = slice(hi * width, (hi + 1) * width)
-        stack[hi * step : hi * step + cols] = own_ref[:, span]
-        stack[hi * step + cols : (hi + 1) * step] = other_ref[:, span]
-
+    copies = [
+        pltpu.make_async_copy(own_ref, own_buf, sems.at[0]),
+        pltpu.make_async_copy(order_ref, order_buf, sems.at[1]),
+        pltpu.make_async_copy(skel_ref, skel_buf, sems.at[2]),
+    ]
+    for j in range(mine):
+        leaf = j * classes + me
+        copies.append(pltpu.make_async_copy(interp_ref.at[leaf], interp_buf.at[j], sems.at[3 + 2 * j]))
+        copies.append(pltpu.make_async_copy(pts_ref.at[leaf], pts_buf.at[j], sems.at[4 + 2 * j]))
+    for copy in copies:
+        copy.start()
     for e in range(cnt_ref.shape[0]):
         wanted = base + e * classes + me
         total = None
@@ -124,9 +135,15 @@
         code = target * 256 + piece * mine + lax.div(within, classes)
         far_ref[k * far_n : (k + 1) * far_n] = jnp.where(lax.rem(within, classes) == me, code, -1)
 
+    for copy in copies:
+        copy.wait()
+    for hi in range(turns):
+        span = slice(hi * width, (hi + 1) * width)
+        stack[hi * step : hi * step + cols] = own_buf[:, span]
+        stack[hi * step + cols : (hi + 1) * step] = other_ref[:, span]
     for j in range(mine):
         leaf = j * classes + me
-        ids = order_ref[:, pl.ds(pl.multiple_of(leaf * size, size), size)]
+        ids = order_buf[:, pl.ds(pl.multiple_of(leaf * size, size), size)]
         hi_ids = lax.shift_right_logical(ids, width.bit_length() - 1)
         picked = dot(stack[...], one_hot(ids & (width - 1), width))
         total = jnp.zeros((step, size), F32)
@@ -134,15 +151,19 @@
             total = total + jnp.where(hi_ids == hi, picked[hi * step : (hi + 1) * step], 0.0)
         tree = total.astype(BF)
         tw_ref[j] = tree
-        if j < halo:
-            down_ref[j] = tree
-        if j >= mine - halo:
-            up_ref[j - (mine - halo)] = tree
-        hot = one_hot(skel_ref[pl.ds(leaf, 1), :], size)
+        for ref, place in ((down_ref, j), (up_ref, j - (mine - halo))):
+            if 0 <= place < halo:
+                for cut in range(cuts):
+                    at = mine * tall + (place * cuts + cut) * step
+                    ref[at : at + step] = tree[:, cut * rank : (cut + 1) * rank]
+        hot = one_hot(skel_buf[pl.ds(leaf, 1), :], size)
         ordered = dot(tree, hot)
-        combined = dot_last(ordered[:, rank:].astype(BF), interp_ref[leaf])
-        message_ref[j, :dim] = dot(pts_ref[leaf], hot[:, :rank]).astype(BF)
-        message_ref[j, dim:] = (ordered[:, :rank] + combined).astype(BF)
+        combined = dot_last(ordered[:, rank:].astype(BF), interp_buf[j])
+        skel_p = dot(pts_buf[j], hot[:, :rank]).astype(BF)
+        skel_w = (ordered[:, :rank] + combined).astype(BF)
+        for ref in (up_ref, mid_ref, down_ref):
+            ref[j * tall : j * tall + dim] = skel_p
+            ref[j * tall + dim : (j + 1) * tall] = skel_w
 
 
 def near_sum(t, first, count, most, scale, cnt_ref, slots, tgt, src, weights, write, shift=0):
@@ -169,7 +190,7 @@
 
 
 def near_body(
-    halo, scale, ids_ref, cnt_ref, pts_ref, tw_ref, left_p, right_p, near_ref, tgt_ref, edge_src, src, slots
+    halo, scale, ids_ref, cnt_ref, pts_ref, tw_ref, first_p, second_p, near_ref, tgt_ref, edge_src, src, slots
 ):
     leaves = pts_ref.shape[0]
     mine = tw_ref.shape[0]
@@ -180,9 +201,10 @@
         return 0
 
     lax.fori_loop(0, mine, sources, 0)
+    odd = lax.rem(ids_ref[0], 2)
     for j in range(halo):
-        edge_src[j] = as_sources(left_p[j])
-        edge_src[halo + j] = as_sources(right_p[j])
+        edge_src[(1 - odd) * halo + j] = as_sources(first_p[j])
+        edge_src[odd * halo + j] = as_sources(second_p[j])
 
     def write(t, value):
         near_ref[t] = value
@@ -196,15 +218,17 @@
 
 
 def edge_body(
-    halo, mine, scale, cnt_ref, near_ref, tgt_ref, src, left_w, right_w, pts_ref, skel_ref, order_ref,
-    own_ref, other_ref, far_tgt_ref, comp_ref, wts, slots,
+    halo, mine, scale, cnt_ref, near_ref, tgt_ref, src, left_m, right_m, pts_ref, skel_ref,
+    own_ref, other_ref, far_tgt_ref, wts, slots,
 ):
     leaves, cols2, size = near_ref.shape
     cols = cols2 // 2
     rank = far_tgt_ref.shape[2]
     for j in range(halo):
-        wts[j] = left_w[j]
-        wts[halo + j] = right_w[j]
+        for side, ref in enumerate((left_m, right_m)):
+            for cut in range(size // rank):
+                at = ref.shape[0] - (halo * (size // rank) - j * (size // rank) - cut) * cols2
+                wts[side * halo + j, :, cut * rank : (cut + 1) * rank] = ref[at : at + cols2]
 
     def write(t, value):
         total = near_ref[t] + value
@@ -214,14 +238,8 @@
     def target(t, _):
         right = jnp.where(t < leaves // 2, 0, 1)
         near_sum(t, right * (halo + mine), halo, halo, scale, cnt_ref, slots, tgt_ref, src, wts, write, right * halo)
-        span = pl.ds(pl.multiple_of(t * size, size), size)
-        hot = one_hot(skel_ref[pl.ds(t, 1), :], size)
-        far_tgt_ref[t] = as_targets(dot(pts_ref[t], hot[:, :rank]).astype(BF))
-        ids = order_ref[:, span]
-        row = lax.broadcasted_iota(jnp.int32, (16, size), 0)
-        halves = jnp.where(row == 0, lax.shift_right_logical(ids, 8), jnp.where(row == 1, ids & 255, 0))
-        moved = dot(halves.astype(F32).astype(BF), hot)
-        comp_ref[:, span] = (moved[:1] * 256.0 + moved[1:2]).astype(jnp.int32)
+        hot = one_hot(skel_ref[pl.ds(t, 1), :rank], size)
+        far_tgt_ref[t] = as_targets(dot(pts_ref[t], hot).astype(BF))
         return 0
 
     lax.fori_loop(0, leaves, target, 0)
@@ -230,11 +248,13 @@
 def sources_body(mine, far_ref, *refs):
     pieces = refs[:-3]
     far_src, far_w, names = refs[-3:]
-    dim = pieces[0].shape[1] - far_w.shape[1]
+    cols2 = far_w.shape[1]
+    dim = far_src.shape[2] - EXTRA
+    tall = dim + cols2
     for k, piece in enumerate(pieces):
         for j in range(mine):
-            far_src[k * mine + j] = as_sources(piece[j, :dim])
-            far_w[k * mine + j] = piece[j, dim:]
+            far_src[k * mine + j] = as_sources(piece[j * tall : j * tall + dim])
+            far_w[k * mine + j] = piece[j * tall + dim : (j + 1) * tall]
     found = jnp.int32(0)
     for t in range(far_ref.shape[1]):
         for i in range(far_ref.shape[0]):
@@ -246,6 +266,10 @@
         names[1 + found + j] = jnp.int32(far_ref.shape[1] * 256)
 
 
+def sum_body(own_ref, back_ref, *refs):
+    refs[-1][...] = (own_ref[...] + back_ref[...].astype(F32)).astype(BF)
+
+
 def far_body(scale, names, far_src, far_w, far_tgt, after_ref, own_ref, other_ref, field):
     leaves, _, rank = far_tgt.shape
     cols = own_ref.shape[0]
@@ -272,8 +296,8 @@
     return dot_last(jnp.concatenate(masked, axis=0), one_hot(ids & (width - 1), width))
 
 
-def place_near_body(order_ref, *refs):
-    near, acc = refs[:-1], refs[-1]
+def place_near_body(order_ref, skel_ref, *refs):
+    near, acc, comp_ref = refs[:-2], refs[-2], refs[-1]
     total = order_ref.shape[1]
     width = acc.shape[1]
     chunk = 1024
@@ -282,10 +306,18 @@
         value = sum(ref[:, span].astype(F32) for ref in near)
         part = scatter(order_ref[:, span], value, width, total // width)
         acc[...] = part if at == 0 else acc[...] + part
+    leaves, size = skel_ref.shape
+    for t in range(leaves):
+        span = slice(t * size, (t + 1) * size)
+        ids = order_ref[:, span]
+        row = lax.broadcasted_iota(jnp.int32, (16, size), 0)
+        halves = jnp.where(row == 0, lax.shift_right_logical(ids, 8), jnp.where(row == 1, ids & 255, 0))
+        moved = dot(halves.astype(F32).astype(BF), one_hot(skel_ref[t : t + 1], size))
+        comp_ref[:, span] = (moved[:1] * 256.0 + moved[1:2]).astype(jnp.int32)
 
 
 def place_far_body(comp_ref, interp_ref, start_ref, *refs):
-    far, out_ref, acc = refs[:-2], refs[-2], refs[-1]
+    far, out_ref, acc, buf = refs[:-3], refs[-3], refs[-2], refs[-1]
     cols, total = out_ref.shape
     width = acc.shape[1]
     turns = total // width
@@ -293,9 +325,13 @@
     size = total // leaves
     for t in range(leaves):
         skel = sum(ref[:, t * rank : (t + 1) * rank].astype(F32) for ref in far).astype(BF)
-        value = jnp.concatenate([skel.astype(F32), dot(skel, interp_ref[t])], axis=1)
-        part = scatter(comp_ref[:, t * size : (t + 1) * size], value, width, turns)
-        acc[...] = (start_ref if t == 0 else acc)[...] + part
+        buf[:, t * size : t * size + rank] = skel.astype(F32)
+        buf[:, t * size + rank : (t + 1) * size] = dot(skel, interp_ref[t])
+    chunk = 1024
+    for at in range(0, total, chunk):
+        span = slice(at, at + chunk)
+        part = scatter(comp_ref[:, span], buf[:, span], width, turns)
+        acc[...] = (start_ref if at == 0 else acc)[...] + part
     for hi in range(turns):
         out_ref[:, hi * width : (hi + 1) * width] = acc[hi * cols : (hi + 1) * cols]
 
@@ -333,49 +369,70 @@
     ids = jnp.stack([block, block * leaves - span, mine_id, jnp.int32(classes)]).astype(jnp.int32)
     pts = points.transpose(0, 2, 1)
     wts = weights.T
-    up, down = [(i, i + 1) for i in range(blocks - 1)], [(i + 1, i) for i in range(blocks - 1)]
     (other_wts,) = from_others(wts, "rhs")
-    up_p, down_p, pairs = call(
+    swaps = []
+    for start in (0, 1):
+        swap = {i: i for i in range(blocks)}
+        for i in range(start, blocks - 1, 2):
+            swap[i], swap[i + 1] = i + 1, i
+        swaps.append(list(swap.items()))
+    hbm = pl.BlockSpec(memory_space=pltpu.HBM)
+    first_p, second_p, pairs = call(
         halo_body,
         [((halo, dim, size), BF), ((halo, dim, size), BF), ((near_n + far_n, leaves), jnp.int32)],
-        [SMEM, pl.BlockSpec(memory_space=pl.ANY), VMEM, VMEM],
+        [SMEM, hbm, hbm, hbm],
         (ids, pts, near_pairs.T, far_pairs.T),
-        [pltpu.SemaphoreType.DMA((2 * halo,))],
+        [
+            pltpu.VMEM((near_n, leaves), jnp.int32),
+            pltpu.VMEM((far_n, leaves), jnp.int32),
+            pltpu.SemaphoreType.DMA((2 * halo + 2,)),
+        ],
+        grant=60,
     )
     every = [pairs] + from_others(pairs, "pair")
-    left_p = lax.ppermute(up_p, "leaf", up)
-    right_p = lax.ppermute(down_p, "leaf", down)
-    tree_w, up_w, down_w, message, cnt, far_ids = call(
+    first_p = lax.ppermute(first_p, "leaf", swaps[0])
+    second_p = lax.ppermute(second_p, "leaf", swaps[1])
+    tall = mine * (dim + 2 * cols)
+    extra = halo * (size // rank) * 2 * cols
+    tree_w, up_m, mid_m, down_m, cnt, far_ids = call(
         functools.partial(weights_body, blocks, classes, near_n),
         [
             ((mine, 2 * cols, size), BF),
-            ((halo, 2 * cols, size), BF),
-            ((halo, 2 * cols, size), BF),
-            ((mine, dim + 2 * cols, rank), BF),
+            ((tall + extra, rank), BF),
+            ((tall, rank), BF),
+            ((tall + extra, rank), BF),
             ((2 * halo + mine, leaves), jnp.int32),
             ((pair_n * far_n, leaves), jnp.int32),
         ],
-        [SMEM] + [VMEM] * (6 + pair_n),
+        [SMEM, hbm, VMEM] + [hbm] * 4 + [VMEM] * pair_n,
         (ids, wts, other_wts, tree_order, skel_order, interp, pts, *every),
-        [pltpu.VMEM((2 * cols * (leaves * size // 256), 256), BF)],
+        [
+            pltpu.VMEM((2 * cols * (leaves * size // 256), 256), BF),
+            pltpu.VMEM((cols, leaves * size), BF),
+            pltpu.VMEM((1, leaves * size), jnp.int32),
+            pltpu.VMEM((leaves, size), jnp.int32),
+            pltpu.VMEM((mine, rank, size - rank), BF),
+            pltpu.VMEM((mine, dim, size), BF),
+            pltpu.SemaphoreType.DMA((3 + 2 * mine,)),
+        ],
         flops=3 * mega,
-    )
-    left_w = lax.ppermute(up_w, "leaf", up)
-    right_w = lax.ppermute(down_w, "leaf", down)
-    pieces = from_others(message, "leaf")
+        grant=60,
+    )
+    outgoing = {by: mid_m for by in range(1, blocks)} | {1: up_m, blocks - 1: down_m}
+    pieces = [lax.ppermute(outgoing[by], "leaf", ring(blocks, by)) for by in range(1, blocks)]
     near, tgt, edge_src = call(
         functools.partial(near_body, halo, scale),
         [((leaves, 2 * cols, size), F32), ((leaves, wide, size), BF), ((2 * halo, size, wide), BF)],
         [SMEM, SMEM, VMEM, VMEM, VMEM, VMEM],
-        (ids, cnt, pts, tree_w, left_p, right_p),
+        (ids, cnt, pts, tree_w, first_p, second_p),
         [pltpu.VMEM((mine, size, wide), BF), pltpu.SMEM((mine + 1,), jnp.int32)],
         flops=14 * mega,
     )
-    near_own, near_other, far_tgt, comp = call(
+    near_own, near_other, far_tgt = call(
         functools.partial(edge_body, halo, mine, scale),
-        [((cols, leaves * size), F32), ((cols, leaves * size), BF), ((leaves, wide, rank), BF), ((1, leaves * size), jnp.int32)],
-        [SMEM] + [VMEM] * 8,
-        (cnt, near, tgt, edge_src, left_w, right_w, pts, skel_order, tree_order),
+        [((cols, leaves * size), F32), ((cols, leaves * size), BF), ((leaves, wide, rank), BF)],
+        [SMEM] + [VMEM] * 7,
+        (cnt, near, tgt, edge_src, pieces[0], pieces[-1], pts, skel_order),
         [
             pltpu.VMEM((2 * halo, 2 * cols, size), BF),
             pltpu.SMEM((halo + 1,), jnp.int32),
@@ -403,21 +460,27 @@
         flops=4 * mega,
     )
     (far_back,) = from_others(far_other, "rhs")
-    far_parts = over_pair((far_own + far_back.astype(F32)).astype(BF), pair_n)
+    (far_sum_own,) = call(
+        sum_body,
+        [((cols, leaves * rank), BF)],
+        [VMEM, VMEM] + [pl.BlockSpec(memory_space=pl.ANY)] * (pair_n - 1),
+        (far_own, far_back, *near_parts[1:]),
+    )
+    far_parts = over_pair(far_sum_own, pair_n)
     acc_shape = (leaves * size // 256 * cols, 256)
-    (acc,) = call(
+    acc, comp = call(
         place_near_body,
-        [(acc_shape, F32)],
-        [VMEM] * (1 + pair_n),
-        (tree_order, *near_parts),
-        flops=3 * mega,
+        [(acc_shape, F32), ((1, leaves * size), jnp.int32)],
+        [VMEM] * (2 + pair_n),
+        (tree_order, skel_order, *near_parts),
+        flops=5 * mega,
     )
     (out,) = call(
         place_far_body,
         [((cols, leaves * size), F32)],
         [VMEM] * (3 + pair_n),
         (comp, interp, acc, *far_parts),
-        [pltpu.VMEM(acc_shape, F32)],
+        [pltpu.VMEM(acc_shape, F32), pltpu.VMEM((cols, leaves * size), F32)],
         flops=4 * mega,
     )
     return out.T

time: 76.9 us -> 61.3 us (0.80)
  the two profiles are of different devices: /device:TPU:8 before, /device:TPU:0 now
where the time goes in v3:
time: 61.3 us; the launch traced here: 61.5 us
  Pallas kernels  39 us (64%)
  starting transfers between devices  13 us (21%)
  waiting for transfers between devices  5.76 us (9%)
  local copies, waits for them, and re-layouts  2.9 us (5%)
  other arithmetic  0.72 us (1%)
    pallas_call x9, Pallas kernels, call(): pl.pallas_call(body, out_shape=outs, in_specs=specs, out_specs=out_specs...  39 us
    ppermute x6, waiting for transfers between devices, from_others(): lax.ppermute(value, axis, ring(count, by))  5.75 us
    ppermute x3, starting transfers between devices, on_device(): lax.ppermute(outgoing[by], 'leaf', ring(blocks, by))  5.09 us
    ppermute x6, starting transfers between devices, from_others(): lax.ppermute(value, axis, ring(count, by))  4.63 us
    unnamed x22, local copies, waits for them, and re-layouts  2.9 us
    ppermute x1, starting transfers between devices, on_device(): second_p = lax.ppermute(second_p, 'leaf', swaps[1])  1.68 us
    ppermute x1, starting transfers between devices, on_device(): first_p = lax.ppermute(first_p, 'leaf', swaps[0])  1.58 us
  transfers between devices with their start and end apart: 11, of which 3 were waited for; matrix products, arithmetic and copies ran while one was open for 1% of the time, Pallas kernels for 58%

profile of v3, /device:TPU:0, one launch (start us, length us, event | category | flops | bytes accessed | tf_op | source)
XLA Modules:
  0.0 61.5 jit_solution(2332013511907228135)
XLA Ops:
  0.0 0.5 collective-permute-start
  0.5 0.7 %pad_add_fusion.ids_ref = s32[4]{0:T(128)} fusion(s32[1]{0:T(128)} %constant.19.clone.1, s32[1]{0:T(128)} %bitcast.2, s32[1]{0:T(128)} %bitcast.1, s32[1]{0:T(128)} %bitcast), kind=kLoop, calls=%fused_computation.1 | loop fusion | flops 12 | bytes 32 | tf_op jit(solution)/shard_map/stack | solution.py:369
  1.1 2.4 %shard_map.73 = (bf16[2,64,512]{2,1,0:T(8,128)(2,1)}, bf16[2,64,512]{2,1,0:T(8,128)(2,1)}, s32[12,16]{1,0:T(8,128)}) custom-call(s32[4]{0:T(128)} %pad_add_fusion.ids_ref, bf16[16,64,512]{2,1,0:T(8,128)(2,1)} %bitcast.8, s32[8,16]{1,0:T(8,128)} %bitcast.12, s32[4,16]{1,0:T(4,128)} %bitcast.13), custom_call_target="tpu_custom_call" | custom-call | bytes 1048576 | tf_op jit(solution)/shard_map/pallas_call | solution.py:21
  3.5 2.6 %collective-permute-start.1 = (s32[12,16]{1,0:T(8,128)}, s32[12,16]{1,0:T(8,128)S(1)}, u32[]{:S(2)}, u32[]{:S(2)}) collective-permute-start(s32[12,16]{1,0:T(8,128)} %get-tuple-element.27.refs_0_), channel_id=1, source_target_pairs={{0,2},{2,0},{1,3},{3,1},{4,6},{6,4},{5,7},{7,5},{8,10},{10,8},{9,1... | collective-permute-start | bytes 2312 | tf_op jit(solution)/shard_map/ppermute | solution.py:345
  6.1 1.6 %collective-permute-start.2 = (bf16[2,64,512]{2,1,0:T(8,128)(2,1)}, bf16[2,64,512]{2,1,0:T(8,128)(2,1)S(1)}, u32[]{:S(2)}, u32[]{:S(2)}) collective-permute-start(bf16[2,64,512]{2,1,0:T(8,128)(2,1)} %get-tuple-element.30), channel_id=1, source_target_pairs={{0,4},{4,0},{8,12},{12,8},{1,5},{5,1},{9,13},{13,9},{2,6},{6,2},{1... | collective-permute-start | bytes 393224 | tf_op jit(solution)/shard_map/ppermute | solution.py:393
  7.7 1.7 %collective-permute-start.3 = (bf16[2,64,512]{2,1,0:T(8,128)(2,1)}, bf16[2,64,512]{2,1,0:T(8,128)(2,1)S(1)}, u32[]{:S(2)}, u32[]{:S(2)}) collective-permute-start(bf16[2,64,512]{2,1,0:T(8,128)(2,1)} %get-tuple-element.31), channel_id=1, source_target_pairs={{0,0},{4,8},{8,4},{12,12},{1,1},{5,9},{9,5},{13,13},{2,2},{6,10},{... | collective-permute-start | bytes 393224 | tf_op jit(solution)/shard_map/ppermute | solution.py:394
  9.4 0.6 copy-done.10
  9.9 0.7 %copy-done.9 = bf16[16,8192]{1,0:T(8,128)(2,1)} copy-done((bf16[16,8192]{1,0:T(8,128)(2,1)}, bf16[16,8192]{1,0:T(8,128)(2,1)S(1)}, u32[]{:S(2)}) %copy-start.9) | copy-done | bytes 262168
  10.6 5.8 %shard_map.74 = (bf16[4,32,512]{2,1,0:T(8,128)(2,1)}, bf16[512,256]{1,0:T(8,128)(2,1)}, bf16[384,256]{1,0:T(8,128)(2,1)}, bf16[512,256]{1,0:T(8,128)(2,1)}, s32[8,16]{1,0:T(8,128)}, /*index=5*/s32[8,16]{1,0:T(8,128)}) custom-call(s32[4]{0:T(128)} %pad_add_fusion.ids_ref, bf16[16,8192]{1,0:T(8,128)(2,1)} %bitcast.15, bf16[16,8192]{1,0:T(8,128)(2,1)} %copy-done.9, ...), custom_call_target="tpu_custom_call" | custom-call | flops 3000000000 | bytes 1048576 | tf_op jit(solution)/shard_map/pallas_call | solution.py:21
  16.4 3.6 %collective-permute-start.4 = (bf16[512,256]{1,0:T(8,128)(2,1)}, bf16[512,256]{1,0:T(8,128)(2,1)S(1)}, u32[]{:S(2)}, u32[]{:S(2)}) collective-permute-start(bf16[512,256]{1,0:T(8,128)(2,1)} %get-tuple-element.35), channel_id=1, source_target_pairs={{0,4},{4,8},{8,12},{12,0},{1,5},{5,9},{9,13},{13,1},{2,6},{6,10},{... | collective-permute-start | bytes 786440 | tf_op jit(solution)/shard_map/ppermute | solution.py:422
  20.3 1.2 %collective-permute-start.8 = (bf16[384,256]{1,0:T(8,128)(2,1)}, bf16[384,256]{1,0:T(8,128)(2,1)S(1)}, u32[]{:S(2)}, u32[]{:S(2)}) collective-permute-start(bf16[384,256]{1,0:T(8,128)(2,1)} %get-tuple-element.42), channel_id=1, source_target_pairs={{0,8},{4,12},{8,0},{12,4},{1,9},{5,13},{9,1},{13,5},{2,10},{6,14},... | collective-permute-start | bytes 589832 | tf_op jit(solution)/shard_map/ppermute | solution.py:422
  21.6 0.9 %copy-done.5 = bf16[4,32,512]{2,1,0:T(8,128)(2,1)S(1)} copy-done((bf16[4,32,512]{2,1,0:T(8,128)(2,1)S(1)}, bf16[4,32,512]{2,1,0:T(8,128)(2,1)}, u32[]{:S(2)}) %copy-start.5) | copy-done | bytes 131096
  22.5 0.7 %copy-done.7 = s32[8,16]{1,0:T(8,128)S(1)} copy-done((s32[8,16]{1,0:T(8,128)S(1)}, s32[8,16]{1,0:T(8,128)}, u32[]{:S(2)}) %copy-start.7) | copy-done | bytes 536
  23.1 12.7 %shard_map.75 = (f32[16,32,512]{2,1,0:T(8,128)S(1)}, bf16[16,80,512]{2,1,0:T(8,128)(2,1)S(1)}, bf16[4,512,80]{2,1,0:T(8,128)(2,1)S(1)}) custom-call(s32[4]{0:T(128)S(1)} %copy-done.1, s32[8,16]{1,0:T(8,128)S(1)} %copy-done.7, bf16[16,64,512]{2,1,0:T(8,128)(2,1)S(1)} %bitcast.10, bf16[4,32,512]{2,1,0:T(8,128)(2,1)S(1)} %copy-done.5, ...), custom_call_target="tpu_custom_call" | custom-call | flops 14000000000 | bytes 1048576 | tf_op jit(solution)/shard_map/pallas_call | solution.py:21
  35.9 6.4 %shard_map.76 = (f32[16,8192]{1,0:T(8,128)S(1)}, bf16[16,8192]{1,0:T(8,128)(2,1)S(1)}, bf16[16,80,256]{2,1,0:T(8,128)(2,1)S(1)}) custom-call(s32[8,16]{1,0:T(8,128)S(1)} %copy-done.8, f32[16,32,512]{2,1,0:T(8,128)S(1)} %get-tuple-element.32.near_ref, bf16[16,80,512]{2,1,0:T(8,128)(2,1)S(1)} %get-tuple-element.33.tgt_ref, ...), custom_call_target="tpu_custom_call" | custom-call | flops 6000000000 | bytes 1048576 | tf_op jit(solution)/shard_map/pallas_call | solution.py:21
  42.4 1.6 %shard_map.78 = (bf16[12,256,80]{2,1,0:T(8,128)(2,1)S(1)}, bf16[12,32,256]{2,1,0:T(8,128)(2,1)S(1)}, s32[144]{0:T(256)S(1)}) custom-call(s32[8,16]{1,0:T(8,128)S(1)} %copy-done.6, bf16[512,256]{1,0:T(8,128)(2,1)S(1)} %collective-permute-done.4.left_m.refs_0_, bf16[384,256]{1,0:T(8,128)(2,1)S(1)} %collective-permute-done.8.refs_1_, ...), custom_call_target="tpu_custom_call" | custom-call | flops 2000000000 | bytes 1048576 | tf_op jit(solution)/shard_map/pallas_call | solution.py:21
  44.2 3.1 %shard_map.79 = (f32[16,4096]{1,0:T(8,128)S(1)}, bf16[16,4096]{1,0:T(8,128)(2,1)S(1)}) custom-call(s32[144]{0:T(256)S(1)} %get-tuple-element.43.names, bf16[12,256,80]{2,1,0:T(8,128)(2,1)S(1)} %get-tuple-element.44.far_src, bf16[12,32,256]{2,1,0:T(8,128)(2,1)S(1)} %get-tuple-element.45.far_w, bf16[16,80,256]{2,1,0:T(8,128)(2,1)S(1)} %get-tuple-element.46.far_tgt, ...), custom_call_target="tpu_custom_call" | custom-call | flops 4000000000 | bytes 1048576 | tf_op jit(solution)/shard_map/pallas_call | solution.py:21
  47.3 1.1 %collective-permute-start.9 = (bf16[16,4096]{1,0:T(8,128)(2,1)S(1)}, bf16[16,4096]{1,0:T(8,128)(2,1)S(1)}, u32[]{:S(2)}, u32[]{:S(2)}) collective-permute-start(bf16[16,4096]{1,0:T(8,128)(2,1)S(1)} %get-tuple-element.48), channel_id=1, source_target_pairs={{0,1},{1,0},{2,3},{3,2},{4,5},{5,4},{6,7},{7,6},{8,9},{9,8},{10,11... | collective-permute-start | bytes 393224 | tf_op jit(solution)/shard_map/ppermute | solution.py:345
  48.4 1.0 %collective-permute-done.9.back_ref = bf16[16,4096]{1,0:T(8,128)(2,1)S(1)} collective-permute-done((bf16[16,4096]{1,0:T(8,128)(2,1)S(1)}, bf16[16,4096]{1,0:T(8,128)(2,1)S(1)}, u32[]{:S(2)}, u32[]{:S(2)}) %collective-permute-start.9) | collective-permute-done | bytes 131104 | tf_op jit(solution)/shard_map/ppermute | solution.py:345
  49.4 3.4 %collective-permute-done.7.refs_1_.refs_0_ = bf16[16,8192]{1,0:T(8,128)(2,1)S(1)} collective-permute-done((bf16[16,8192]{1,0:T(8,128)(2,1)S(1)}, bf16[16,8192]{1,0:T(8,128)(2,1)S(1)}, u32[]{:S(2)}, u32[]{:S(2)}) %collective-permute-start.7) | collective-permute-done | bytes 262176 | tf_op jit(solution)/shard_map/ppermute | solution.py:345
  52.9 0.4 collective-permute-start.10
  53.2 3.5 %shard_map.77 = (f32[512,256]{1,0:T(8,128)S(1)}, s32[1,8192]{1,0:T(1,128)S(1)}) custom-call(s32[1,8192]{1,0:T(1,128)S(1)} %copy-done.3, s32[16,512]{1,0:T(8,128)S(1)} %copy-done.4, bf16[16,8192]{1,0:T(8,128)(2,1)S(1)} %add_convert_fusion.refs_0_.after_ref, bf16[16,8192]{1,0:T(8,128)(2,1)S(1)} %collective-permute-done.7.refs_1_.refs_0_), custom_call_target="tpu_custom_call" | custom-call | flops 5000000000 | bytes 1048576 | tf_op jit(solution)/shard_map/pallas_call | solution.py:21
  56.7 1.3 %collective-permute-done.10.refs_1_ = bf16[16,4096]{1,0:T(8,128)(2,1)S(1)} collective-permute-done((bf16[16,4096]{1,0:T(8,128)(2,1)S(1)}, bf16[16,4096]{1,0:T(8,128)(2,1)S(1)}, u32[]{:S(2)}, u32[]{:S(2)}) %collective-permute-start.10) | collective-permute-done | bytes 131104 | tf_op jit(solution)/shard_map/ppermute | solution.py:345
  58.1 3.5 %shard_map.81 = f32[16,8192]{1,0:T(8,128)} custom-call(s32[1,8192]{1,0:T(1,128)S(1)} %get-tuple-element.39.comp_ref, bf16[16,256,256]{2,1,0:T(8,128)(2,1)S(1)} %copy-done.2, f32[512,256]{1,0:T(8,128)S(1)} %get-tuple-element.40.start_ref, bf16[16,4096]{1,0:T(8,128)(2,1)S(1)} %shard_map.80.refs_0_, bf16[16,4096]{1,0:T(8,128)(2,1)S(1)} %collective-permute-done.10.refs_1_), custom_call_target="tpu_custom_call" | custom-call | flops 4000000000 | bytes 1048576 | tf_op jit(solution)/shard_map/pallas_call | solution.py:21
  (31 shorter events, 0.6 us)
Async XLA Ops:
  0.0 9.4 %collective-permute-start = (bf16[16,8192]{1,0:T(8,128)(2,1)}, bf16[16,8192]{1,0:T(8,128)(2,1)S(1)}, u32[]{:S(2)}, u32[]{:S(2)}) collective-permute-start(bf16[16,8192]{1,0:T(8,128)(2,1)} %bitcast.14), channel_id=1, source_target_pairs={{0,1},{1,0},{2,3},{3,2},{4,5},{5,4},{6,7},{7,6},{8,9},{9,8},{10,11... | collective-permute-start | bytes 786440 | tf_op jit(solution)/shard_map/ppermute | solution.py:345
  3.5 5.8 %collective-permute-start.1 = (s32[12,16]{1,0:T(8,128)}, s32[12,16]{1,0:T(8,128)S(1)}, u32[]{:S(2)}, u32[]{:S(2)}) collective-permute-start(s32[12,16]{1,0:T(8,128)} %get-tuple-element.27.refs_0_), channel_id=1, source_target_pairs={{0,2},{2,0},{1,3},{3,1},{4,6},{6,4},{5,7},{7,5},{8,10},{10,8},{9,1... | collective-permute-start | bytes 2312 | tf_op jit(solution)/shard_map/ppermute | solution.py:345
  6.1 15.4 %collective-permute-start.2 = (bf16[2,64,512]{2,1,0:T(8,128)(2,1)}, bf16[2,64,512]{2,1,0:T(8,128)(2,1)S(1)}, u32[]{:S(2)}, u32[]{:S(2)}) collective-permute-start(bf16[2,64,512]{2,1,0:T(8,128)(2,1)} %get-tuple-element.30), channel_id=1, source_target_pairs={{0,4},{4,0},{8,12},{12,8},{1,5},{5,1},{9,13},{13,9},{2,6},{6,2},{1... | collective-permute-start | bytes 393224 | tf_op jit(solution)/shard_map/ppermute | solution.py:393
  7.7 13.9 %copy-start = (bf16[16,512,64]{1,2,0:T(8,128)(2,1)S(1)}, bf16[16,512,64]{1,2,0:T(8,128)(2,1)}, u32[]{:S(2)}) copy-start(bf16[16,512,64]{1,2,0:T(8,128)(2,1)} %param.7) | copy-start | bytes 3145732
  7.7 13.9 %copy-start.1 = (s32[4]{0:T(128)S(1)}, s32[4]{0:T(128)}, u32[]{:S(2)}) copy-start(s32[4]{0:T(128)} %pad_add_fusion.ids_ref) | copy-start | bytes 52
  7.7 13.9 %collective-permute-start.3 = (bf16[2,64,512]{2,1,0:T(8,128)(2,1)}, bf16[2,64,512]{2,1,0:T(8,128)(2,1)S(1)}, u32[]{:S(2)}, u32[]{:S(2)}) collective-permute-start(bf16[2,64,512]{2,1,0:T(8,128)(2,1)} %get-tuple-element.31), channel_id=1, source_target_pairs={{0,0},{4,8},{8,4},{12,12},{1,1},{5,9},{9,5},{13,13},{2,2},{6,10},{... | collective-permute-start | bytes 393224 | tf_op jit(solution)/shard_map/ppermute | solution.py:394
  9.3 0.6 copy-start.10
  9.9 0.7 %copy-start.9 = (bf16[16,8192]{1,0:T(8,128)(2,1)}, bf16[16,8192]{1,0:T(8,128)(2,1)S(1)}, u32[]{:S(2)}) copy-start(bf16[16,8192]{1,0:T(8,128)(2,1)S(1)} %collective-permute-done.other_ref) | copy-start | bytes 786436
  16.4 19.4 %collective-permute-start.4 = (bf16[512,256]{1,0:T(8,128)(2,1)}, bf16[512,256]{1,0:T(8,128)(2,1)S(1)}, u32[]{:S(2)}, u32[]{:S(2)}) collective-permute-start(bf16[512,256]{1,0:T(8,128)(2,1)} %get-tuple-element.35), channel_id=1, source_target_pairs={{0,4},{4,8},{8,12},{12,0},{1,5},{5,9},{9,13},{13,1},{2,6},{6,10},{... | collective-permute-start | bytes 786440 | tf_op jit(solution)/shard_map/ppermute | solution.py:422
  20.0 15.8 %collective-permute-start.5 = (bf16[512,256]{1,0:T(8,128)(2,1)}, bf16[512,256]{1,0:T(8,128)(2,1)S(1)}, u32[]{:S(2)}, u32[]{:S(2)}) collective-permute-start(bf16[512,256]{1,0:T(8,128)(2,1)} %get-tuple-element.36), channel_id=1, source_target_pairs={{0,12},{4,0},{8,4},{12,8},{1,13},{5,1},{9,5},{13,9},{2,14},{6,2},{... | collective-permute-start | bytes 786440 | tf_op jit(solution)/shard_map/ppermute | solution.py:422
  20.3 22.1 %collective-permute-start.8 = (bf16[384,256]{1,0:T(8,128)(2,1)}, bf16[384,256]{1,0:T(8,128)(2,1)S(1)}, u32[]{:S(2)}, u32[]{:S(2)}) collective-permute-start(bf16[384,256]{1,0:T(8,128)(2,1)} %get-tuple-element.42), channel_id=1, source_target_pairs={{0,8},{4,12},{8,0},{12,4},{1,9},{5,13},{9,1},{13,5},{2,10},{6,14},... | collective-permute-start | bytes 589832 | tf_op jit(solution)/shard_map/ppermute | solution.py:422
  21.5 0.9 %copy-start.5 = (bf16[4,32,512]{2,1,0:T(8,128)(2,1)S(1)}, bf16[4,32,512]{2,1,0:T(8,128)(2,1)}, u32[]{:S(2)}) copy-start(bf16[4,32,512]{2,1,0:T(8,128)(2,1)} %get-tuple-element.29.tw_ref) | copy-start | bytes 393220
  22.5 0.7 %copy-start.7 = (s32[8,16]{1,0:T(8,128)S(1)}, s32[8,16]{1,0:T(8,128)}, u32[]{:S(2)}) copy-start(s32[8,16]{1,0:T(8,128)} %get-tuple-element.28.cnt_ref) | copy-start | bytes 1540
  23.1 12.7 %copy-start.4 = (s32[16,512]{1,0:T(8,128)S(1)}, s32[16,512]{1,0:T(8,128)}, u32[]{:S(2)}) copy-start(s32[16,512]{1,0:T(8,128)} %skel_ref.5) | copy-start | bytes 98308
  23.1 12.7 %copy-start.8 = (s32[8,16]{1,0:T(8,128)S(1)}, s32[8,16]{1,0:T(8,128)}, u32[]{:S(2)}) copy-start(s32[8,16]{1,0:T(8,128)} %get-tuple-element.28.cnt_ref) | copy-start | bytes 1540
  35.9 6.5 %copy-start.6 = (s32[8,16]{1,0:T(8,128)S(1)}, s32[8,16]{1,0:T(8,128)}, u32[]{:S(2)}) copy-start(s32[8,16]{1,0:T(8,128)} %get-tuple-element.41.far_ref) | copy-start | bytes 1540
  42.3 1.7 %collective-permute-start.6 = (bf16[16,8192]{1,0:T(8,128)(2,1)S(1)}, bf16[16,8192]{1,0:T(8,128)(2,1)S(1)}, u32[]{:S(2)}, u32[]{:S(2)}) collective-permute-start(bf16[16,8192]{1,0:T(8,128)(2,1)S(1)} %get-tuple-element.38), channel_id=1, source_target_pairs={{0,1},{1,0},{2,3},{3,2},{4,5},{5,4},{6,7},{7,6},{8,9},{9,8},{10,11... | collective-permute-start | bytes 786440 | tf_op jit(solution)/shard_map/ppermute | solution.py:345
  44.1 8.8 %collective-permute-start.7 = (bf16[16,8192]{1,0:T(8,128)(2,1)S(1)}, bf16[16,8192]{1,0:T(8,128)(2,1)S(1)}, u32[]{:S(2)}, u32[]{:S(2)}) collective-permute-start(bf16[16,8192]{1,0:T(8,128)(2,1)S(1)} %add_convert_fusion.refs_0_.after_ref), channel_id=1, source_target_pairs={{0,2},{2,0},{1,3},{3,1},{4,6},{6,4},{5,7},{7,5},{8,10},{10,8},{9,1... | collective-permute-start | bytes 786440 | tf_op jit(solution)/shard_map/ppermute | solution.py:345
  44.2 9.1 %copy-start.3 = (s32[1,8192]{1,0:T(1,128)S(1)}, s32[1,8192]{1,0:T(1,128)}, u32[]{:S(2)}) copy-start(s32[1,8192]{1,0:T(1,128)} %order_ref.3) | copy-start | bytes 98308
  47.3 2.1 %collective-permute-start.9 = (bf16[16,4096]{1,0:T(8,128)(2,1)S(1)}, bf16[16,4096]{1,0:T(8,128)(2,1)S(1)}, u32[]{:S(2)}, u32[]{:S(2)}) collective-permute-start(bf16[16,4096]{1,0:T(8,128)(2,1)S(1)} %get-tuple-element.48), channel_id=1, source_target_pairs={{0,1},{1,0},{2,3},{3,2},{4,5},{5,4},{6,7},{7,6},{8,9},{9,8},{10,11... | collective-permute-start | bytes 393224 | tf_op jit(solution)/shard_map/ppermute | solution.py:345
  52.9 5.2 %copy-start.2 = (bf16[16,256,256]{2,1,0:T(8,128)(2,1)S(1)}, bf16[16,256,256]{2,1,0:T(8,128)(2,1)}, u32[]{:S(2)}) copy-start(bf16[16,256,256]{2,1,0:T(8,128)(2,1)} %interp_ref.3) | copy-start | bytes 6291460
  52.9 5.2 %collective-permute-start.10 = (bf16[16,4096]{1,0:T(8,128)(2,1)S(1)}, bf16[16,4096]{1,0:T(8,128)(2,1)S(1)}, u32[]{:S(2)}, u32[]{:S(2)}) collective-permute-start(bf16[16,4096]{1,0:T(8,128)(2,1)S(1)} %shard_map.80.refs_0_), channel_id=1, source_target_pairs={{0,2},{2,0},{1,3},{3,1},{4,6},{6,4},{5,7},{7,5},{8,10},{10,8},{9,1... | collective-permute-start | bytes 393224 | tf_op jit(solution)/shard_map/ppermute | solution.py:345

commit v4 on v3

--- a/solution.py
+++ b/solution.py
@@ -67,19 +67,21 @@
     return jnp.exp2(dot(sources, targets) * scale).astype(BF)
 
 
-def halo_body(ids_ref, pts_ref, near_ref, far_ref, first_ref, second_ref, pairs_ref, near_buf, far_buf, sems):
-    halo = first_ref.shape[0]
-    even = 1 - lax.rem(ids_ref[0], 2)
-    mine, classes = ids_ref[2], ids_ref[3]
+def class_of():
+    return lax.axis_index("pair") * lax.axis_size("rhs") + lax.axis_index("rhs")
+
+
+def halo_body(classes, pts_ref, near_ref, far_ref, up_ref, down_ref, pairs_ref, near_buf, far_buf, sems):
+    halo = up_ref.shape[0]
     half = pts_ref.shape[0] // 2
     copies = [
         pltpu.make_async_copy(near_ref, near_buf, sems.at[2 * halo]),
         pltpu.make_async_copy(far_ref, far_buf, sems.at[2 * halo + 1]),
     ]
     for j in range(halo):
-        leaf = mine + j * classes
-        copies.append(pltpu.make_async_copy(pts_ref.at[leaf + even * half], first_ref.at[j], sems.at[j]))
-        copies.append(pltpu.make_async_copy(pts_ref.at[leaf + (1 - even) * half], second_ref.at[j], sems.at[halo + j]))
+        leaf = class_of() + j * classes
+        copies.append(pltpu.make_async_copy(pts_ref.at[leaf + half], up_ref.at[j], sems.at[j]))
+        copies.append(pltpu.make_async_copy(pts_ref.at[leaf], down_ref.at[j], sems.at[halo + j]))
     for copy in copies:
         copy.start()
     for copy in copies:
@@ -90,7 +92,7 @@
 
 
 def weights_body(
-    blocks, classes, near_n, ids_ref, own_ref, other_ref, order_ref, skel_ref, interp_ref, pts_ref, *refs
+    blocks, classes, near_n, span, own_ref, other_ref, order_ref, skel_ref, interp_ref, pts_ref, *refs
 ):
     pair_refs = refs[:-13]
     tw_ref, up_ref, mid_ref, down_ref, cnt_ref, far_ref = refs[-13:-7]
@@ -106,7 +108,8 @@
     cuts = size // rank
     halo = (up_ref.shape[0] - mid_ref.shape[0]) // (cuts * step)
     leaves = pts_ref.shape[0]
-    block, base, me = ids_ref[0], ids_ref[1], ids_ref[2]
+    block, me = lax.axis_index("leaf"), class_of()
+    base = block * leaves - span
     copies = [
         pltpu.make_async_copy(own_ref, own_buf, sems.at[0]),
         pltpu.make_async_copy(order_ref, order_buf, sems.at[1]),
@@ -135,8 +138,8 @@
         code = target * 256 + piece * mine + lax.div(within, classes)
         far_ref[k * far_n : (k + 1) * far_n] = jnp.where(lax.rem(within, classes) == me, code, -1)
 
-    for copy in copies:
-        copy.wait()
+    copies[0].wait()
+    copies[1].wait()
     for hi in range(turns):
         span = slice(hi * width, (hi + 1) * width)
         stack[hi * step : hi * step + cols] = own_buf[:, span]
@@ -156,6 +159,9 @@
                 for cut in range(cuts):
                     at = mine * tall + (place * cuts + cut) * step
                     ref[at : at + step] = tree[:, cut * rank : (cut + 1) * rank]
+        if j == 0:
+            for copy in copies[2:]:
+                copy.wait()
         hot = one_hot(skel_buf[pl.ds(leaf, 1), :], size)
         ordered = dot(tree, hot)
         combined = dot_last(ordered[:, rank:].astype(BF), interp_buf[j])
@@ -166,83 +172,103 @@
             ref[j * tall + dim : (j + 1) * tall] = skel_w
 
 
-def near_sum(t, first, count, most, scale, cnt_ref, slots, tgt, src, weights, write, shift=0):
+def list_named(t, first, count, cnt_ref, slots, at):
     found = jnp.int32(0)
     for e in range(count):
-        slots[found] = jnp.int32(e)
+        slots[at + found] = jnp.int32(e)
         found = found + jnp.where(cnt_ref[first + e, t] > 0, 1, 0)
-    for k in range(most + 1):
-
-        @pl.when(found == k)
-        def _():
-            names = [slots[j] for j in range(k)]
-            if k == 0:
-                write(t, jnp.zeros((weights.shape[1], tgt.shape[2]), F32))
-                return
-            size = src.shape[1]
-            block = gauss(jnp.concatenate([src[s + shift] for s in names], axis=0), tgt[t], scale)
-            total = None
-            for j, s in enumerate(names):
-                times = cnt_ref[first + s, t].astype(F32)
-                part = dot(weights[s + shift], block[j * size : (j + 1) * size]) * times
-                total = part if total is None else total + part
-            write(t, total)
+    return found
+
+
+def named_sum(t, k, first, scale, cnt_ref, slots, at, tgt, src, weights, shift):
+    if k == 0:
+        return jnp.zeros((weights.shape[1], tgt.shape[2]), F32)
+    names = [slots[at + j] for j in range(k)]
+    size = src.shape[1]
+    block = gauss(jnp.concatenate([src[s + shift] for s in names], axis=0), tgt[t], scale)
+    total = None
+    for j, s in enumerate(names):
+        times = cnt_ref[first + s, t].astype(F32)
+        part = dot(weights[s + shift], block[j * size : (j + 1) * size]) * times
+        total = part if total is None else total + part
+    return total
 
 
 def near_body(
-    halo, scale, ids_ref, cnt_ref, pts_ref, tw_ref, first_p, second_p, near_ref, tgt_ref, edge_src, src, slots
+    halo, scale, cnt_ref, pts_ref, tw_ref, left_p, right_p, skel_ref,
+    near_ref, tgt_ref, edge_src, far_tgt_ref, src, slots,
 ):
-    leaves = pts_ref.shape[0]
+    leaves, _, size = pts_ref.shape
     mine = tw_ref.shape[0]
     classes = leaves // mine
+    rank = far_tgt_ref.shape[2]
 
     def sources(j, _):
-        src[j] = as_sources(pts_ref[j * classes + ids_ref[2]])
+        src[j] = as_sources(pts_ref[j * classes + class_of()])
         return 0
 
     lax.fori_loop(0, mine, sources, 0)
-    odd = lax.rem(ids_ref[0], 2)
+    tgt_ref[0] = as_targets(pts_ref[0])
+
+    def target(t, _):
+        found = list_named(t, halo, mine, cnt_ref, slots, 0)
+        for k in range(mine + 1):
+
+            @pl.when(found == k)
+            def _():
+                total = named_sum(t, k, halo, scale, cnt_ref, slots, 0, tgt_ref, src, tw_ref, 0)
+                hot = one_hot(skel_ref[pl.ds(t, 1), :rank], size)
+                far_tgt = as_targets(dot(pts_ref[t], hot).astype(BF))
+                later = jnp.minimum(t + 1, leaves - 1)
+                following = as_targets(pts_ref[later])
+                near_ref[t] = total
+                far_tgt_ref[t] = far_tgt
+                tgt_ref[later] = following
+
+        return 0
+
+    lax.fori_loop(0, leaves, target, 0)
     for j in range(halo):
-        edge_src[(1 - odd) * halo + j] = as_sources(first_p[j])
-        edge_src[odd * halo + j] = as_sources(second_p[j])
-
-    def write(t, value):
-        near_ref[t] = value
-
-    def target(t, _):
-        tgt_ref[t] = as_targets(pts_ref[t])
-        near_sum(t, halo, mine, mine, scale, cnt_ref, slots, tgt_ref, src, tw_ref, write)
-        return 0
-
-    lax.fori_loop(0, leaves, target, 0)
+        edge_src[j] = as_sources(left_p[j])
+        edge_src[halo + j] = as_sources(right_p[j])
 
 
 def edge_body(
-    halo, mine, scale, cnt_ref, near_ref, tgt_ref, src, left_m, right_m, pts_ref, skel_ref,
-    own_ref, other_ref, far_tgt_ref, wts, slots,
+    halo, mine, rank, scale, cnt_ref, near_ref, tgt_ref, src, left_m, right_m, own_ref, other_ref, wts, slots
 ):
     leaves, cols2, size = near_ref.shape
     cols = cols2 // 2
-    rank = far_tgt_ref.shape[2]
-    for j in range(halo):
-        for side, ref in enumerate((left_m, right_m)):
-            for cut in range(size // rank):
-                at = ref.shape[0] - (halo * (size // rank) - j * (size // rank) - cut) * cols2
-                wts[side * halo + j, :, cut * rank : (cut + 1) * rank] = ref[at : at + cols2]
-
-    def write(t, value):
-        total = near_ref[t] + value
-        own_ref[:, pl.ds(pl.multiple_of(t * size, size), size)] = total[:cols]
-        other_ref[:, pl.ds(pl.multiple_of(t * size, size), size)] = total[cols:].astype(BF)
-
-    def target(t, _):
-        right = jnp.where(t < leaves // 2, 0, 1)
-        near_sum(t, right * (halo + mine), halo, halo, scale, cnt_ref, slots, tgt_ref, src, wts, write, right * halo)
-        hot = one_hot(skel_ref[pl.ds(t, 1), :rank], size)
-        far_tgt_ref[t] = as_targets(dot(pts_ref[t], hot).astype(BF))
+    quarter = leaves // 4
+    cuts = size // rank
+    for side, message in enumerate((left_m, right_m)):
+        for j in range(halo):
+            for cut in range(cuts):
+                at = message.shape[0] - (halo * cuts - j * cuts - cut) * cols2
+                wts[side * halo + j, :, cut * rank : (cut + 1) * rank] = message[at : at + cols2]
+
+    def targets(i, _):
+        right = lax.div(i, quarter)
+        first = right * (halo + mine)
+        pair = (right * quarter + i, right * quarter + i + quarter)
+        founds = [list_named(t, first, halo, cnt_ref, slots, n * (halo + 1)) for n, t in enumerate(pair)]
+        for k in range((halo + 1) ** 2):
+            counts = divmod(k, halo + 1)
+
+            @pl.when((founds[0] == counts[0]) & (founds[1] == counts[1]))
+            def _():
+                sums = [
+                    named_sum(t, c, first, scale, cnt_ref, slots, n * (halo + 1), tgt_ref, src, wts, right * halo)
+                    for n, (t, c) in enumerate(zip(pair, counts))
+                ]
+                totals = [near_ref[t] + part for t, part in zip(pair, sums)]
+                for t, total in zip(pair, totals):
+                    span = pl.ds(pl.multiple_of(t * size, size), size)
+                    own_ref[:, span] = total[:cols]
+                    other_ref[:, span] = total[cols:].astype(BF)
+
         return 0
 
-    lax.fori_loop(0, leaves, target, 0)
+    lax.fori_loop(0, 2 * quarter, targets, 0)
 
 
 def sources_body(mine, far_ref, *refs):
@@ -336,6 +362,10 @@
         out_ref[:, hi * width : (hi + 1) * width] = acc[hi * cols : (hi + 1) * cols]
 
 
+def pin(value):
+    return pltpu.with_memory_space_constraint(value, pltpu.HBM)
+
+
 def ring(count, by):
     return [(i, (i + by) % count) for i in range(count)]
 
@@ -360,42 +390,34 @@
     mine = leaves // classes
     span = min(8, leaves)
     halo = span // classes
-    block = lax.axis_index("leaf")
-    mine_id = lax.axis_index("pair") * rhs_n + lax.axis_index("rhs")
     scale = 2.0 * 2.5 / dim * LOG2E
     near_n, far_n = near_pairs.shape[1], far_pairs.shape[1]
     wide = dim + EXTRA
     mega = 10 ** 9
-    ids = jnp.stack([block, block * leaves - span, mine_id, jnp.int32(classes)]).astype(jnp.int32)
     pts = points.transpose(0, 2, 1)
     wts = weights.T
     (other_wts,) = from_others(wts, "rhs")
-    swaps = []
-    for start in (0, 1):
-        swap = {i: i for i in range(blocks)}
-        for i in range(start, blocks - 1, 2):
-            swap[i], swap[i + 1] = i + 1, i
-        swaps.append(list(swap.items()))
     hbm = pl.BlockSpec(memory_space=pltpu.HBM)
-    first_p, second_p, pairs = call(
-        halo_body,
+    up_p, down_p, pairs = call(
+        functools.partial(halo_body, classes),
         [((halo, dim, size), BF), ((halo, dim, size), BF), ((near_n + far_n, leaves), jnp.int32)],
-        [SMEM, hbm, hbm, hbm],
-        (ids, pts, near_pairs.T, far_pairs.T),
+        [hbm, hbm, hbm],
+        (pin(pts), pin(near_pairs.T), pin(far_pairs.T)),
         [
             pltpu.VMEM((near_n, leaves), jnp.int32),
             pltpu.VMEM((far_n, leaves), jnp.int32),
             pltpu.SemaphoreType.DMA((2 * halo + 2,)),
         ],
-        grant=60,
+        out_specs=[hbm, hbm, VMEM],
+        grant=48,
     )
     every = [pairs] + from_others(pairs, "pair")
-    first_p = lax.ppermute(first_p, "leaf", swaps[0])
-    second_p = lax.ppermute(second_p, "leaf", swaps[1])
+    left_p = lax.ppermute(up_p, "leaf", ring(blocks, 1))
+    right_p = lax.ppermute(down_p, "leaf", ring(blocks, blocks - 1))
     tall = mine * (dim + 2 * cols)
     extra = halo * (size // rank) * 2 * cols
     tree_w, up_m, mid_m, down_m, cnt, far_ids = call(
-        functools.partial(weights_body, blocks, classes, near_n),
+        functools.partial(weights_body, blocks, classes, near_n, span),
         [
             ((mine, 2 * cols, size), BF),
             ((tall + extra, rank), BF),
@@ -404,8 +426,8 @@
             ((2 * halo + mine, leaves), jnp.int32),
             ((pair_n * far_n, leaves), jnp.int32),
         ],
-        [SMEM, hbm, VMEM] + [hbm] * 4 + [VMEM] * pair_n,
-        (ids, wts, other_wts, tree_order, skel_order, interp, pts, *every),
+        [hbm, VMEM] + [hbm] * 4 + [VMEM] * pair_n,
+        (pin(wts), other_wts, pin(tree_order), pin(skel_order), pin(interp), pin(pts), *every),
         [
             pltpu.VMEM((2 * cols * (leaves * size // 256), 256), BF),
             pltpu.VMEM((cols, leaves * size), BF),
@@ -416,33 +438,44 @@
             pltpu.SemaphoreType.DMA((3 + 2 * mine,)),
         ],
         flops=3 * mega,
-        grant=60,
+        grant=48,
     )
     outgoing = {by: mid_m for by in range(1, blocks)} | {1: up_m, blocks - 1: down_m}
     pieces = [lax.ppermute(outgoing[by], "leaf", ring(blocks, by)) for by in range(1, blocks)]
-    near, tgt, edge_src = call(
+    near, tgt, edge_src, far_tgt = call(
         functools.partial(near_body, halo, scale),
-        [((leaves, 2 * cols, size), F32), ((leaves, wide, size), BF), ((2 * halo, size, wide), BF)],
-        [SMEM, SMEM, VMEM, VMEM, VMEM, VMEM],
-        (ids, cnt, pts, tree_w, first_p, second_p),
+        [
+            ((leaves, 2 * cols, size), F32),
+            ((leaves, wide, size), BF),
+            ((2 * halo, size, wide), BF),
+            ((leaves, wide, rank), BF),
+        ],
+        [SMEM] + [VMEM] * 5,
+        (cnt, pts, tree_w, left_p, right_p, skel_order),
         [pltpu.VMEM((mine, size, wide), BF), pltpu.SMEM((mine + 1,), jnp.int32)],
         flops=14 * mega,
     )
-    near_own, near_other, far_tgt = call(
-        functools.partial(edge_body, halo, mine, scale),
-        [((cols, leaves * size), F32), ((cols, leaves * size), BF), ((leaves, wide, rank), BF)],
-        [SMEM] + [VMEM] * 7,
-        (cnt, near, tgt, edge_src, pieces[0], pieces[-1], pts, skel_order),
-        [
-            pltpu.VMEM((2 * halo, 2 * cols, size), BF),
-            pltpu.SMEM((halo + 1,), jnp.int32),
-        ],
+
+    near_own, near_other = call(
+        functools.partial(edge_body, halo, mine, rank, scale),
+        [((cols, leaves * size), F32), ((cols, leaves * size), BF)],
+        [SMEM] + [VMEM] * 5,
+        (cnt, near, tgt, edge_src, pieces[0], pieces[-1]),
+        [pltpu.VMEM((2 * halo, 2 * cols, size), BF), pltpu.SMEM((2 * halo + 2,), jnp.int32)],
         flops=6 * mega,
     )
     (near_back,) = from_others(near_other, "rhs")
     near_sum_own = (near_own + near_back.astype(F32)).astype(BF)
     near_parts = over_pair(near_sum_own, pair_n)
     piece_n = (blocks - 1) * mine
+    far_src, far_w, names = call(
+        functools.partial(sources_body, mine),
+        [((piece_n, rank, wide), BF), ((piece_n, 2 * cols, rank), BF), ((leaves * pair_n * far_n + 16,), jnp.int32)],
+        [SMEM] + [VMEM] * (blocks - 1),
+        (far_ids, *pieces),
+        out_specs=[VMEM, VMEM, SMEM],
+        flops=2 * mega,
+    )
     far_src, far_w, names = call(
         functools.partial(sources_body, mine),
         [((piece_n, rank, wide), BF), ((piece_n, 2 * cols, rank), BF), ((leaves * pair_n * far_n + 16,), jnp.int32)],

time: 61.3 us -> 54.2 us (0.88)
  the two profiles are of different devices: /device:TPU:0 before, /device:TPU:12 now
where the time goes in v4:
time: 54.2 us; the launch traced here: 54.3 us
  Pallas kernels  35.1 us (65%)
  waiting for transfers between devices  9.71 us (18%)
  starting transfers between devices  9.3 us (17%)
    pallas_call x9, Pallas kernels, call(): pl.pallas_call(body, out_shape=outs, in_specs=specs, out_specs=out_specs...  35.1 us
    ppermute x6, waiting for transfers between devices, from_others(): lax.ppermute(value, axis, ring(count, by))  5.9 us
    ppermute x3, starting transfers between devices, on_device(): lax.ppermute(outgoing[by], 'leaf', ring(blocks, by))  4.66 us
    ppermute x3, waiting for transfers between devices, on_device(): lax.ppermute(outgoing[by], 'leaf', ring(blocks, by))  3.81 us
    ppermute x6, starting transfers between devices, from_others(): lax.ppermute(value, axis, ring(count, by))  2.62 us
    ppermute x1, starting transfers between devices, on_device(): left_p = lax.ppermute(up_p, 'leaf', ring(blocks, 1))  1.58 us
  transfers between devices with their start and end apart: 11, of which 6 were waited for; matrix products, arithmetic and copies ran while one was open for 0% of the time, Pallas kernels for 58%

profile of v4, /device:TPU:12, one launch (start us, length us, event | category | flops | bytes accessed | tf_op | source)
XLA Modules:
  0.0 54.3 jit_solution(315519030437198273)
XLA Ops:
  0.0 1.0 %shard_map.73 = (bf16[2,64,512]{2,1,0:T(8,128)(2,1)S(1)}, bf16[2,64,512]{2,1,0:T(8,128)(2,1)S(1)}, s32[12,16]{1,0:T(8,128)S(1)}) custom-call(bf16[16,64,512]{2,1,0:T(8,128)(2,1)} %bitcast.5, s32[8,16]{1,0:T(8,128)} %bitcast.8, s32[4,16]{1,0:T(4,128)} %bitcast.9), custom_call_target="tpu_custom_call" | custom-call | bytes 1048576 | tf_op jit(solution)/shard_map/pallas_call | solution.py:21
  1.0 1.6 %collective-permute-start.1 = (s32[12,16]{1,0:T(8,128)S(1)}, s32[12,16]{1,0:T(8,128)S(1)}, u32[]{:S(2)}, u32[]{:S(2)}) collective-permute-start(s32[12,16]{1,0:T(8,128)S(1)} %get-tuple-element.27.refs_0_), channel_id=1, source_target_pairs={{0,2},{2,0},{1,3},{3,1},{4,6},{6,4},{5,7},{7,5},{8,10},{10,8},{9,1... | collective-permute-start | bytes 2312 | tf_op jit(solution)/shard_map/ppermute | solution.py:375
  2.6 1.6 %collective-permute-start.2 = (bf16[2,64,512]{2,1,0:T(8,128)(2,1)S(1)}, bf16[2,64,512]{2,1,0:T(8,128)(2,1)S(1)}, u32[]{:S(2)}, u32[]{:S(2)}) collective-permute-start(bf16[2,64,512]{2,1,0:T(8,128)(2,1)S(1)} %get-tuple-element.30), channel_id=1, source_target_pairs={{0,4},{4,8},{8,12},{12,0},{1,5},{5,9},{9,13},{13,1},{2,6},{6,10},{... | collective-permute-start | bytes 393224 | tf_op jit(solution)/shard_map/ppermute | solution.py:415
  4.2 0.4 collective-permute-start.3
  4.6 0.1 collective-permute-done.1.refs_1_
  4.7 3.7 %shard_map.74 = (bf16[4,32,512]{2,1,0:T(8,128)(2,1)S(1)}, bf16[512,256]{1,0:T(8,128)(2,1)S(1)}, bf16[384,256]{1,0:T(8,128)(2,1)S(1)}, bf16[512,256]{1,0:T(8,128)...) custom-call(bf16[16,8192]{1,0:T(8,128)(2,1)} %bitcast.11, bf16[16,8192]{1,0:T(8,128)(2,1)S(1)} %collective-permute-done.other_ref, ...), custom_call_target="tpu_custom_call" | custom-call | flops 3000000000 | bytes 1048576 | tf_op jit(solution)/shard_map/pallas_call | solution.py:21
  8.5 1.6 %collective-permute-start.4 = (bf16[512,256]{1,0:T(8,128)(2,1)S(1)}, bf16[512,256]{1,0:T(8,128)(2,1)S(1)}, u32[]{:S(2)}, u32[]{:S(2)}) collective-permute-start(bf16[512,256]{1,0:T(8,128)(2,1)S(1)} %get-tuple-element.35), channel_id=1, source_target_pairs={{0,4},{4,8},{8,12},{12,0},{1,5},{5,9},{9,13},{13,1},{2,6},{6,10},{... | collective-permute-start | bytes 786440 | tf_op jit(solution)/shard_map/ppermute | solution.py:444
  10.1 0.6 %collective-permute-start.5 = (bf16[512,256]{1,0:T(8,128)(2,1)S(1)}, bf16[512,256]{1,0:T(8,128)(2,1)S(1)}, u32[]{:S(2)}, u32[]{:S(2)}) collective-permute-start(bf16[512,256]{1,0:T(8,128)(2,1)S(1)} %get-tuple-element.36), channel_id=1, source_target_pairs={{0,12},{4,0},{8,4},{12,8},{1,13},{5,1},{9,5},{13,9},{2,14},{6,2},{... | collective-permute-start | bytes 786440 | tf_op jit(solution)/shard_map/ppermute | solution.py:444
  10.7 2.4 %collective-permute-start.8 = (bf16[384,256]{1,0:T(8,128)(2,1)S(1)}, bf16[384,256]{1,0:T(8,128)(2,1)S(1)}, u32[]{:S(2)}, u32[]{:S(2)}) collective-permute-start(bf16[384,256]{1,0:T(8,128)(2,1)S(1)} %get-tuple-element.42), channel_id=1, source_target_pairs={{0,8},{4,12},{8,0},{12,4},{1,9},{5,13},{9,1},{13,5},{2,10},{6,14},... | collective-permute-start | bytes 589832 | tf_op jit(solution)/shard_map/ppermute | solution.py:444
  13.1 11.9 %shard_map.75 = (f32[16,32,512]{2,1,0:T(8,128)S(1)}, bf16[16,80,512]{2,1,0:T(8,128)(2,1)S(1)}, bf16[4,512,80]{2,1,0:T(8,128)(2,1)S(1)}, bf16[16,80,256]{2,1,0:T(8,128)(2,1)S(1)}) custom-call(s32[8,16]{1,0:T(8,128)S(1)} %get-tuple-element.28.cnt_ref, bf16[16,64,512]{2,1,0:T(8,128)(2,1)S(1)} %bitcast.7, bf16[4,32,512]{2,1,0:T(8,128)(2,1)S(1)} %get-tuple-element.29.tw_ref, ...), custom_call_target="tpu_custom_call" | custom-call | flops 14000000000 | bytes 1048576 | tf_op jit(solution)/shard_map/pallas_call | solution.py:21
  25.1 1.6 %collective-permute-done.4.left_m.refs_0_ = bf16[512,256]{1,0:T(8,128)(2,1)S(1)} collective-permute-done((bf16[512,256]{1,0:T(8,128)(2,1)S(1)}, bf16[512,256]{1,0:T(8,128)(2,1)S(1)}, u32[]{:S(2)}, u32[]{:S(2)}) %collective-permute-start.4) | collective-permute-done | bytes 262176 | tf_op jit(solution)/shard_map/ppermute | solution.py:444
  26.7 2.2 %collective-permute-done.5.right_m.refs_2_ = bf16[512,256]{1,0:T(8,128)(2,1)S(1)} collective-permute-done((bf16[512,256]{1,0:T(8,128)(2,1)S(1)}, bf16[512,256]{1,0:T(8,128)(2,1)S(1)}, u32[]{:S(2)}, u32[]{:S(2)}) %collective-permute-start.5) | collective-permute-done | bytes 262176 | tf_op jit(solution)/shard_map/ppermute | solution.py:444
  28.9 6.1 %shard_map.76 = (f32[16,8192]{1,0:T(8,128)S(1)}, bf16[16,8192]{1,0:T(8,128)(2,1)S(1)}) custom-call(s32[8,16]{1,0:T(8,128)S(1)} %get-tuple-element.28.cnt_ref, f32[16,32,512]{2,1,0:T(8,128)S(1)} %get-tuple-element.32.near_ref, bf16[16,80,512]{2,1,0:T(8,128)(2,1)S(1)} %get-tuple-element.33.tgt_ref, bf16[4,512,80]{2,1,0:T(8,128)(2,1)S(1)} %get-tuple-element.34.src, ...), custom_call_target="tpu_custom_call" | custom-call | flops 6000000000 | bytes 1048576 | tf_op jit(solution)/shard_map/pallas_call | solution.py:21
  35.0 0.1 collective-permute-start.6
  35.1 1.6 %shard_map.78 = (bf16[12,256,80]{2,1,0:T(8,128)(2,1)S(1)}, bf16[12,32,256]{2,1,0:T(8,128)(2,1)S(1)}, s32[144]{0:T(256)S(1)}) custom-call(s32[8,16]{1,0:T(8,128)S(1)} %get-tuple-element.41.far_ref, bf16[512,256]{1,0:T(8,128)(2,1)S(1)} %collective-permute-done.4.left_m.refs_0_, bf16[384,256]{1,0:T(8,128)(2,1)S(1)} %collective-permute-done.8.refs_1_, ...), custom_call_target="tpu_custom_call" | custom-call | flops 2000000000 | bytes 1048576 | tf_op jit(solution)/shard_map/pallas_call | solution.py:21
  36.8 0.1 collective-permute-start.7
  36.9 3.7 %shard_map.79 = (f32[16,4096]{1,0:T(8,128)S(1)}, bf16[16,4096]{1,0:T(8,128)(2,1)S(1)}) custom-call(s32[144]{0:T(256)S(1)} %get-tuple-element.43.names, bf16[12,256,80]{2,1,0:T(8,128)(2,1)S(1)} %get-tuple-element.44.far_src, bf16[12,32,256]{2,1,0:T(8,128)(2,1)S(1)} %get-tuple-element.45.far_w, bf16[16,80,256]{2,1,0:T(8,128)(2,1)S(1)} %get-tuple-element.46.far_tgt, ...), custom_call_target="tpu_custom_call" | custom-call | flops 4000000000 | bytes 1048576 | tf_op jit(solution)/shard_map/pallas_call | solution.py:21
  40.6 0.6 %collective-permute-start.9 = (bf16[16,4096]{1,0:T(8,128)(2,1)S(1)}, bf16[16,4096]{1,0:T(8,128)(2,1)S(1)}, u32[]{:S(2)}, u32[]{:S(2)}) collective-permute-start(bf16[16,4096]{1,0:T(8,128)(2,1)S(1)} %get-tuple-element.48), channel_id=1, source_target_pairs={{0,1},{1,0},{2,3},{3,2},{4,5},{5,4},{6,7},{7,6},{8,9},{9,8},{10,11... | collective-permute-start | bytes 393224 | tf_op jit(solution)/shard_map/ppermute | solution.py:375
  41.1 1.0 %collective-permute-done.9.back_ref = bf16[16,4096]{1,0:T(8,128)(2,1)S(1)} collective-permute-done((bf16[16,4096]{1,0:T(8,128)(2,1)S(1)}, bf16[16,4096]{1,0:T(8,128)(2,1)S(1)}, u32[]{:S(2)}, u32[]{:S(2)}) %collective-permute-start.9) | collective-permute-done | bytes 131104 | tf_op jit(solution)/shard_map/ppermute | solution.py:375
  42.1 3.5 %collective-permute-done.7.refs_1_.refs_0_ = bf16[16,8192]{1,0:T(8,128)(2,1)S(1)} collective-permute-done((bf16[16,8192]{1,0:T(8,128)(2,1)S(1)}, bf16[16,8192]{1,0:T(8,128)(2,1)S(1)}, u32[]{:S(2)}, u32[]{:S(2)}) %collective-permute-start.7) | collective-permute-done | bytes 262176 | tf_op jit(solution)/shard_map/ppermute | solution.py:375
  45.6 0.4 collective-permute-start.10
  46.0 3.5 %shard_map.77 = (f32[512,256]{1,0:T(8,128)S(1)}, s32[1,8192]{1,0:T(1,128)S(1)}) custom-call(s32[1,8192]{1,0:T(1,128)S(1)} %copy-done.2, s32[16,512]{1,0:T(8,128)S(1)} %copy-done.3, bf16[16,8192]{1,0:T(8,128)(2,1)S(1)} %add_convert_fusion.refs_0_.after_ref, bf16[16,8192]{1,0:T(8,128)(2,1)S(1)} %collective-permute-done.7.refs_1_.refs_0_), custom_call_target="tpu_custom_call" | custom-call | flops 5000000000 | bytes 1048576 | tf_op jit(solution)/shard_map/pallas_call | solution.py:21
  49.5 1.3 %collective-permute-done.10.refs_1_ = bf16[16,4096]{1,0:T(8,128)(2,1)S(1)} collective-permute-done((bf16[16,4096]{1,0:T(8,128)(2,1)S(1)}, bf16[16,4096]{1,0:T(8,128)(2,1)S(1)}, u32[]{:S(2)}, u32[]{:S(2)}) %collective-permute-start.10) | collective-permute-done | bytes 131104 | tf_op jit(solution)/shard_map/ppermute | solution.py:375
  50.8 3.5 %shard_map.81 = f32[16,8192]{1,0:T(8,128)} custom-call(s32[1,8192]{1,0:T(1,128)S(1)} %get-tuple-element.39.comp_ref, bf16[16,256,256]{2,1,0:T(8,128)(2,1)S(1)} %copy-done.1, f32[512,256]{1,0:T(8,128)S(1)} %get-tuple-element.40.start_ref, bf16[16,4096]{1,0:T(8,128)(2,1)S(1)} %shard_map.80.refs_0_, bf16[16,4096]{1,0:T(8,128)(2,1)S(1)} %collective-permute-done.10.refs_1_), custom_call_target="tpu_custom_call" | custom-call | flops 4000000000 | bytes 1048576 | tf_op jit(solution)/shard_map/pallas_call | solution.py:21
  (16 shorter events, 0.1 us)
Async XLA Ops:
  0.0 4.7 %collective-permute-start = (bf16[16,8192]{1,0:T(8,128)(2,1)}, bf16[16,8192]{1,0:T(8,128)(2,1)S(1)}, u32[]{:S(2)}, u32[]{:S(2)}) collective-permute-start(bf16[16,8192]{1,0:T(8,128)(2,1)} %bitcast.10), channel_id=1, source_target_pairs={{0,1},{1,0},{2,3},{3,2},{4,5},{5,4},{6,7},{7,6},{8,9},{9,8},{10,11... | collective-permute-start | bytes 786440 | tf_op jit(solution)/shard_map/ppermute | solution.py:375
  1.0 3.7 %collective-permute-start.1 = (s32[12,16]{1,0:T(8,128)S(1)}, s32[12,16]{1,0:T(8,128)S(1)}, u32[]{:S(2)}, u32[]{:S(2)}) collective-permute-start(s32[12,16]{1,0:T(8,128)S(1)} %get-tuple-element.27.refs_0_), channel_id=1, source_target_pairs={{0,2},{2,0},{1,3},{3,1},{4,6},{6,4},{5,7},{7,5},{8,10},{10,8},{9,1... | collective-permute-start | bytes 2312 | tf_op jit(solution)/shard_map/ppermute | solution.py:375
  2.6 10.5 %collective-permute-start.2 = (bf16[2,64,512]{2,1,0:T(8,128)(2,1)S(1)}, bf16[2,64,512]{2,1,0:T(8,128)(2,1)S(1)}, u32[]{:S(2)}, u32[]{:S(2)}) collective-permute-start(bf16[2,64,512]{2,1,0:T(8,128)(2,1)S(1)} %get-tuple-element.30), channel_id=1, source_target_pairs={{0,4},{4,8},{8,12},{12,0},{1,5},{5,9},{9,13},{13,1},{2,6},{6,10},{... | collective-permute-start | bytes 393224 | tf_op jit(solution)/shard_map/ppermute | solution.py:415
  4.2 9.0 %copy-start = (bf16[16,512,64]{1,2,0:T(8,128)(2,1)S(1)}, bf16[16,512,64]{1,2,0:T(8,128)(2,1)}, u32[]{:S(2)}) copy-start(bf16[16,512,64]{1,2,0:T(8,128)(2,1)} %param.7) | copy-start | bytes 3145732
  4.2 9.0 %copy-start.3 = (s32[16,512]{1,0:T(8,128)S(1)}, s32[16,512]{1,0:T(8,128)}, u32[]{:S(2)}) copy-start(s32[16,512]{1,0:T(8,128)} %skel_ref.5) | copy-start | bytes 98308
  4.2 9.0 %collective-permute-start.3 = (bf16[2,64,512]{2,1,0:T(8,128)(2,1)S(1)}, bf16[2,64,512]{2,1,0:T(8,128)(2,1)S(1)}, u32[]{:S(2)}, u32[]{:S(2)}) collective-permute-start(bf16[2,64,512]{2,1,0:T(8,128)(2,1)S(1)} %get-tuple-element.31), channel_id=1, source_target_pairs={{0,12},{4,0},{8,4},{12,8},{1,13},{5,1},{9,5},{13,9},{2,14},{6,2},{... | collective-permute-start | bytes 393224 | tf_op jit(solution)/shard_map/ppermute | solution.py:416
  8.5 18.2 %collective-permute-start.4 = (bf16[512,256]{1,0:T(8,128)(2,1)S(1)}, bf16[512,256]{1,0:T(8,128)(2,1)S(1)}, u32[]{:S(2)}, u32[]{:S(2)}) collective-permute-start(bf16[512,256]{1,0:T(8,128)(2,1)S(1)} %get-tuple-element.35), channel_id=1, source_target_pairs={{0,4},{4,8},{8,12},{12,0},{1,5},{5,9},{9,13},{13,1},{2,6},{6,10},{... | collective-permute-start | bytes 786440 | tf_op jit(solution)/shard_map/ppermute | solution.py:444
  10.1 18.8 %collective-permute-start.5 = (bf16[512,256]{1,0:T(8,128)(2,1)S(1)}, bf16[512,256]{1,0:T(8,128)(2,1)S(1)}, u32[]{:S(2)}, u32[]{:S(2)}) collective-permute-start(bf16[512,256]{1,0:T(8,128)(2,1)S(1)} %get-tuple-element.36), channel_id=1, source_target_pairs={{0,12},{4,0},{8,4},{12,8},{1,13},{5,1},{9,5},{13,9},{2,14},{6,2},{... | collective-permute-start | bytes 786440 | tf_op jit(solution)/shard_map/ppermute | solution.py:444
  10.7 24.4 %collective-permute-start.8 = (bf16[384,256]{1,0:T(8,128)(2,1)S(1)}, bf16[384,256]{1,0:T(8,128)(2,1)S(1)}, u32[]{:S(2)}, u32[]{:S(2)}) collective-permute-start(bf16[384,256]{1,0:T(8,128)(2,1)S(1)} %get-tuple-element.42), channel_id=1, source_target_pairs={{0,8},{4,12},{8,0},{12,4},{1,9},{5,13},{9,1},{13,5},{2,10},{6,14},... | collective-permute-start | bytes 589832 | tf_op jit(solution)/shard_map/ppermute | solution.py:444
  35.0 1.7 %collective-permute-start.6 = (bf16[16,8192]{1,0:T(8,128)(2,1)S(1)}, bf16[16,8192]{1,0:T(8,128)(2,1)S(1)}, u32[]{:S(2)}, u32[]{:S(2)}) collective-permute-start(bf16[16,8192]{1,0:T(8,128)(2,1)S(1)} %get-tuple-element.38), channel_id=1, source_target_pairs={{0,1},{1,0},{2,3},{3,2},{4,5},{5,4},{6,7},{7,6},{8,9},{9,8},{10,11... | collective-permute-start | bytes 786440 | tf_op jit(solution)/shard_map/ppermute | solution.py:375
  36.8 8.8 %collective-permute-start.7 = (bf16[16,8192]{1,0:T(8,128)(2,1)S(1)}, bf16[16,8192]{1,0:T(8,128)(2,1)S(1)}, u32[]{:S(2)}, u32[]{:S(2)}) collective-permute-start(bf16[16,8192]{1,0:T(8,128)(2,1)S(1)} %add_convert_fusion.refs_0_.after_ref), channel_id=1, source_target_pairs={{0,2},{2,0},{1,3},{3,1},{4,6},{6,4},{5,7},{7,5},{8,10},{10,8},{9,1... | collective-permute-start | bytes 786440 | tf_op jit(solution)/shard_map/ppermute | solution.py:375
  36.9 9.1 %copy-start.2 = (s32[1,8192]{1,0:T(1,128)S(1)}, s32[1,8192]{1,0:T(1,128)}, u32[]{:S(2)}) copy-start(s32[1,8192]{1,0:T(1,128)} %order_ref.3) | copy-start | bytes 98308
  40.6 1.6 %collective-permute-start.9 = (bf16[16,4096]{1,0:T(8,128)(2,1)S(1)}, bf16[16,4096]{1,0:T(8,128)(2,1)S(1)}, u32[]{:S(2)}, u32[]{:S(2)}) collective-permute-start(bf16[16,4096]{1,0:T(8,128)(2,1)S(1)} %get-tuple-element.48), channel_id=1, source_target_pairs={{0,1},{1,0},{2,3},{3,2},{4,5},{5,4},{6,7},{7,6},{8,9},{9,8},{10,11... | collective-permute-start | bytes 393224 | tf_op jit(solution)/shard_map/ppermute | solution.py:375
  45.6 5.2 %copy-start.1 = (bf16[16,256,256]{2,1,0:T(8,128)(2,1)S(1)}, bf16[16,256,256]{2,1,0:T(8,128)(2,1)}, u32[]{:S(2)}) copy-start(bf16[16,256,256]{2,1,0:T(8,128)(2,1)} %interp_ref.3) | copy-start | bytes 6291460
  45.6 5.2 %collective-permute-start.10 = (bf16[16,4096]{1,0:T(8,128)(2,1)S(1)}, bf16[16,4096]{1,0:T(8,128)(2,1)S(1)}, u32[]{:S(2)}, u32[]{:S(2)}) collective-permute-start(bf16[16,4096]{1,0:T(8,128)(2,1)S(1)} %shard_map.80.refs_0_), channel_id=1, source_target_pairs={{0,2},{2,0},{1,3},{3,1},{4,6},{6,4},{5,7},{7,5},{8,10},{10,8},{9,1... | collective-permute-start | bytes 393224 | tf_op jit(solution)/shard_map/ppermute | solution.py:375
